TPU v7x, 128 devices: a whole 4x4x4 slice. The times are simulated.
128 devices in a mesh: row: 8 (over z, core), col: 16 (over x, y).
Axes of the slice: x: 4, y: 4, z: 4, core: 2. Of those that a mesh axis runs over, the one named last changes fastest.
Arguments:
- images: bfloat16 [16384, 512], P(('row', 'col')), as said below
- texts: bfloat16 [16384, 512], P(('row', 'col')), as said below
- partner: int32 [16384], P('row'), may hold values from 0 to 16383, as said below
- log_scale: float32 [1], replicated, may hold values from 2.3 to 5.71
Outputs:
- image_grad: float32 [16384, 512], P(('row', 'col'))
- text_grad: float32 [16384, 512], P(('row', 'col'))
- loss: float32 [1], replicated
- temp_grad: float32 [1], replicated
Inputs may be any that keep to these rules, and one draw needn't show every extreme that they name: `images`: finite image embeddings. `texts`: finite text embeddings. A permutation: every text is the partner of exactly one image.
All inputs are finite; a program needn't handle non-finite values.
Results may differ from a plain program's by a relative error of at most 0.017.
Values may be sent and summed in bfloat16 or wider, within the bound.
No kernel may reach another device: no remote copies, remote signals or barrier semaphores. Data moves between devices by JAX's collectives and lax.ppermute only.
A program may use at most 64 MiB of HBM per device.

v0:
```python
import math

import jax
import jax.numpy as jnp
from jax import lax
from jax.sharding import PartitionSpec as P


def unit_rows(values):
    widened = values.astype(jnp.float32)
    inverse = lax.rsqrt(jnp.sum(widened * widened, axis=1, keepdims=True) + 1e-06)
    return (widened * inverse, inverse)


def through_norm(grad_unit, unit_values, inverse):
    return inverse * (
        grad_unit - unit_values * jnp.sum(unit_values * grad_unit, axis=1, keepdims=True)
    )


def tile_logits(row_piece, col_piece, temp_scale):
    return temp_scale * lax.dot_general(
        row_piece, col_piece, (((1,), (1,)), ((), ())), preferred_element_type=jnp.float32
    )


def on_device(images, texts, partner, log_scale):
    unit_img, inv_img = unit_rows(images)
    unit_txt, inv_txt = unit_rows(texts)
    temp_scale = jnp.exp(log_scale[0])
    img_rows = lax.all_gather(unit_img.astype(jnp.bfloat16), "col", axis=0, tiled=True)
    txt_cols = lax.all_gather(unit_txt.astype(jnp.bfloat16), "row", axis=0, tiled=True)
    shard_rows = images.shape[0]
    row_devices = lax.axis_size("row")
    col_devices = lax.axis_size("col")
    row_index = lax.axis_index("row")
    col_index = lax.axis_index("col")
    batch_total = shard_rows * row_devices * col_devices
    image_count = img_rows.shape[0]
    text_count = txt_cols.shape[0]
    positions = jnp.arange(text_count, dtype=jnp.int32)
    column_ids = (
        positions // shard_rows * (col_devices * shard_rows)
        + col_index * shard_rows
        + positions % shard_rows
    )
    block_rows = math.gcd(image_count, 512)
    count_blocks = image_count // block_rows

    def forward(running, inputs):
        row_piece, targets = inputs
        logits = tile_logits(row_piece, txt_cols, temp_scale)
        matched = targets[:, None] == column_ids[None, :]
        picked = jnp.where(matched, logits, 0.0)
        row_high = jnp.max(logits, axis=1)
        weights = jnp.exp(logits - row_high[:, None])
        row_out = (
            row_high,
            jnp.sum(weights, axis=1),
            jnp.sum(weights * logits, axis=1),
            jnp.sum(picked, axis=1),
        )
        col_high = jnp.maximum(running[0], jnp.max(logits, axis=0))
        rescale = jnp.exp(running[0] - col_high)
        col_weights = jnp.exp(logits - col_high[None, :])
        updated = (
            col_high,
            running[1] * rescale + jnp.sum(col_weights, axis=0),
            running[2] * rescale + jnp.sum(col_weights * logits, axis=0),
        )
        return (updated, row_out)

    start_state = (
        jnp.full((text_count,), -jnp.inf, dtype=jnp.float32),
        jnp.zeros((text_count,), jnp.float32),
        jnp.zeros((text_count,), jnp.float32),
    )
    col_local, row_part = lax.scan(
        forward,
        start_state,
        (img_rows.reshape(count_blocks, block_rows, -1), partner.reshape(count_blocks, block_rows)),
    )
    row_local = tuple((piece.reshape(image_count) for piece in row_part[:3]))
    pick_local = jnp.sum(row_part[3])
    row_high = lax.pmax(row_local[0], "col")
    row_rescale = jnp.exp(row_local[0] - row_high)
    row_sums = lax.psum((row_local[1] * row_rescale, row_local[2] * row_rescale), "col")
    row_stats = (row_high, row_sums[0], row_sums[1])
    col_high = lax.pmax(col_local[0], "row")
    col_rescale = jnp.exp(col_local[0] - col_high)
    col_sums = lax.psum((col_local[1] * col_rescale, col_local[2] * col_rescale), "row")
    col_stats = (col_high, col_sums[0], col_sums[1])
    row_logsum = row_stats[0] + jnp.log(row_stats[1])
    col_logsum = col_stats[0] + jnp.log(col_stats[1])

    def own_rows(values):
        return lax.dynamic_slice_in_dim(values, col_index * shard_rows, shard_rows, 0)

    def own_cols(values):
        return lax.dynamic_slice_in_dim(values, row_index * shard_rows, shard_rows, 0)

    loss_part = jnp.sum(own_rows(row_logsum)) + jnp.sum(own_cols(col_logsum)) - 2.0 * pick_local
    temp_part = (
        jnp.sum(own_rows(row_stats[2] / row_stats[1]))
        + jnp.sum(own_cols(col_stats[2] / col_stats[1]))
        - 2.0 * pick_local
    )
    loss_total, temp_total = lax.psum((loss_part, temp_part), ("row", "col"))
    loss = (loss_total / (2 * batch_total)).reshape(1)
    temp_grad = (temp_total / (2 * batch_total)).reshape(1)

    def dlogit(row_first, row_count):
        row_piece = lax.dynamic_slice_in_dim(img_rows, row_first, row_count, 0)
        logits = tile_logits(row_piece, txt_cols, temp_scale)
        targets = lax.dynamic_slice_in_dim(partner, row_first, row_count, 0)
        matched = jnp.where(targets[:, None] == column_ids[None, :], 1.0, 0.0)
        row_part_lse = lax.dynamic_slice_in_dim(row_logsum, row_first, row_count, 0)
        soft = 0.5 * (
            jnp.exp(logits - row_part_lse[:, None]) + jnp.exp(logits - col_logsum[None, :])
        )
        return (soft - matched).astype(jnp.bfloat16)

    piece_rows = math.gcd(lax.axis_size("col") * shard_rows, 512)

    def piece_term(step_index):
        piece_first = step_index * piece_rows
        grad_tile = dlogit(piece_first, piece_rows)
        return temp_scale * jnp.dot(grad_tile, txt_cols, preferred_element_type=jnp.float32)

    pieces = lax.map(
        piece_term, jnp.arange(lax.axis_size("col") * shard_rows // piece_rows, dtype=jnp.int32)
    )
    img_unit_grad = lax.psum_scatter(
        pieces.reshape(lax.axis_size("col") * shard_rows, -1).astype(jnp.bfloat16),
        "col",
        scatter_dimension=0,
        tiled=True,
    ).astype(jnp.float32)

    def add_block(running, step_index):
        grad_tile = dlogit(step_index * block_rows, block_rows)
        row_piece = lax.dynamic_slice_in_dim(img_rows, step_index * block_rows, block_rows, 0)
        product = lax.dot_general(
            grad_tile, row_piece, (((0,), (0,)), ((), ())), preferred_element_type=jnp.float32
        )
        return (running + temp_scale * product, None)

    summed, unused = lax.scan(
        add_block,
        jnp.zeros((lax.axis_size("row") * shard_rows, img_rows.shape[1]), jnp.float32),
        jnp.arange(count_blocks, dtype=jnp.int32),
    )
    txt_unit_grad = lax.psum_scatter(
        summed.astype(jnp.bfloat16), "row", scatter_dimension=0, tiled=True
    ).astype(jnp.float32)
    image_grad = through_norm(img_unit_grad, unit_img, inv_img)
    text_grad = through_norm(txt_unit_grad, unit_txt, inv_txt)
    return (image_grad, text_grad, loss, temp_grad)


def solution(mesh):
    placed = (P(("row", "col"), None), P(("row", "col"), None), P("row"), P())
    return jax.shard_map(
        on_device,
        mesh=mesh,
        in_specs=placed,
        out_specs=(P(("row", "col"), None), P(("row", "col"), None), P(), P()),
        check_vma=False,
    )
```

profile of v0, /device:TPU:0, one launch (start us, length us, event | category | flops | bytes accessed | tf_op | source)
XLA Modules:
  0.0 375.9 jit_solution(1241832492938940498)
XLA Ops:
  7.2 1.0 fusion.72
  8.2 1.7 fusion.68
  10.0 1.0 fusion.71
  11.0 1.7 fusion.70
  13.5 0.7 reshape.64
  14.2 22.2 %all-gather.5.cloned.1.call-done = bf16[1024,512]{1,0:T(8,128)(2,1)} async-done(((bf16[128,512]{1,0:T(8,128)(2,1)}), bf16[1024,512]{1,0:T(8,128)(2,1)}) %all-gather.5.cloned.1.call-update) | async-done | bytes 1048592 | tf_op jit(solution)/shard_map/all_gather | solution.py:32
  36.4 47.4 %all-gather.3.cloned.1.call-done = bf16[2048,512]{1,0:T(8,128)(2,1)} async-done(((bf16[128,512]{1,0:T(8,128)(2,1)}), bf16[2048,512]{1,0:T(8,128)(2,1)}) %all-gather.3.cloned.1.call-update) | async-done | bytes 2097168 | tf_op jit(solution)/shard_map/all_gather | solution.py:31
  83.8 16.9 %while.46 = (s32[]{:T(128)}, f32[1024]{0:T(1024)S(1)}, f32[1024]{0:T(1024)S(1)}, f32[1024]{0:T(1024)S(1)}, f32[4,512]{1,0:T(4,128)S(1)}, /*index=5*/f32[4,512]{1...) while((s32[]{:T(128)}, f32[1024]{0:T(1024)S(1)}, ...), condition=%wide.region_10.11_spmd.clone, body=%wide.region_2.10_spmd.clone.sunk | while | flops 544231424 | bytes 5878960 | solution.py:78
  83.8 2.2 fusion.107
  86.1 1.7 multiply_reduce_fusion.3
  88.0 2.2 fusion.107
  90.3 1.7 multiply_reduce_fusion.3
  92.2 2.2 fusion.107
  94.5 1.7 multiply_reduce_fusion.3
  96.4 2.2 fusion.107
  98.7 1.7 multiply_reduce_fusion.3
  100.7 38.6 %pmax.14 = f32[2048]{0:T(1024)S(1)} all-reduce(f32[2048]{0:T(1024)S(1)} %bitcast.63), channel_id=1, replica_groups=mesh['row'=8,'col'=16] {'col'}, use_global_device_ids=true, to_apply=%region_11.12 | all-reduce | flops 2048 | bytes 16384 | tf_op jit(solution)/shard_map/pmax | solution.py:85
  139.3 69.5 %all-reduce.1 = (f32[2048]{0:T(1024)S(1)}, f32[2048]{0:T(1024)S(1)}) all-reduce(f32[2048]{0:T(1024)S(1)} %get-tuple-element.379, f32[2048]{0:T(1024)S(1)} %get-tuple-element.378), channel_id=1, replica_groups=mesh['row'=8,'col'=16] {'col'}, use_global_device_ids=true, to_apply=%region_12.13 | all-reduce | flops 4096 | bytes 32768 | tf_op jit(solution)/shard_map/psum | solution.py:87
  208.9 12.4 %pmax.15 = f32[1024]{0:T(1024)S(1)} all-reduce(f32[1024]{0:T(1024)S(1)} %get-tuple-element.183), channel_id=1, replica_groups=mesh['row'=8,'col'=16] {'row'}, use_global_device_ids=true, to_apply=%region_13.14 | all-reduce | flops 1024 | bytes 8192 | tf_op jit(solution)/shard_map/pmax | solution.py:89
  221.3 12.7 %all-reduce.2 = (f32[1024]{0:T(1024)S(1)}, f32[1024]{0:T(1024)S(1)}) all-reduce(f32[1024]{0:T(1024)S(1)} %get-tuple-element.381, f32[1024]{0:T(1024)S(1)} %get-tuple-element.380), channel_id=1, replica_groups=mesh['row'=8,'col'=16] {'row'}, use_global_device_ids=true, to_apply=%region_14.15 | all-reduce | flops 2048 | bytes 16384 | tf_op jit(solution)/shard_map/psum | solution.py:91
  234.0 25.7 %while.47 = (s32[]{:T(128)}, f32[1024,512]{1,0:T(8,128)}, f32[]{:T(128)}, s32[4]{0:T(128)S(1)}, bf16[2048,512]{1,0:T(8,128)(2,1)}, /*index=5*/bf16[1024,512]{1,0...) while((s32[]{:T(128)}, f32[1024,512]{1,0:T(8,128)}, ...), condition=%wide.region_20.21_spmd.clone, body=%wide.region_19.20_spmd.clone.sunk | while | flops 1080048640 | bytes 6318804 | solution.py:148
  234.0 0.6 dynamic_slice.103
  235.3 0.1 dynamic_slice.104
  235.4 0.1 dynamic_slice.105
  235.4 4.5 %select_add_fusion.2 = f32[1024,512]{1,0:T(8,128)} fusion(f32[1024,512]{1,0:T(8,128)} %get-tuple-element.709, f32[]{:T(128)} %get-tuple-element.724, pred[]{:T(512)S(6)} %compare.10, bf16[1024,512]{1,0:T(8,128)(2,1)} %get-tuple-element.727, s32[1024]{0:T(1024)S(1)} %fusion.113, f32[1024]{0:T(1024)S(1)} %get-tuple-element.729, ...), kind=kOutput, calls=%fused_computation.66.clone.1 | convolution fusion | flops 1080033280 | bytes 6306304 | tf_op jit(solution)/shard_map/while/body/eval_jaxpr/dot_general | solution.py:143
  239.9 0.6 dynamic_slice.103
  241.2 0.1 dynamic_slice.104
  241.2 0.1 dynamic_slice.105
  241.3 5.2 %select_add_fusion.2 = f32[1024,512]{1,0:T(8,128)} fusion(f32[1024,512]{1,0:T(8,128)} %get-tuple-element.709, f32[]{:T(128)} %get-tuple-element.724, pred[]{:T(512)S(6)} %compare.10, bf16[1024,512]{1,0:T(8,128)(2,1)} %get-tuple-element.727, s32[1024]{0:T(1024)S(1)} %fusion.113, f32[1024]{0:T(1024)S(1)} %get-tuple-element.729, ...), kind=kOutput, calls=%fused_computation.66.clone.1 | convolution fusion | flops 1080033280 | bytes 6306304 | tf_op jit(solution)/shard_map/while/body/eval_jaxpr/dot_general | solution.py:143
  246.5 0.6 dynamic_slice.103
  247.7 0.1 dynamic_slice.104
  247.8 0.1 dynamic_slice.105
  247.9 5.2 %select_add_fusion.2 = f32[1024,512]{1,0:T(8,128)} fusion(f32[1024,512]{1,0:T(8,128)} %get-tuple-element.709, f32[]{:T(128)} %get-tuple-element.724, pred[]{:T(512)S(6)} %compare.10, bf16[1024,512]{1,0:T(8,128)(2,1)} %get-tuple-element.727, s32[1024]{0:T(1024)S(1)} %fusion.113, f32[1024]{0:T(1024)S(1)} %get-tuple-element.729, ...), kind=kOutput, calls=%fused_computation.66.clone.1 | convolution fusion | flops 1080033280 | bytes 6306304 | tf_op jit(solution)/shard_map/while/body/eval_jaxpr/dot_general | solution.py:143
  253.1 0.6 dynamic_slice.103
  254.3 0.1 dynamic_slice.104
  254.4 0.1 dynamic_slice.105
  254.5 5.2 %select_add_fusion.2 = f32[1024,512]{1,0:T(8,128)} fusion(f32[1024,512]{1,0:T(8,128)} %get-tuple-element.709, f32[]{:T(128)} %get-tuple-element.724, pred[]{:T(512)S(6)} %compare.10, bf16[1024,512]{1,0:T(8,128)(2,1)} %get-tuple-element.727, s32[1024]{0:T(1024)S(1)} %fusion.113, f32[1024]{0:T(1024)S(1)} %get-tuple-element.729, ...), kind=kOutput, calls=%fused_computation.66.clone.1 | convolution fusion | flops 1080033280 | bytes 6306304 | tf_op jit(solution)/shard_map/while/body/eval_jaxpr/dot_general | solution.py:143
  259.7 2.8 convert_element_type.40
  262.6 19.6 %while.45 = (s32[]{:T(128)}, bf16[4,512,512]{2,1,0:T(8,128)(2,1)}, f32[]{:T(128)}, s32[4]{0:T(128)S(1)}, bf16[2048,512]{1,0:T(8,128)(2,1)}, /*index=5*/bf16[1024...) while((s32[]{:T(128)}, bf16[4,512,512]{2,1,0:T(8,128)(2,1)}, ...), condition=%wide.region_16.17_spmd.clone, body=%wide.region_15.16_spmd.clone.sunk | while | flops 1078737920 | bytes 3696335 | solution.py:130
  262.6 0.6 dynamic_slice.96
  263.8 0.1 dynamic_slice.97
  263.9 0.1 dynamic_slice.98
  264.0 3.5 fusion.105
  267.5 0.6 dynamic_slice.96
  268.7 0.1 dynamic_slice.97
  268.8 0.1 dynamic_slice.98
  268.9 3.5 fusion.105
  272.4 0.6 dynamic_slice.96
  273.6 0.1 dynamic_slice.97
  273.8 3.5 fusion.105
  277.3 0.6 dynamic_slice.96
  278.5 0.1 dynamic_slice.97
  278.6 0.1 dynamic_slice.98
  278.7 3.5 fusion.105
  282.2 0.7 dynamic-slice_reduce_fusion.1
  282.9 0.7 dynamic-slice_reduce_fusion
  283.5 0.7 dynamic-slice_reduce_fusion.2
  285.5 0.6 reduce_sum.132
  288.1 62.8 %all-reduce = (f32[]{:T(128)}, f32[]{:T(128)}) all-reduce(f32[]{:T(128)S(6)} %sub.86, f32[]{:T(128)S(6)} %sub.87), channel_id=1, replica_groups=mesh['row'=8,'col'=16] {'row','col'}, use_global_device_ids=true, to_apply=%region_26.27 | all-reduce | flops 2 | bytes 16 | tf_op jit(solution)/shard_map/psum | solution.py:108
  352.2 1.1 fusion.75
  353.3 1.8 fusion.76
  355.1 9.2 %reduce-scatter.3.cloned.1.call-done = bf16[128,512]{1,0:T(8,128)(2,1)} async-done(((bf16[2048,512]{1,0:T(8,128)(2,1)}), bf16[128,512]{1,0:T(8,128)(2,1)}) %reduce-scatter.3.cloned.1.call-update) | async-done | bytes 131088 | tf_op jit(solution)/shard_map/reduce_scatter | solution.py:133
  364.2 1.1 fusion.73
  365.3 1.8 fusion.74
  (82 shorter events, 1.4 us)
Async XLA Ops:
  7.2 29.2 %all-gather.5.cloned.1.call-start = ((), (), s32[]{:S(2)}) async-start(), calls=%async_computation.3 | async-start | bytes 1179648 | tf_op jit(solution)/shard_map/all_gather | solution.py:32
  9.9 73.9 %all-gather.3.cloned.1.call-start = ((), (), s32[]{:S(2)}) async-start(), calls=%async_computation.2 | async-start | bytes 2228224 | tf_op jit(solution)/shard_map/all_gather | solution.py:31
  12.7 339.5 %reduce-scatter.5.cloned.1.call-start = ((), (), s32[]{:S(2)}) async-start(), calls=%async_computation.5 | async-start | bytes 1179648 | tf_op jit(solution)/shard_map/reduce_scatter | solution.py:153
  83.8 150.2 %copy-start.2 = (s32[2048]{0:T(1024)S(1)}, s32[2048]{0:T(1024)}, u32[]{:S(2)}) copy-start(s32[2048]{0:T(1024)} %param.12) | copy-start | bytes 24580
  259.7 2.9 copy-start.3
  262.5 101.8 %reduce-scatter.3.cloned.1.call-start = ((), (), s32[]{:S(2)}) async-start(), calls=%async_computation.4 | async-start | bytes 2228224 | tf_op jit(solution)/shard_map/reduce_scatter | solution.py:133
  282.2 70.0 %copy-start = (bf16[128,512]{1,0:T(8,128)(2,1)S(1)}, bf16[128,512]{1,0:T(8,128)(2,1)}, u32[]{:S(2)}) copy-start(bf16[128,512]{1,0:T(8,128)(2,1)} %param.11) | copy-start | bytes 393220
  282.2 82.1 %copy-start.1 = (bf16[128,512]{1,0:T(8,128)(2,1)S(1)}, bf16[128,512]{1,0:T(8,128)(2,1)}, u32[]{:S(2)}) copy-start(bf16[128,512]{1,0:T(8,128)(2,1)} %param.10) | copy-start | bytes 393220
Sparse Core Ops, SparseCore 0:
  10.3 26.0 all-gather.4
  39.1 44.6 all-gather.2
  262.6 25.5 reduce-scatter.4
  291.3 72.9 reduce-scatter.2
where the time goes:
time: 377 us; the launch traced here: 376 us
  blocking collectives  196 us (52%)
  waiting for transfers between devices  78.8 us (21%)
  matrix products  42.9 us (11%)
  other arithmetic  23.4 us (6%)
  between operations  21.5 us (6%)
  local copies, waits for them, and re-layouts  7.46 us (2%)
  loops' own time  5.54 us (1%)
    psum x1, blocking collectives, on_device(): lax.psum((row_local[1] * row_rescale, row_local[2] * row_rescale), 'col')  69.5 us
    psum x1, blocking collectives, on_device(): loss_total, temp_total = lax.psum((loss_part, temp_part), ('row', 'col'))  62.8 us
    all_gather x1, waiting for transfers between devices, on_device(): lax.all_gather(unit_img.astype(jnp.bfloat16), 'col', axis=0, tiled=True)  47.4 us
    pmax x1, blocking collectives, on_device(): row_high = lax.pmax(row_local[0], 'col')  38.6 us
    all_gather x1, waiting for transfers between devices, on_device(): lax.all_gather(unit_txt.astype(jnp.bfloat16), 'row', axis=0, tiled=True)  22.2 us
    dot_general x4, matrix products, add_block(): lax.dot_general(grad_tile, row_piece, (((0,), (0,)), ((), ())), preferred...  20 us
    dot_general x4, matrix products, piece_term(): jnp.dot(grad_tile, txt_cols, preferred_element_type=jnp.float32)  14 us
    psum x1, blocking collectives, on_device(): lax.psum((col_local[1] * col_rescale, col_local[2] * col_rescale), 'row')  12.7 us
  transfers between devices with their start and end apart: 4, of which 3 were waited for; matrix products, arithmetic and copies ran while one was open for 7% of the time, Pallas kernels for 0%

commit v1 on v0

v1 whole, which is shorter than its diff:
```python
import functools

import jax
import jax.numpy as jnp
from jax import lax
from jax.experimental import pallas as pl
from jax.experimental.pallas import tpu as pltpu
from jax.sharding import PartitionSpec as P

ROWS = 128
WIDTH = 512
QUAD = 4 * ROWS
EXTRA = 16
OFFS = (0, 2, 1, 3)
LOG2E = 1.4426950408889634
LN2 = 0.6931471805599453
RC = ("row", "col")
F32 = jnp.float32
BF16 = jnp.bfloat16
VMEM = pl.BlockSpec(memory_space=pltpu.VMEM)
SMEM = pl.BlockSpec(memory_space=pltpu.SMEM)
PARAMS = pltpu.CompilerParams(vmem_limit_bytes=40 * 1024 * 1024)


def device(z, k, x, y):
    return (z * 2 + k) * 16 + x * 4 + y


def shifted(value, move):
    pairs = []
    for z in range(4):
        for k in range(2):
            for x in range(4):
                for y in range(4):
                    pairs.append((device(z, k, x, y), device(*move(z, k, x, y))))
    return lax.ppermute(value, RC, pairs)


def ring_a(by):
    return lambda z, k, x, y: (z, k, x, (y + by) % 4) if k else (z, k, (x + by) % 4, y)


def ring_b(by):
    return lambda z, k, x, y: (z, k, (x + by) % 4, y) if k else (z, k, x, (y + by) % 4)


def ring_z(by):
    return lambda z, k, x, y: ((z + by) % 4, k, x, y)


def other_core(z, k, x, y):
    return (z, 1 - k, x, y)


def call(kernel, outs, *args, specs=None, cost=None, scratch=()):
    return pl.pallas_call(
        kernel,
        out_shape=outs,
        in_specs=specs or [VMEM] * len(args),
        out_specs=jax.tree.map(lambda o: VMEM, outs),
        scratch_shapes=scratch,
        compiler_params=PARAMS,
        cost_estimate=cost,
    )(*args)


def shape(dims, dtype):
    return jax.ShapeDtypeStruct(dims, dtype)


def unit_rows(values):
    widened = values.astype(F32)
    inverse = lax.rsqrt(jnp.sum(widened * widened, axis=1, keepdims=True) + 1e-06)
    return widened * inverse, inverse


def unit_kernel(img_ref, txt_ref, img_out, txt_out):
    img_out[...] = unit_rows(img_ref[...])[0].astype(BF16)
    txt_out[...] = unit_rows(txt_ref[...])[0].astype(BF16)


def places(ids_ref):
    row, col = ids_ref[0], ids_ref[1]
    z, k, x, y = row // 2, row % 2, col // 4, col % 4
    pos_a = jnp.where(k == 0, x, y)
    pos_b = jnp.where(k == 0, y, x)

    def col_of(q, a):
        in_b = (pos_b + 4 - OFFS[q]) % 4
        in_a = (pos_a + 4 - OFFS[a]) % 4
        return jnp.where(k == 0, in_a * 4 + in_b, in_b * 4 + in_a)

    def row_of(j, t):
        return (z + 4 - OFFS[t]) % 4 * 2 + (k if j == 0 else 1 - k)

    return col_of, row_of


def to_lanes(column):
    return jnp.transpose(jnp.broadcast_to(column, (ROWS, ROWS)))[0:1, :]


def logits2(rows, t_refs, scale2):
    parts = [
        lax.dot_general(rows, t[...], (((1,), (1,)), ((), ())), preferred_element_type=F32)
        for t in t_refs
    ]
    return jnp.concatenate(parts, axis=1) * scale2


CHUNK = 256


def forward_kernel(ids_ref, scale_ref, pos_ref, i0, i1, i2, i3, t0, t1, row_out, col_out, col_state):
    scale2 = scale_ref[0] * LOG2E
    col_of, row_of = places(ids_ref)
    lanes = lax.broadcasted_iota(jnp.int32, (CHUNK, 8 * ROWS), 1)
    col_state[0:1, :] = jnp.full((1, 8 * ROWS), -jnp.inf, F32)
    col_state[1:3, :] = jnp.zeros((2, 8 * ROWS), F32)
    picked = jnp.zeros((1, 8 * ROWS), F32)
    for q, rows_ref in enumerate((i0, i1, i2, i3)):
        for h in range(QUAD // CHUNK):
            logits = logits2(rows_ref[h * CHUNK : (h + 1) * CHUNK, :], (t0, t1), scale2)
            high = jnp.max(logits, axis=1, keepdims=True)
            weights = jnp.exp2(logits - high)
            total = jnp.sum(weights, axis=1, keepdims=True)
            mean = jnp.sum(weights * logits, axis=1, keepdims=True) / total
            lse = high + jnp.log2(total)
            pos = []
            for b in range(CHUNK // ROWS):
                place = col_of(q, h * (CHUNK // ROWS) + b)
                row_out[pl.ds(place, 1), :] = to_lanes(lse[b * ROWS : (b + 1) * ROWS])
                row_out[pl.ds(16 + place, 1), :] = to_lanes(mean[b * ROWS : (b + 1) * ROWS])
                pos.append(pos_ref[pl.ds(pl.multiple_of(place * ROWS, ROWS), ROWS), :])
            pos = jnp.concatenate(pos, axis=0)
            pos = jnp.concatenate([pos] * 8, axis=1)
            picked += jnp.sum(jnp.where(pos == lanes, logits, 0.0), axis=0, keepdims=True)
            old = col_state[0:1, :]
            col_high = jnp.maximum(old, jnp.max(logits, axis=0, keepdims=True))
            rescale = jnp.exp2(old - col_high)
            col_weights = jnp.exp2(logits - col_high)
            col_state[0:1, :] = col_high
            col_state[1:2, :] = col_state[1:2, :] * rescale + jnp.sum(col_weights, axis=0, keepdims=True)
            col_state[2:3, :] = col_state[2:3, :] * rescale + jnp.sum(
                col_weights * logits, axis=0, keepdims=True
            )
    row_out[32:40, :] = jnp.broadcast_to(jnp.sum(picked, axis=1, keepdims=True), (8, ROWS))
    col_lse = col_state[0:1, :] + jnp.log2(col_state[1:2, :])
    col_mean = col_state[2:3, :] / col_state[1:2, :]
    for j in range(2):
        for t in range(4):
            at = (j * 4 + t) * ROWS
            place = row_of(j, t)
            col_out[pl.ds(place, 1), :] = col_lse[:, at : at + ROWS]
            col_out[pl.ds(8 + place, 1), :] = col_mean[:, at : at + ROWS]


def combined(refs, count):
    parts = [r[0:count, :] for r in refs]
    means = [r[count : 2 * count, :] for r in refs]
    high = functools.reduce(jnp.maximum, parts)
    weights = [jnp.exp2(p - high) for p in parts]
    total = sum(weights)
    mean = sum(w * m for w, m in zip(weights, means)) / total
    return high + jnp.log2(total), mean


def combine_kernel(r0, r1, r2, r3, c0, c1, c2, c3, row_out, col_out):
    row_out[0:16, :], row_out[16:32, :] = combined((r0, r1, r2, r3), 16)
    row_out[32:40, :] = r0[32:40, :] + r1[32:40, :] + r2[32:40, :] + r3[32:40, :]
    col_out[0:8, :], col_out[8:16, :] = combined((c0, c1, c2, c3), 8)


def in_parts(first, second):
    lane = lax.broadcasted_iota(jnp.int32, (EXTRA, WIDTH), 1)
    part = lax.broadcasted_iota(jnp.int32, (EXTRA, WIDTH), 0)
    value = jnp.where(lane == 0, first, jnp.where(lane == 1, second, 0.0))
    high = value.astype(BF16)
    rest = value - high.astype(F32)
    mid = rest.astype(BF16)
    low = (rest - mid.astype(F32)).astype(BF16)
    zero = jnp.zeros((EXTRA, WIDTH), F32)
    out = jnp.where(part == 0, high.astype(F32), zero)
    out = jnp.where(part == 1, mid.astype(F32), out)
    return jnp.where(part == 2, low.astype(F32), out).astype(BF16)


def backward_kernel(
    ids_ref, scale_ref, pos_ref, r0, r1, r2, r3, c0, c1, i0, i1, i2, i3, t0, t1,
    g0, g1, g2, g3, h0, h1, row_shift, col_shift, acc,
):
    scale = scale_ref[0]
    scale2 = scale * LOG2E
    col_of, row_of = places(ids_ref)
    row_lse, row_mean = combined((r0, r1, r2, r3), 16)
    col_lse, col_mean = combined((c0, c1), 8)
    picked = r0[32:33, 0:1] + r1[32:33, 0:1] + r2[32:33, 0:1] + r3[32:33, 0:1]
    row_shift[...] = row_lse + 1.0
    col_shift[...] = col_lse + 1.0
    row_tail = in_parts(
        (jnp.sum(row_lse, keepdims=True) - 2.0 * picked) * LN2,
        (jnp.sum(row_mean, keepdims=True) - 2.0 * picked) * LN2,
    )
    col_tail = in_parts(jnp.sum(col_lse, keepdims=True) * LN2, jnp.sum(col_mean, keepdims=True) * LN2)
    columns = jnp.concatenate(
        [col_shift[pl.ds(row_of(j, t), 1), :] for j in range(2) for t in range(4)], axis=1
    )
    lanes = lax.broadcasted_iota(jnp.int32, (ROWS, 8 * ROWS), 1)
    for q, (rows_ref, g_ref) in enumerate(zip((i0, i1, i2, i3), (g0, g1, g2, g3))):
        for h in range(QUAD // CHUNK):
            rows = rows_ref[h * CHUNK : (h + 1) * CHUNK, :]
            logits = logits2(rows, (t0, t1), scale2)
            pieces = []
            for b in range(CHUNK // ROWS):
                place = col_of(q, h * (CHUNK // ROWS) + b)
                shift = jnp.transpose(
                    jnp.broadcast_to(row_shift[pl.ds(place, 1), :], (ROWS, ROWS))
                )
                pos = pos_ref[pl.ds(pl.multiple_of(place * ROWS, ROWS), ROWS), :]
                shift = jnp.concatenate([shift] * 8, axis=1)
                pos = jnp.concatenate([pos] * 8, axis=1)
                part = logits[b * ROWS : (b + 1) * ROWS]
                soft = jnp.exp2(part - shift) + jnp.exp2(part - columns)
                pieces.append(jnp.where(pos == lanes, soft - 1.0, soft).astype(BF16))
            grad = jnp.concatenate(pieces, axis=0)
            product = jnp.dot(grad[:, :QUAD], t0[...], preferred_element_type=F32)
            product += jnp.dot(grad[:, QUAD:], t1[...], preferred_element_type=F32)
            g_ref[h * CHUNK : (h + 1) * CHUNK, :] = (scale * product).astype(BF16)
            update = lax.dot_general(grad, rows, (((0,), (0,)), ((), ())), preferred_element_type=F32)
            if q == 0 and h == 0:
                acc[...] = update
            else:
                acc[...] += update
        g_ref[QUAD : QUAD + EXTRA, :] = col_tail
    h0[0:QUAD, :] = (scale * acc[0:QUAD, :]).astype(BF16)
    h1[0:QUAD, :] = (scale * acc[QUAD : 2 * QUAD, :]).astype(BF16)
    h0[QUAD : QUAD + EXTRA, :] = row_tail
    h1[QUAD : QUAD + EXTRA, :] = row_tail


def tail_sum(refs, first):
    total = sum(r[first : first + EXTRA, :].astype(F32) for r in refs)
    total = jnp.sum(total, axis=0, keepdims=True)
    return total[:, 0:1], total[:, 1:2]


def partial_kernel(*refs):
    sources, outs = refs[:-4], refs[-4:]
    tail = in_parts(*tail_sum(sources, QUAD))
    for t, out in enumerate(outs):
        rows = slice(t * ROWS, (t + 1) * ROWS)
        out[0:ROWS, :] = sum(r[rows, :].astype(F32) for r in sources).astype(BF16)
        out[ROWS : ROWS + EXTRA, :] = tail


def finish_kernel(batch, img_ref, txt_ref, a0, a1, a2, a3, b0, b1, b2, b3, img_out, txt_out, loss_out, temp_out):
    for raw, parts, out in ((img_ref, (a0, a1, a2, a3), img_out), (txt_ref, (b0, b1, b2, b3), txt_out)):
        unit, inverse = unit_rows(raw[...])
        grad = sum(p[0:ROWS, :].astype(F32) for p in parts)
        out[...] = inverse * (grad - unit * jnp.sum(unit * grad, axis=1, keepdims=True))
    cols = tail_sum((a0, a1, a2, a3), ROWS)
    rows = tail_sum((b0, b1, b2, b3), ROWS)
    loss_out[0] = jnp.sum(cols[0] + rows[0]) / (2 * batch)
    temp_out[0] = jnp.sum(cols[1] + rows[1]) / (2 * batch)


def gathered(value, moves):
    return [value] + [shifted(value, moves(by)) for by in OFFS[1:]]


def scattered(parts, moves):
    return [parts[0]] + [shifted(p, moves(-by)) for p, by in zip(parts[1:], OFFS[1:])]


def on_device(images, texts, partner, log_scale):
    row, col = lax.axis_index("row"), lax.axis_index("col")
    ids = jnp.stack([row, col]).astype(jnp.int32)
    scale = jnp.exp(log_scale)
    unit_img, unit_txt = call(unit_kernel, [shape((ROWS, WIDTH), BF16)] * 2, images, texts)
    txt0 = jnp.concatenate(gathered(unit_txt, ring_z), axis=0)
    img_own = jnp.concatenate(gathered(unit_img, ring_a), axis=0)
    txt1 = shifted(txt0, other_core)
    imgs = gathered(img_own, ring_b)

    owner = partner // (16 * ROWS)
    steps = (row // 2 - owner // 2) % 4
    slot = steps % 2 * 2 + steps // 2
    core = jnp.where(owner % 2 == row % 2, 0, 1)
    pos = (core * 4 + slot) * ROWS + partner % ROWS
    pos = jnp.where(partner // ROWS % 16 == col, pos, -1)
    pos = jnp.broadcast_to(pos[:, None], (16 * ROWS, ROWS))

    row_stat, col_stat = call(
        forward_kernel,
        [shape((40, ROWS), F32), shape((16, ROWS), F32)],
        ids, scale, pos, *imgs, txt0, txt1,
        specs=[SMEM, SMEM] + [VMEM] * 7,
        scratch=[pltpu.VMEM((8, 8 * ROWS), F32)],
    )
    row_stat, col_stat = call(
        combine_kernel,
        [shape((40, ROWS), F32), shape((16, ROWS), F32)],
        *gathered(row_stat, ring_a), *gathered(col_stat, ring_z),
    )
    row_stats = gathered(row_stat, ring_b)
    col_stats = [col_stat, shifted(col_stat, other_core)]

    sent = shape((QUAD + EXTRA, WIDTH), BF16)
    grads = call(
        backward_kernel,
        [sent] * 6,
        ids, scale, pos, *row_stats, *col_stats, *imgs, txt0, txt1,
        specs=[SMEM, SMEM] + [VMEM] * 13,
        scratch=[
            pltpu.VMEM((16, ROWS), F32),
            pltpu.VMEM((8, ROWS), F32),
            pltpu.VMEM((8 * ROWS, WIDTH), F32),
        ],
    )
    small = [shape((ROWS + EXTRA, WIDTH), BF16)] * 4
    txt_parts = call(partial_kernel, small, grads[4], shifted(grads[5], other_core))
    img_parts = call(partial_kernel, small, *scattered(grads[:4], ring_b))
    txt_parts = scattered(txt_parts, ring_z)
    img_parts = scattered(img_parts, ring_a)
    whole = shape((ROWS, WIDTH), F32)
    one = shape((1,), F32)
    return pl.pallas_call(
        functools.partial(finish_kernel, 128 * ROWS),
        out_shape=(whole, whole, one, one),
        in_specs=[VMEM] * 10,
        out_specs=(VMEM, VMEM, SMEM, SMEM),
        compiler_params=PARAMS,
    )(images, texts, *img_parts, *txt_parts)


def solution(mesh):
    placed = (P(("row", "col"), None), P(("row", "col"), None), P("row"), P())
    return jax.shard_map(
        on_device,
        mesh=mesh,
        in_specs=placed,
        out_specs=(P(("row", "col"), None), P(("row", "col"), None), P(), P()),
        check_vma=False,
    )
```

time: 377 us -> 112 us (0.30)
  blocking collectives: 196 us -> 0 us
  matrix products: 42.9 us -> 0 us
  starting transfers between devices: 0.16 us -> 38.3 us
  waiting for transfers between devices: 78.8 us -> 50.8 us
  other arithmetic: 23.4 us -> 0.13 us
  between operations: 21.5 us -> 1.69 us
  Pallas kernels: 0 us -> 18.7 us
  loops' own time: 5.54 us -> 0 us
  local copies, waits for them, and re-layouts: 7.46 us -> 2.22 us
    psum x3 -> x0, blocking collectives: 145 us -> none  [the longest x1 69.5 us: on_device(): lax.psum((row_local[1] * row_rescale, row_local[2] * row_rescale), 'col')]
    all_gather x2 -> x0, waiting for transfers between devices: 69.6 us -> none  [the longest x1 47.4 us: on_device(): lax.all_gather(unit_img.astype(jnp.bfloat16), 'col', axis=0, tiled=True)]
    pmax x2 -> x0, blocking collectives: 51 us -> none  [the longest x1 38.6 us: on_device(): row_high = lax.pmax(row_local[0], 'col')]
    ppermute x0 -> x30, waiting for transfers between devices: none -> 50.8 us  [shifted(): return lax.ppermute(value, RC, pairs)]
    dot_general x12 -> x0, matrix products: 42.9 us -> none  [the longest x4 20 us: add_block(): lax.dot_general(grad_tile, row_piece, (((0,), (0,)), ((), ())), preferred...]
    ppermute x0 -> x30, starting transfers between devices: none -> 38.3 us  [shifted(): return lax.ppermute(value, RC, pairs)]
    pallas_call x0 -> x7, Pallas kernels: none -> 18.7 us  [the longest x6 17.6 us: call(): pl.pallas_call(kernel, out_shape=outs, in_specs=specs or [VMEM] * len(arg...]
    reduce_sum x12 -> x0, other arithmetic: 13.6 us -> none  [the longest x4 6.79 us: forward(): jnp.sum(weights * logits, axis=1)]
  transfers between devices with their start and end apart: 4 -> 30, of which waited for: 3 -> 17; matrix products, arithmetic and copies ran while one was open for 7% -> 0% of each run, Pallas kernels for 0% -> 0%
where the time goes in v1:
time: 112 us
  waiting for transfers between devices  50.8 us (45%)
  starting transfers between devices  38.3 us (34%)
  Pallas kernels  18.7 us (17%)
  local copies, waits for them, and re-layouts  2.22 us (2%)
  between operations  1.69 us (2%)
    ppermute x30, waiting for transfers between devices, shifted(): return lax.ppermute(value, RC, pairs)  50.8 us
    ppermute x30, starting transfers between devices, shifted(): return lax.ppermute(value, RC, pairs)  38.3 us
    pallas_call x6, Pallas kernels, call(): pl.pallas_call(kernel, out_shape=outs, in_specs=specs or [VMEM] * len(arg...  17.6 us
  transfers between devices with their start and end apart: 30, of which 17 were waited for; matrix products, arithmetic and copies ran while one was open for 0% of the time, Pallas kernels for 0%

profile of v1, /device:TPU:0, one launch (start us, length us, event | category | flops | bytes accessed | tf_op | source)
XLA Modules:
  0.0 111.8 jit_solution(15176260328229494577)
XLA Ops:
  0.6 0.0 copy-start
  0.6 0.9 copy-done
  1.5 0.9 copy-done.2
  2.4 0.1 shard_map.75
  2.6 2.9 %collective-permute-start.2 = (bf16[128,512]{1,0:T(8,128)(2,1)S(1)}, bf16[128,512]{1,0:T(8,128)(2,1)S(1)}, u32[]{:S(2)}, u32[]{:S(2)}) collective-permute-start(bf16[128,512]{1,0:T(8,128)(2,1)S(1)} %get-tuple-element.24), channel_id=1, source_target_pairs={{0,12},{1,13},{2,14},{3,15},{4,0},{5,1},{6,2},{7,3},{8,4},{9,5},{1... | collective-permute-start | bytes 393224 | tf_op jit(solution)/shard_map/ppermute | solution.py:36
  5.5 0.0 collective-permute-start.1
  5.5 2.3 %collective-permute-start = (bf16[128,512]{1,0:T(8,128)(2,1)S(1)}, bf16[128,512]{1,0:T(8,128)(2,1)S(1)}, u32[]{:S(2)}, u32[]{:S(2)}) collective-permute-start(bf16[128,512]{1,0:T(8,128)(2,1)S(1)} %get-tuple-element.24), channel_id=1, source_target_pairs={{0,8},{1,9},{2,10},{3,11},{4,12},{5,13},{6,14},{7,15},{8,0},{9,1},... | collective-permute-start | bytes 393224 | tf_op jit(solution)/shard_map/ppermute | solution.py:36
  7.8 1.9 %collective-permute-start.7 = (bf16[128,512]{1,0:T(8,128)(2,1)S(1)}, bf16[128,512]{1,0:T(8,128)(2,1)S(1)}, u32[]{:S(2)}, u32[]{:S(2)}) collective-permute-start(bf16[128,512]{1,0:T(8,128)(2,1)S(1)} %get-tuple-element.25), channel_id=1, source_target_pairs={{0,32},{1,33},{2,34},{3,35},{4,36},{5,37},{6,38},{7,39},{8,40},{9,... | collective-permute-start | bytes 393224 | tf_op jit(solution)/shard_map/ppermute | solution.py:36
  9.7 3.6 %collective-permute-start.6 = (bf16[128,512]{1,0:T(8,128)(2,1)S(1)}, bf16[128,512]{1,0:T(8,128)(2,1)S(1)}, u32[]{:S(2)}, u32[]{:S(2)}) collective-permute-start(bf16[128,512]{1,0:T(8,128)(2,1)S(1)} %get-tuple-element.25), channel_id=1, source_target_pairs={{0,64},{1,65},{2,66},{3,67},{4,68},{5,69},{6,70},{7,71},{8,72},{9,... | collective-permute-start | bytes 393224 | tf_op jit(solution)/shard_map/ppermute | solution.py:36
  13.3 5.3 %collective-permute-done.6 = bf16[128,512]{1,0:T(8,128)(2,1)S(1)} collective-permute-done((bf16[128,512]{1,0:T(8,128)(2,1)S(1)}, bf16[128,512]{1,0:T(8,128)(2,1)S(1)}, u32[]{:S(2)}, u32[]{:S(2)}) %collective-permute-start.6) | collective-permute-done | bytes 131104 | tf_op jit(solution)/shard_map/ppermute | solution.py:36
  18.7 4.9 %collective-permute-done.8 = bf16[128,512]{1,0:T(8,128)(2,1)S(1)} collective-permute-done((bf16[128,512]{1,0:T(8,128)(2,1)S(1)}, bf16[128,512]{1,0:T(8,128)(2,1)S(1)}, u32[]{:S(2)}, u32[]{:S(2)}) %collective-permute-start.8) | collective-permute-done | bytes 131104 | tf_op jit(solution)/shard_map/ppermute | solution.py:36
  23.6 0.1 collective-permute-start.9
  23.7 0.0 collective-permute-done.1
  23.8 0.0 collective-permute-done.2
  23.8 2.1 %collective-permute-start.5 = (bf16[512,512]{1,0:T(8,128)(2,1)S(1)}, bf16[512,512]{1,0:T(8,128)(2,1)S(1)}, u32[]{:S(2)}, u32[]{:S(2)}) collective-permute-start(bf16[512,512]{1,0:T(8,128)(2,1)S(1)} %constant_dynamic-update-slice_fusion.i0), channel_id=1, source_target_pairs={{0,3},{1,0},{2,1},{3,2},{4,7},{5,4},{6,5},{7,6},{8,11},{9,8},{10,9... | collective-permute-start | bytes 1572872 | tf_op jit(solution)/shard_map/ppermute | solution.py:36
  25.9 0.0 collective-permute-start.4
  25.9 2.2 %collective-permute-start.3 = (bf16[512,512]{1,0:T(8,128)(2,1)S(1)}, bf16[512,512]{1,0:T(8,128)(2,1)S(1)}, u32[]{:S(2)}, u32[]{:S(2)}) collective-permute-start(bf16[512,512]{1,0:T(8,128)(2,1)S(1)} %constant_dynamic-update-slice_fusion.i0), channel_id=1, source_target_pairs={{0,2},{1,3},{2,0},{3,1},{4,6},{5,7},{6,4},{7,5},{8,10},{9,11},{10,... | collective-permute-start | bytes 1572872 | tf_op jit(solution)/shard_map/ppermute | solution.py:36
  28.8 0.1 pad_add_fusion.ids_ref
  28.9 0.0 collective-permute-done.9.t1
  28.9 9.3 %collective-permute-done.5.i3 = bf16[512,512]{1,0:T(8,128)(2,1)S(1)} collective-permute-done((bf16[512,512]{1,0:T(8,128)(2,1)S(1)}, bf16[512,512]{1,0:T(8,128)(2,1)S(1)}, u32[]{:S(2)}, u32[]{:S(2)}) %collective-permute-start.5) | collective-permute-done | bytes 524320 | tf_op jit(solution)/shard_map/ppermute | solution.py:36
  38.2 3.7 %collective-permute-done.4.i2 = bf16[512,512]{1,0:T(8,128)(2,1)S(1)} collective-permute-done((bf16[512,512]{1,0:T(8,128)(2,1)S(1)}, bf16[512,512]{1,0:T(8,128)(2,1)S(1)}, u32[]{:S(2)}, u32[]{:S(2)}) %collective-permute-start.4) | collective-permute-done | bytes 524320 | tf_op jit(solution)/shard_map/ppermute | solution.py:36
  41.9 0.0 collective-permute-done.3.i1
  41.9 0.3 broadcast_in_dim.8.pos_ref
  42.2 7.6 %shard_map.76 = (f32[40,128]{1,0:T(8,128)S(1)}, f32[16,128]{1,0:T(8,128)S(1)}) custom-call(s32[2]{0:T(128)S(1)} %pad_add_fusion.ids_ref, f32[1]{0:T(128)S(6)} %exp.3.scale_ref, s32[2048,128]{1,0:T(8,128)S(1)} %broadcast_in_dim.8.pos_ref, bf16[512,512]{1,0:T(8,128)(2,1)S(1)} %constant_dynamic-update-slice_fusion.i0, ...), custom_call_target="tpu_custom_call" | custom-call | tf_op jit(solution)/shard_map/pallas_call | solution.py:56
  49.8 2.1 %collective-permute-start.12 = (f32[40,128]{1,0:T(8,128)S(1)}, f32[40,128]{1,0:T(8,128)S(1)}, u32[]{:S(2)}, u32[]{:S(2)}) collective-permute-start(f32[40,128]{1,0:T(8,128)S(1)} %get-tuple-element.26.r0), channel_id=1, source_target_pairs={{0,12},{1,13},{2,14},{3,15},{4,0},{5,1},{6,2},{7,3},{8,4},{9,5},{1... | collective-permute-start | bytes 61448 | tf_op jit(solution)/shard_map/ppermute | solution.py:36
  51.9 2.3 %collective-permute-start.10 = (f32[40,128]{1,0:T(8,128)S(1)}, f32[40,128]{1,0:T(8,128)S(1)}, u32[]{:S(2)}, u32[]{:S(2)}) collective-permute-start(f32[40,128]{1,0:T(8,128)S(1)} %get-tuple-element.26.r0), channel_id=1, source_target_pairs={{0,8},{1,9},{2,10},{3,11},{4,12},{5,13},{6,14},{7,15},{8,0},{9,1},... | collective-permute-start | bytes 61448 | tf_op jit(solution)/shard_map/ppermute | solution.py:36
  54.2 1.4 %collective-permute-start.15 = (f32[16,128]{1,0:T(8,128)S(1)}, f32[16,128]{1,0:T(8,128)S(1)}, u32[]{:S(2)}, u32[]{:S(2)}) collective-permute-start(f32[16,128]{1,0:T(8,128)S(1)} %get-tuple-element.27.c0), channel_id=1, source_target_pairs={{0,96},{1,97},{2,98},{3,99},{4,100},{5,101},{6,102},{7,103},{8,104... | collective-permute-start | bytes 24584 | tf_op jit(solution)/shard_map/ppermute | solution.py:36
  55.6 0.6 collective-permute-start.14
  56.2 1.6 %collective-permute-done.15.c3 = f32[16,128]{1,0:T(8,128)S(1)} collective-permute-done((f32[16,128]{1,0:T(8,128)S(1)}, f32[16,128]{1,0:T(8,128)S(1)}, u32[]{:S(2)}, u32[]{:S(2)}) %collective-permute-start.15) | collective-permute-done | bytes 8224 | tf_op jit(solution)/shard_map/ppermute | solution.py:36
  57.8 1.7 %collective-permute-start.13 = (f32[16,128]{1,0:T(8,128)S(1)}, f32[16,128]{1,0:T(8,128)S(1)}, u32[]{:S(2)}, u32[]{:S(2)}) collective-permute-start(f32[16,128]{1,0:T(8,128)S(1)} %get-tuple-element.27.c0), channel_id=1, source_target_pairs={{0,64},{1,65},{2,66},{3,67},{4,68},{5,69},{6,70},{7,71},{8,72},{9,... | collective-permute-start | bytes 24584 | tf_op jit(solution)/shard_map/ppermute | solution.py:36
  59.5 1.0 collective-permute-done.14.c2
  60.5 2.5 %collective-permute-done.13.c1 = f32[16,128]{1,0:T(8,128)S(1)} collective-permute-done((f32[16,128]{1,0:T(8,128)S(1)}, f32[16,128]{1,0:T(8,128)S(1)}, u32[]{:S(2)}, u32[]{:S(2)}) %collective-permute-start.13) | collective-permute-done | bytes 8224 | tf_op jit(solution)/shard_map/ppermute | solution.py:36
  63.0 0.7 collective-permute-start.18
  63.8 1.4 %collective-permute-start.17 = (f32[40,128]{1,0:T(8,128)S(1)}, f32[40,128]{1,0:T(8,128)S(1)}, u32[]{:S(2)}, u32[]{:S(2)}) collective-permute-start(f32[40,128]{1,0:T(8,128)S(1)} %get-tuple-element.28.r0), channel_id=1, source_target_pairs={{0,1},{1,2},{2,3},{3,0},{4,5},{5,6},{6,7},{7,4},{8,9},{9,10},{10,1... | collective-permute-start | bytes 61448 | tf_op jit(solution)/shard_map/ppermute | solution.py:36
  65.1 1.5 %collective-permute-start.16 = (f32[40,128]{1,0:T(8,128)S(1)}, f32[40,128]{1,0:T(8,128)S(1)}, u32[]{:S(2)}, u32[]{:S(2)}) collective-permute-start(f32[40,128]{1,0:T(8,128)S(1)} %get-tuple-element.28.r0), channel_id=1, source_target_pairs={{0,2},{1,3},{2,0},{3,1},{4,6},{5,7},{6,4},{7,5},{8,10},{9,11},{10,... | collective-permute-start | bytes 61448 | tf_op jit(solution)/shard_map/ppermute | solution.py:36
  66.7 0.0 collective-permute-start.19
  66.7 1.2 %collective-permute-done.19.c1 = f32[16,128]{1,0:T(8,128)S(1)} collective-permute-done((f32[16,128]{1,0:T(8,128)S(1)}, f32[16,128]{1,0:T(8,128)S(1)}, u32[]{:S(2)}, u32[]{:S(2)}) %collective-permute-start.19) | collective-permute-done | bytes 8224 | tf_op jit(solution)/shard_map/ppermute | solution.py:36
  67.8 0.0 collective-permute-done.18.r3
  67.8 0.9 collective-permute-done.17.r2
  68.8 1.7 %collective-permute-done.16.r1 = f32[40,128]{1,0:T(8,128)S(1)} collective-permute-done((f32[40,128]{1,0:T(8,128)S(1)}, f32[40,128]{1,0:T(8,128)S(1)}, u32[]{:S(2)}, u32[]{:S(2)}) %collective-permute-start.16) | collective-permute-done | bytes 20512 | tf_op jit(solution)/shard_map/ppermute | solution.py:36
  70.4 9.4 %shard_map.78 = (bf16[528,512]{1,0:T(8,128)(2,1)S(1)}, bf16[528,512]{1,0:T(8,128)(2,1)S(1)}, bf16[528,512]{1,0:T(8,128)(2,1)S(1)}, bf16[528,512]{1,0:T(8,128)(2,...) custom-call(s32[2]{0:T(128)S(1)} %pad_add_fusion.ids_ref, f32[1]{0:T(128)S(6)} %exp.3.scale_ref, ...), custom_call_target="tpu_custom_call" | custom-call | tf_op jit(solution)/shard_map/pallas_call | solution.py:56
  79.8 1.6 %collective-permute-start.20 = (bf16[528,512]{1,0:T(8,128)(2,1)S(1)}, bf16[528,512]{1,0:T(8,128)(2,1)S(1)}, u32[]{:S(2)}, u32[]{:S(2)}) collective-permute-start(bf16[528,512]{1,0:T(8,128)(2,1)S(1)} %get-tuple-element.31), channel_id=1, source_target_pairs={{0,2},{1,3},{2,0},{3,1},{4,6},{5,7},{6,4},{7,5},{8,10},{9,11},{10,... | collective-permute-start | bytes 1622024 | tf_op jit(solution)/shard_map/ppermute | solution.py:36
  81.4 1.1 %collective-permute-start.21 = (bf16[528,512]{1,0:T(8,128)(2,1)S(1)}, bf16[528,512]{1,0:T(8,128)(2,1)S(1)}, u32[]{:S(2)}, u32[]{:S(2)}) collective-permute-start(bf16[528,512]{1,0:T(8,128)(2,1)S(1)} %get-tuple-element.32), channel_id=1, source_target_pairs={{0,3},{1,0},{2,1},{3,2},{4,7},{5,4},{6,5},{7,6},{8,11},{9,8},{10,9... | collective-permute-start | bytes 1622024 | tf_op jit(solution)/shard_map/ppermute | solution.py:36
  82.6 0.9 collective-permute-start.22
  83.4 0.0 collective-permute-start.26
  83.4 7.4 %collective-permute-done.20.refs_1_ = bf16[528,512]{1,0:T(8,128)(2,1)S(1)} collective-permute-done((bf16[528,512]{1,0:T(8,128)(2,1)S(1)}, bf16[528,512]{1,0:T(8,128)(2,1)S(1)}, u32[]{:S(2)}, u32[]{:S(2)}) %collective-permute-start.20) | collective-permute-done | bytes 540704 | tf_op jit(solution)/shard_map/ppermute | solution.py:36
  90.8 4.9 %collective-permute-done.21.refs_2_ = bf16[528,512]{1,0:T(8,128)(2,1)S(1)} collective-permute-done((bf16[528,512]{1,0:T(8,128)(2,1)S(1)}, bf16[528,512]{1,0:T(8,128)(2,1)S(1)}, u32[]{:S(2)}, u32[]{:S(2)}) %collective-permute-start.21) | collective-permute-done | bytes 540704 | tf_op jit(solution)/shard_map/ppermute | solution.py:36
  95.8 0.7 collective-permute-done.22.refs_3_
  96.5 0.3 shard_map.79
  96.9 1.3 %collective-permute-start.23 = (bf16[144,512]{1,0:T(8,128)(2,1)S(1)}, bf16[144,512]{1,0:T(8,128)(2,1)S(1)}, u32[]{:S(2)}, u32[]{:S(2)}) collective-permute-start(bf16[144,512]{1,0:T(8,128)(2,1)S(1)} %get-tuple-element.35), channel_id=1, source_target_pairs={{0,8},{1,9},{2,10},{3,11},{4,12},{5,13},{6,14},{7,15},{8,0},{9,1},... | collective-permute-start | bytes 442376 | tf_op jit(solution)/shard_map/ppermute | solution.py:36
  98.2 3.2 %collective-permute-start.24 = (bf16[144,512]{1,0:T(8,128)(2,1)S(1)}, bf16[144,512]{1,0:T(8,128)(2,1)S(1)}, u32[]{:S(2)}, u32[]{:S(2)}) collective-permute-start(bf16[144,512]{1,0:T(8,128)(2,1)S(1)} %get-tuple-element.36), channel_id=1, source_target_pairs={{0,12},{1,13},{2,14},{3,15},{4,0},{5,1},{6,2},{7,3},{8,4},{9,5},{1... | collective-permute-start | bytes 442376 | tf_op jit(solution)/shard_map/ppermute | solution.py:36
  101.5 0.0 collective-permute-done.26.refs_1_
  101.5 0.0 copy-start.3
  101.5 0.2 shard_map.80
  101.7 1.3 %collective-permute-start.27 = (bf16[144,512]{1,0:T(8,128)(2,1)S(1)}, bf16[144,512]{1,0:T(8,128)(2,1)S(1)}, u32[]{:S(2)}, u32[]{:S(2)}) collective-permute-start(bf16[144,512]{1,0:T(8,128)(2,1)S(1)} %get-tuple-element.41), channel_id=1, source_target_pairs={{0,64},{1,65},{2,66},{3,67},{4,68},{5,69},{6,70},{7,71},{8,72},{9,... | collective-permute-start | bytes 442376 | tf_op jit(solution)/shard_map/ppermute | solution.py:36
  102.9 1.3 %collective-permute-start.28 = (bf16[144,512]{1,0:T(8,128)(2,1)S(1)}, bf16[144,512]{1,0:T(8,128)(2,1)S(1)}, u32[]{:S(2)}, u32[]{:S(2)}) collective-permute-start(bf16[144,512]{1,0:T(8,128)(2,1)S(1)} %get-tuple-element.42), channel_id=1, source_target_pairs={{0,96},{1,97},{2,98},{3,99},{4,100},{5,101},{6,102},{7,103},{8,104... | collective-permute-start | bytes 442376 | tf_op jit(solution)/shard_map/ppermute | solution.py:36
  104.2 0.0 collective-permute-done.23.a1
  104.2 0.8 collective-permute-start.29
  105.0 0.0 collective-permute-done.24.a2
  105.0 2.8 %collective-permute-done.25.a3 = bf16[144,512]{1,0:T(8,128)(2,1)S(1)} collective-permute-done((bf16[144,512]{1,0:T(8,128)(2,1)S(1)}, bf16[144,512]{1,0:T(8,128)(2,1)S(1)}, u32[]{:S(2)}, u32[]{:S(2)}) %collective-permute-start.25) | collective-permute-done | bytes 147488 | tf_op jit(solution)/shard_map/ppermute | solution.py:36
  107.8 0.6 collective-permute-done.27.b1
  108.4 1.4 %collective-permute-done.28.b2 = bf16[144,512]{1,0:T(8,128)(2,1)S(1)} collective-permute-done((bf16[144,512]{1,0:T(8,128)(2,1)S(1)}, bf16[144,512]{1,0:T(8,128)(2,1)S(1)}, u32[]{:S(2)}, u32[]{:S(2)}) %collective-permute-start.28) | collective-permute-done | bytes 147488 | tf_op jit(solution)/shard_map/ppermute | solution.py:36
  109.7 0.8 collective-permute-done.29.b3
  110.6 1.1 shard_map.81
  (24 shorter events, 0.2 us)
Async XLA Ops:
  0.6 0.9 copy-start
  1.5 0.9 copy-start.2
  2.6 21.2 %collective-permute-start.2 = (bf16[128,512]{1,0:T(8,128)(2,1)S(1)}, bf16[128,512]{1,0:T(8,128)(2,1)S(1)}, u32[]{:S(2)}, u32[]{:S(2)}) collective-permute-start(bf16[128,512]{1,0:T(8,128)(2,1)S(1)} %get-tuple-element.24), channel_id=1, source_target_pairs={{0,12},{1,13},{2,14},{3,15},{4,0},{5,1},{6,2},{7,3},{8,4},{9,5},{1... | collective-permute-start | bytes 393224 | tf_op jit(solution)/shard_map/ppermute | solution.py:36
  5.5 18.2 %collective-permute-start.1 = (bf16[128,512]{1,0:T(8,128)(2,1)S(1)}, bf16[128,512]{1,0:T(8,128)(2,1)S(1)}, u32[]{:S(2)}, u32[]{:S(2)}) collective-permute-start(bf16[128,512]{1,0:T(8,128)(2,1)S(1)} %get-tuple-element.24), channel_id=1, source_target_pairs={{0,4},{1,5},{2,6},{3,7},{4,8},{5,9},{6,10},{7,11},{8,12},{9,13},{1... | collective-permute-start | bytes 393224 | tf_op jit(solution)/shard_map/ppermute | solution.py:36
  5.5 18.2 %collective-permute-start = (bf16[128,512]{1,0:T(8,128)(2,1)S(1)}, bf16[128,512]{1,0:T(8,128)(2,1)S(1)}, u32[]{:S(2)}, u32[]{:S(2)}) collective-permute-start(bf16[128,512]{1,0:T(8,128)(2,1)S(1)} %get-tuple-element.24), channel_id=1, source_target_pairs={{0,8},{1,9},{2,10},{3,11},{4,12},{5,13},{6,14},{7,15},{8,0},{9,1},... | collective-permute-start | bytes 393224 | tf_op jit(solution)/shard_map/ppermute | solution.py:36
  7.8 10.9 %collective-permute-start.7 = (bf16[128,512]{1,0:T(8,128)(2,1)S(1)}, bf16[128,512]{1,0:T(8,128)(2,1)S(1)}, u32[]{:S(2)}, u32[]{:S(2)}) collective-permute-start(bf16[128,512]{1,0:T(8,128)(2,1)S(1)} %get-tuple-element.25), channel_id=1, source_target_pairs={{0,32},{1,33},{2,34},{3,35},{4,36},{5,37},{6,38},{7,39},{8,40},{9,... | collective-permute-start | bytes 393224 | tf_op jit(solution)/shard_map/ppermute | solution.py:36
  9.7 8.9 %collective-permute-start.6 = (bf16[128,512]{1,0:T(8,128)(2,1)S(1)}, bf16[128,512]{1,0:T(8,128)(2,1)S(1)}, u32[]{:S(2)}, u32[]{:S(2)}) collective-permute-start(bf16[128,512]{1,0:T(8,128)(2,1)S(1)} %get-tuple-element.25), channel_id=1, source_target_pairs={{0,64},{1,65},{2,66},{3,67},{4,68},{5,69},{6,70},{7,71},{8,72},{9,... | collective-permute-start | bytes 393224 | tf_op jit(solution)/shard_map/ppermute | solution.py:36
  18.6 5.0 %collective-permute-start.8 = (bf16[128,512]{1,0:T(8,128)(2,1)S(1)}, bf16[128,512]{1,0:T(8,128)(2,1)S(1)}, u32[]{:S(2)}, u32[]{:S(2)}) collective-permute-start(bf16[128,512]{1,0:T(8,128)(2,1)S(1)} %get-tuple-element.25), channel_id=1, source_target_pairs={{0,96},{1,97},{2,98},{3,99},{4,100},{5,101},{6,102},{7,103},{8,104... | collective-permute-start | bytes 393224 | tf_op jit(solution)/shard_map/ppermute | solution.py:36
  23.6 5.3 %collective-permute-start.9 = (bf16[512,512]{1,0:T(8,128)(2,1)S(1)}, bf16[512,512]{1,0:T(8,128)(2,1)S(1)}, u32[]{:S(2)}, u32[]{:S(2)}) collective-permute-start(bf16[512,512]{1,0:T(8,128)(2,1)S(1)} %constant_dynamic-update-slice_fusion.4.t0), channel_id=1, source_target_pairs={{0,16},{1,17},{2,18},{3,19},{4,20},{5,21},{6,22},{7,23},{8,24},{9,... | collective-permute-start | bytes 1572872 | tf_op jit(solution)/shard_map/ppermute | solution.py:36
  23.8 14.4 %collective-permute-start.5 = (bf16[512,512]{1,0:T(8,128)(2,1)S(1)}, bf16[512,512]{1,0:T(8,128)(2,1)S(1)}, u32[]{:S(2)}, u32[]{:S(2)}) collective-permute-start(bf16[512,512]{1,0:T(8,128)(2,1)S(1)} %constant_dynamic-update-slice_fusion.i0), channel_id=1, source_target_pairs={{0,3},{1,0},{2,1},{3,2},{4,7},{5,4},{6,5},{7,6},{8,11},{9,8},{10,9... | collective-permute-start | bytes 1572872 | tf_op jit(solution)/shard_map/ppermute | solution.py:36
  25.9 16.0 %collective-permute-start.4 = (bf16[512,512]{1,0:T(8,128)(2,1)S(1)}, bf16[512,512]{1,0:T(8,128)(2,1)S(1)}, u32[]{:S(2)}, u32[]{:S(2)}) collective-permute-start(bf16[512,512]{1,0:T(8,128)(2,1)S(1)} %constant_dynamic-update-slice_fusion.i0), channel_id=1, source_target_pairs={{0,1},{1,2},{2,3},{3,0},{4,5},{5,6},{6,7},{7,4},{8,9},{9,10},{10,1... | collective-permute-start | bytes 1572872 | tf_op jit(solution)/shard_map/ppermute | solution.py:36
  25.9 16.0 %collective-permute-start.3 = (bf16[512,512]{1,0:T(8,128)(2,1)S(1)}, bf16[512,512]{1,0:T(8,128)(2,1)S(1)}, u32[]{:S(2)}, u32[]{:S(2)}) collective-permute-start(bf16[512,512]{1,0:T(8,128)(2,1)S(1)} %constant_dynamic-update-slice_fusion.i0), channel_id=1, source_target_pairs={{0,2},{1,3},{2,0},{3,1},{4,6},{5,7},{6,4},{7,5},{8,10},{9,11},{10,... | collective-permute-start | bytes 1572872 | tf_op jit(solution)/shard_map/ppermute | solution.py:36
  28.1 0.8 copy-start.4
  49.8 13.2 %collective-permute-start.12 = (f32[40,128]{1,0:T(8,128)S(1)}, f32[40,128]{1,0:T(8,128)S(1)}, u32[]{:S(2)}, u32[]{:S(2)}) collective-permute-start(f32[40,128]{1,0:T(8,128)S(1)} %get-tuple-element.26.r0), channel_id=1, source_target_pairs={{0,12},{1,13},{2,14},{3,15},{4,0},{5,1},{6,2},{7,3},{8,4},{9,5},{1... | collective-permute-start | bytes 61448 | tf_op jit(solution)/shard_map/ppermute | solution.py:36
  51.9 11.1 %collective-permute-start.11 = (f32[40,128]{1,0:T(8,128)S(1)}, f32[40,128]{1,0:T(8,128)S(1)}, u32[]{:S(2)}, u32[]{:S(2)}) collective-permute-start(f32[40,128]{1,0:T(8,128)S(1)} %get-tuple-element.26.r0), channel_id=1, source_target_pairs={{0,4},{1,5},{2,6},{3,7},{4,8},{5,9},{6,10},{7,11},{8,12},{9,13},{1... | collective-permute-start | bytes 61448 | tf_op jit(solution)/shard_map/ppermute | solution.py:36
  51.9 11.1 %collective-permute-start.10 = (f32[40,128]{1,0:T(8,128)S(1)}, f32[40,128]{1,0:T(8,128)S(1)}, u32[]{:S(2)}, u32[]{:S(2)}) collective-permute-start(f32[40,128]{1,0:T(8,128)S(1)} %get-tuple-element.26.r0), channel_id=1, source_target_pairs={{0,8},{1,9},{2,10},{3,11},{4,12},{5,13},{6,14},{7,15},{8,0},{9,1},... | collective-permute-start | bytes 61448 | tf_op jit(solution)/shard_map/ppermute | solution.py:36
  54.2 3.7 %collective-permute-start.15 = (f32[16,128]{1,0:T(8,128)S(1)}, f32[16,128]{1,0:T(8,128)S(1)}, u32[]{:S(2)}, u32[]{:S(2)}) collective-permute-start(f32[16,128]{1,0:T(8,128)S(1)} %get-tuple-element.27.c0), channel_id=1, source_target_pairs={{0,96},{1,97},{2,98},{3,99},{4,100},{5,101},{6,102},{7,103},{8,104... | collective-permute-start | bytes 24584 | tf_op jit(solution)/shard_map/ppermute | solution.py:36
  55.6 4.9 %collective-permute-start.14 = (f32[16,128]{1,0:T(8,128)S(1)}, f32[16,128]{1,0:T(8,128)S(1)}, u32[]{:S(2)}, u32[]{:S(2)}) collective-permute-start(f32[16,128]{1,0:T(8,128)S(1)} %get-tuple-element.27.c0), channel_id=1, source_target_pairs={{0,32},{1,33},{2,34},{3,35},{4,36},{5,37},{6,38},{7,39},{8,40},{9,... | collective-permute-start | bytes 24584 | tf_op jit(solution)/shard_map/ppermute | solution.py:36
  57.8 5.2 %collective-permute-start.13 = (f32[16,128]{1,0:T(8,128)S(1)}, f32[16,128]{1,0:T(8,128)S(1)}, u32[]{:S(2)}, u32[]{:S(2)}) collective-permute-start(f32[16,128]{1,0:T(8,128)S(1)} %get-tuple-element.27.c0), channel_id=1, source_target_pairs={{0,64},{1,65},{2,66},{3,67},{4,68},{5,69},{6,70},{7,71},{8,72},{9,... | collective-permute-start | bytes 24584 | tf_op jit(solution)/shard_map/ppermute | solution.py:36
  63.0 4.8 %collective-permute-start.18 = (f32[40,128]{1,0:T(8,128)S(1)}, f32[40,128]{1,0:T(8,128)S(1)}, u32[]{:S(2)}, u32[]{:S(2)}) collective-permute-start(f32[40,128]{1,0:T(8,128)S(1)} %get-tuple-element.28.r0), channel_id=1, source_target_pairs={{0,3},{1,0},{2,1},{3,2},{4,7},{5,4},{6,5},{7,6},{8,11},{9,8},{10,9... | collective-permute-start | bytes 61448 | tf_op jit(solution)/shard_map/ppermute | solution.py:36
  63.8 5.0 %collective-permute-start.17 = (f32[40,128]{1,0:T(8,128)S(1)}, f32[40,128]{1,0:T(8,128)S(1)}, u32[]{:S(2)}, u32[]{:S(2)}) collective-permute-start(f32[40,128]{1,0:T(8,128)S(1)} %get-tuple-element.28.r0), channel_id=1, source_target_pairs={{0,1},{1,2},{2,3},{3,0},{4,5},{5,6},{6,7},{7,4},{8,9},{9,10},{10,1... | collective-permute-start | bytes 61448 | tf_op jit(solution)/shard_map/ppermute | solution.py:36
  65.1 5.3 %collective-permute-start.16 = (f32[40,128]{1,0:T(8,128)S(1)}, f32[40,128]{1,0:T(8,128)S(1)}, u32[]{:S(2)}, u32[]{:S(2)}) collective-permute-start(f32[40,128]{1,0:T(8,128)S(1)} %get-tuple-element.28.r0), channel_id=1, source_target_pairs={{0,2},{1,3},{2,0},{3,1},{4,6},{5,7},{6,4},{7,5},{8,10},{9,11},{10,... | collective-permute-start | bytes 61448 | tf_op jit(solution)/shard_map/ppermute | solution.py:36
  66.7 1.2 %collective-permute-start.19 = (f32[16,128]{1,0:T(8,128)S(1)}, f32[16,128]{1,0:T(8,128)S(1)}, u32[]{:S(2)}, u32[]{:S(2)}) collective-permute-start(f32[16,128]{1,0:T(8,128)S(1)} %get-tuple-element.29.c0), channel_id=1, source_target_pairs={{0,16},{1,17},{2,18},{3,19},{4,20},{5,21},{6,22},{7,23},{8,24},{9,... | collective-permute-start | bytes 24584 | tf_op jit(solution)/shard_map/ppermute | solution.py:36
  79.8 11.0 %collective-permute-start.20 = (bf16[528,512]{1,0:T(8,128)(2,1)S(1)}, bf16[528,512]{1,0:T(8,128)(2,1)S(1)}, u32[]{:S(2)}, u32[]{:S(2)}) collective-permute-start(bf16[528,512]{1,0:T(8,128)(2,1)S(1)} %get-tuple-element.31), channel_id=1, source_target_pairs={{0,2},{1,3},{2,0},{3,1},{4,6},{5,7},{6,4},{7,5},{8,10},{9,11},{10,... | collective-permute-start | bytes 1622024 | tf_op jit(solution)/shard_map/ppermute | solution.py:36
  81.4 14.4 %collective-permute-start.21 = (bf16[528,512]{1,0:T(8,128)(2,1)S(1)}, bf16[528,512]{1,0:T(8,128)(2,1)S(1)}, u32[]{:S(2)}, u32[]{:S(2)}) collective-permute-start(bf16[528,512]{1,0:T(8,128)(2,1)S(1)} %get-tuple-element.32), channel_id=1, source_target_pairs={{0,3},{1,0},{2,1},{3,2},{4,7},{5,4},{6,5},{7,6},{8,11},{9,8},{10,9... | collective-permute-start | bytes 1622024 | tf_op jit(solution)/shard_map/ppermute | solution.py:36
  82.6 14.0 %collective-permute-start.22 = (bf16[528,512]{1,0:T(8,128)(2,1)S(1)}, bf16[528,512]{1,0:T(8,128)(2,1)S(1)}, u32[]{:S(2)}, u32[]{:S(2)}) collective-permute-start(bf16[528,512]{1,0:T(8,128)(2,1)S(1)} %get-tuple-element.33), channel_id=1, source_target_pairs={{0,1},{1,2},{2,3},{3,0},{4,5},{5,6},{6,7},{7,4},{8,9},{9,10},{10,1... | collective-permute-start | bytes 1622024 | tf_op jit(solution)/shard_map/ppermute | solution.py:36
  83.4 18.0 %collective-permute-start.26 = (bf16[528,512]{1,0:T(8,128)(2,1)S(1)}, bf16[528,512]{1,0:T(8,128)(2,1)S(1)}, u32[]{:S(2)}, u32[]{:S(2)}) collective-permute-start(bf16[528,512]{1,0:T(8,128)(2,1)S(1)} %get-tuple-element.39), channel_id=1, source_target_pairs={{0,16},{1,17},{2,18},{3,19},{4,20},{5,21},{6,22},{7,23},{8,24},{9,... | collective-permute-start | bytes 1622024 | tf_op jit(solution)/shard_map/ppermute | solution.py:36
  96.9 7.3 %collective-permute-start.23 = (bf16[144,512]{1,0:T(8,128)(2,1)S(1)}, bf16[144,512]{1,0:T(8,128)(2,1)S(1)}, u32[]{:S(2)}, u32[]{:S(2)}) collective-permute-start(bf16[144,512]{1,0:T(8,128)(2,1)S(1)} %get-tuple-element.35), channel_id=1, source_target_pairs={{0,8},{1,9},{2,10},{3,11},{4,12},{5,13},{6,14},{7,15},{8,0},{9,1},... | collective-permute-start | bytes 442376 | tf_op jit(solution)/shard_map/ppermute | solution.py:36
  98.2 6.8 %collective-permute-start.24 = (bf16[144,512]{1,0:T(8,128)(2,1)S(1)}, bf16[144,512]{1,0:T(8,128)(2,1)S(1)}, u32[]{:S(2)}, u32[]{:S(2)}) collective-permute-start(bf16[144,512]{1,0:T(8,128)(2,1)S(1)} %get-tuple-element.36), channel_id=1, source_target_pairs={{0,12},{1,13},{2,14},{3,15},{4,0},{5,1},{6,2},{7,3},{8,4},{9,5},{1... | collective-permute-start | bytes 442376 | tf_op jit(solution)/shard_map/ppermute | solution.py:36
  101.5 6.4 %collective-permute-start.25 = (bf16[144,512]{1,0:T(8,128)(2,1)S(1)}, bf16[144,512]{1,0:T(8,128)(2,1)S(1)}, u32[]{:S(2)}, u32[]{:S(2)}) collective-permute-start(bf16[144,512]{1,0:T(8,128)(2,1)S(1)} %get-tuple-element.37), channel_id=1, source_target_pairs={{0,4},{1,5},{2,6},{3,7},{4,8},{5,9},{6,10},{7,11},{8,12},{9,13},{1... | collective-permute-start | bytes 442376 | tf_op jit(solution)/shard_map/ppermute | solution.py:36
  101.5 9.1 %copy-start.1 = (bf16[128,512]{1,0:T(8,128)(2,1)S(1)}, bf16[128,512]{1,0:T(8,128)(2,1)}, u32[]{:S(2)}) copy-start(bf16[128,512]{1,0:T(8,128)(2,1)} %img_ref.3) | copy-start | bytes 393220
  101.5 9.1 %copy-start.3 = (bf16[128,512]{1,0:T(8,128)(2,1)S(1)}, bf16[128,512]{1,0:T(8,128)(2,1)}, u32[]{:S(2)}) copy-start(bf16[128,512]{1,0:T(8,128)(2,1)} %txt_ref.3) | copy-start | bytes 393220
  101.7 6.7 %collective-permute-start.27 = (bf16[144,512]{1,0:T(8,128)(2,1)S(1)}, bf16[144,512]{1,0:T(8,128)(2,1)S(1)}, u32[]{:S(2)}, u32[]{:S(2)}) collective-permute-start(bf16[144,512]{1,0:T(8,128)(2,1)S(1)} %get-tuple-element.41), channel_id=1, source_target_pairs={{0,64},{1,65},{2,66},{3,67},{4,68},{5,69},{6,70},{7,71},{8,72},{9,... | collective-permute-start | bytes 442376 | tf_op jit(solution)/shard_map/ppermute | solution.py:36
  102.9 6.8 %collective-permute-start.28 = (bf16[144,512]{1,0:T(8,128)(2,1)S(1)}, bf16[144,512]{1,0:T(8,128)(2,1)S(1)}, u32[]{:S(2)}, u32[]{:S(2)}) collective-permute-start(bf16[144,512]{1,0:T(8,128)(2,1)S(1)} %get-tuple-element.42), channel_id=1, source_target_pairs={{0,96},{1,97},{2,98},{3,99},{4,100},{5,101},{6,102},{7,103},{8,104... | collective-permute-start | bytes 442376 | tf_op jit(solution)/shard_map/ppermute | solution.py:36
  104.2 6.4 %collective-permute-start.29 = (bf16[144,512]{1,0:T(8,128)(2,1)S(1)}, bf16[144,512]{1,0:T(8,128)(2,1)S(1)}, u32[]{:S(2)}, u32[]{:S(2)}) collective-permute-start(bf16[144,512]{1,0:T(8,128)(2,1)S(1)} %get-tuple-element.43), channel_id=1, source_target_pairs={{0,32},{1,33},{2,34},{3,35},{4,36},{5,37},{6,38},{7,39},{8,40},{9,... | collective-permute-start | bytes 442376 | tf_op jit(solution)/shard_map/ppermute | solution.py:36

commit v2 on v1

v2 whole, which is shorter than its diff:
```python
import functools

import jax
import jax.numpy as jnp
from jax import lax
from jax.experimental import pallas as pl
from jax.experimental.pallas import tpu as pltpu
from jax.sharding import PartitionSpec as P

ROWS = 128
WIDTH = 512
QUAD = 4 * ROWS
EXTRA = 16
OFFS = (0, 1, 3, 2)
LOG2E = 1.4426950408889634
LN2 = 0.6931471805599453
RC = ("row", "col")
F32 = jnp.float32
BF16 = jnp.bfloat16
VMEM = pl.BlockSpec(memory_space=pltpu.VMEM)
SMEM = pl.BlockSpec(memory_space=pltpu.SMEM)
PARAMS = pltpu.CompilerParams(vmem_limit_bytes=24 * 1024 * 1024)


def device(z, k, x, y):
    return (z * 2 + k) * 16 + x * 4 + y


def shifted(value, move):
    pairs = []
    for z in range(4):
        for k in range(2):
            for x in range(4):
                for y in range(4):
                    pairs.append((device(z, k, x, y), device(*move(z, k, x, y))))
    return lax.ppermute(value, RC, pairs)


def ring_a(by):
    return lambda z, k, x, y: (z, k, x, (y + by) % 4) if k else (z, k, (x + by) % 4, y)


def ring_b(by):
    return lambda z, k, x, y: (z, k, (x + by) % 4, y) if k else (z, k, x, (y + by) % 4)


def ring_z(by):
    return lambda z, k, x, y: ((z + by) % 4, k, x, y)


def other_core(z, k, x, y):
    return (z, 1 - k, x, y)


def call(kernel, outs, *args, specs=None, cost=None, scratch=()):
    return pl.pallas_call(
        kernel,
        out_shape=outs,
        in_specs=specs or [VMEM] * len(args),
        out_specs=jax.tree.map(lambda o: VMEM, outs),
        scratch_shapes=scratch,
        compiler_params=PARAMS,
        cost_estimate=cost,
    )(*args)


def shape(dims, dtype):
    return jax.ShapeDtypeStruct(dims, dtype)


def unit_rows(values):
    widened = values.astype(F32)
    inverse = lax.rsqrt(jnp.sum(widened * widened, axis=1, keepdims=True) + 1e-06)
    return widened * inverse, inverse


def unit_kernel(raw_ref, *refs):
    refs[-1][...] = unit_rows(raw_ref[...])[0].astype(BF16)


def after_kernel(*refs):
    refs[-1][...] = jnp.zeros_like(refs[-1])


def places(ids_ref):
    row, col = ids_ref[0], ids_ref[1]
    z, k, x, y = row // 2, row % 2, col // 4, col % 4
    pos_a = jnp.where(k == 0, x, y)
    pos_b = jnp.where(k == 0, y, x)

    def col_of(q, a):
        in_b = (pos_b + 4 - OFFS[q]) % 4
        in_a = (pos_a + 4 - OFFS[a]) % 4
        return jnp.where(k == 0, in_a * 4 + in_b, in_b * 4 + in_a)

    def row_of(j, t):
        return (z + 4 - OFFS[t]) % 4 * 2 + (k if j == 0 else 1 - k)

    return col_of, row_of


def to_lanes(column):
    return jnp.transpose(jnp.broadcast_to(column, (ROWS, ROWS)))[0:1, :]


def logits2(rows, t0, t1, scale2):
    parts = [
        lax.dot_general(rows, t[...], (((1,), (1,)), ((), ())), preferred_element_type=F32)
        for t in (t0, t1)
    ]
    return jnp.concatenate(parts, axis=1) * scale2


CHUNK = 256


def forward_kernel(
    ids_ref, scale_ref, pos_ref, i0, i1, i2, i3, t0, t1, _, row_out, col_out
):
    scale2 = scale_ref[0] * LOG2E
    col_of, row_of = places(ids_ref)
    lanes = lax.broadcasted_iota(jnp.int32, (CHUNK, 8 * ROWS), 1)
    col_high = jnp.full((1, 8 * ROWS), -jnp.inf, F32)
    col_total = col_weighted = picked = jnp.zeros((1, 8 * ROWS), F32)
    for q, rows_ref in enumerate((i0, i1, i2, i3)):
        for h in range(QUAD // CHUNK):
            logits = logits2(rows_ref[h * CHUNK : (h + 1) * CHUNK, :], t0, t1, scale2)
            high = jnp.max(logits, axis=1, keepdims=True)
            weights = jnp.exp2(logits - high)
            total = jnp.sum(weights, axis=1, keepdims=True)
            mean = jnp.sum(weights * logits, axis=1, keepdims=True) / total
            lse = high + jnp.log2(total)
            pos = []
            for b in range(CHUNK // ROWS):
                place = col_of(q, h * (CHUNK // ROWS) + b)
                row_out[pl.ds(place, 1), :] = to_lanes(lse[b * ROWS : (b + 1) * ROWS])
                row_out[pl.ds(16 + place, 1), :] = to_lanes(mean[b * ROWS : (b + 1) * ROWS])
                pos.append(pos_ref[pl.ds(pl.multiple_of(place * ROWS, ROWS), ROWS), :])
            pos = jnp.concatenate(pos, axis=0)
            pos = jnp.concatenate([pos] * 8, axis=1)
            picked += jnp.sum(jnp.where(pos == lanes, logits, 0.0), axis=0, keepdims=True)
            old = col_high
            col_high = jnp.maximum(old, jnp.max(logits, axis=0, keepdims=True))
            rescale = jnp.exp2(old - col_high)
            weights = jnp.exp2(logits - col_high)
            col_total = col_total * rescale + jnp.sum(weights, axis=0, keepdims=True)
            col_weighted = col_weighted * rescale + jnp.sum(weights * logits, axis=0, keepdims=True)
    row_out[32:40, :] = jnp.broadcast_to(jnp.sum(picked, axis=1, keepdims=True), (8, ROWS))
    col_lse = col_high + jnp.log2(col_total)
    col_mean = col_weighted / col_total
    for j in range(2):
        for t in range(4):
            at = (j * 4 + t) * ROWS
            place = row_of(j, t)
            col_out[pl.ds(place, 1), :] = col_lse[:, at : at + ROWS]
            col_out[pl.ds(8 + place, 1), :] = col_mean[:, at : at + ROWS]


def merged(parts, count):
    lse = [p[0:count, :] for p in parts]
    high = functools.reduce(jnp.maximum, lse)
    weights = [jnp.exp2(p - high) for p in lse]
    total = sum(weights)
    mean = sum(w * p[count : 2 * count, :] for w, p in zip(weights, parts)) / total
    return high + jnp.log2(total), mean


def merge_kernel(r0, r1, r2, r3, c0, c1, row_out, col_out):
    refs = (r0, r1, r2, r3)
    row_out[0:16, :], row_out[16:32, :] = merged(refs, 16)
    row_out[32:40, :] = sum(r[32:40, :] for r in refs)
    col_out[0:8, :], col_out[8:16, :] = merged((c0, c1), 8)


def in_parts(first, second):
    lane = lax.broadcasted_iota(jnp.int32, (EXTRA, WIDTH), 1)
    part = lax.broadcasted_iota(jnp.int32, (EXTRA, WIDTH), 0)
    value = jnp.where(lane == 0, first, jnp.where(lane == 1, second, 0.0))
    high = value.astype(BF16)
    rest = value - high.astype(F32)
    mid = rest.astype(BF16)
    low = (rest - mid.astype(F32)).astype(BF16)
    zero = jnp.zeros((EXTRA, WIDTH), F32)
    out = jnp.where(part == 0, high.astype(F32), zero)
    out = jnp.where(part == 1, mid.astype(F32), out)
    return jnp.where(part == 2, low.astype(F32), out).astype(BF16)


def shifts_kernel(ids_ref, row_ref, c0, c1, row_shift, columns, row_tail, col_tail, col_shift):
    _, row_of = places(ids_ref)
    row_lse, row_mean = row_ref[0:16, :], row_ref[16:32, :]
    col_lse, col_mean = merged((c0, c1), 8)
    picked = row_ref[32:33, 0:1]
    row_shift[...] = row_lse + 1.0
    col_shift[...] = col_lse + 1.0
    columns[...] = jnp.concatenate(
        [col_shift[pl.ds(row_of(j, t), 1), :] for j in range(2) for t in range(4)], axis=1
    )
    row_tail[...] = in_parts(
        (jnp.sum(row_lse, keepdims=True) - 2.0 * picked) * LN2,
        (jnp.sum(row_mean, keepdims=True) - 2.0 * picked) * LN2,
    )
    col_tail[...] = in_parts(
        jnp.sum(col_lse, keepdims=True) * LN2, jnp.sum(col_mean, keepdims=True) * LN2
    )


def dlogit_kernel(
    ids_ref, scale_ref, pos_ref, row_shift, col_shift, row_tail, i0, i1, i2, i3, t0, t1,
    d0, d1, d2, d3, h0, h1, acc,
):
    scale = scale_ref[0]
    scale2 = scale * LOG2E
    col_of, row_of = places(ids_ref)
    columns = col_shift[...]
    lanes = lax.broadcasted_iota(jnp.int32, (ROWS, 8 * ROWS), 1)
    for q, (rows_ref, d_ref) in enumerate(zip((i0, i1, i2, i3), (d0, d1, d2, d3))):
        for h in range(QUAD // CHUNK):
            rows = rows_ref[h * CHUNK : (h + 1) * CHUNK, :]
            logits = logits2(rows, t0, t1, scale2)
            pieces = []
            for b in range(CHUNK // ROWS):
                place = col_of(q, h * (CHUNK // ROWS) + b)
                shift = jnp.transpose(jnp.broadcast_to(row_shift[pl.ds(place, 1), :], (ROWS, ROWS)))
                pos = pos_ref[pl.ds(pl.multiple_of(place * ROWS, ROWS), ROWS), :]
                shift = jnp.concatenate([shift] * 8, axis=1)
                pos = jnp.concatenate([pos] * 8, axis=1)
                part = logits[b * ROWS : (b + 1) * ROWS]
                soft = jnp.exp2(part - shift) + jnp.exp2(part - columns)
                pieces.append(jnp.where(pos == lanes, soft - 1.0, soft).astype(BF16))
            grad = jnp.concatenate(pieces, axis=0)
            d_ref[h * CHUNK : (h + 1) * CHUNK, :] = grad
            update = lax.dot_general(
                grad, rows, (((0,), (0,)), ((), ())), preferred_element_type=F32
            )
            if q == 0 and h == 0:
                acc[...] = update
            else:
                acc[...] += update
    for j, out in enumerate((h0, h1)):
        out[0:QUAD, :] = (scale * acc[j * QUAD : (j + 1) * QUAD, :]).astype(BF16)
        out[QUAD : QUAD + EXTRA, :] = row_tail[...]


def images_kernel(scale_ref, col_tail, t0, t1, d_ref, g_ref):
    product = jnp.dot(d_ref[:, :QUAD], t0[...], preferred_element_type=F32)
    product += jnp.dot(d_ref[:, QUAD:], t1[...], preferred_element_type=F32)
    g_ref[0:QUAD, :] = (scale_ref[0] * product).astype(BF16)
    g_ref[QUAD : QUAD + EXTRA, :] = col_tail[...]


def tail_sum(refs, first):
    total = sum(r[first : first + EXTRA, :].astype(F32) for r in refs)
    total = jnp.sum(total, axis=0, keepdims=True)
    return total[:, 0:1], total[:, 1:2]


def partial_kernel(*refs):
    sources, outs = refs[:-4], refs[-4:]
    tail = in_parts(*tail_sum(sources, QUAD))
    for t, out in enumerate(outs):
        rows = slice(t * ROWS, (t + 1) * ROWS)
        out[0:ROWS, :] = sum(r[rows, :].astype(F32) for r in sources).astype(BF16)
        out[ROWS : ROWS + EXTRA, :] = tail


def finish_kernel(batch, img_ref, txt_ref, a0, a1, a2, a3, b0, b1, b2, b3, img_out, txt_out, loss_out, temp_out):
    for raw, parts, out in ((img_ref, (a0, a1, a2, a3), img_out), (txt_ref, (b0, b1, b2, b3), txt_out)):
        unit, inverse = unit_rows(raw[...])
        grad = sum(p[0:ROWS, :].astype(F32) for p in parts)
        out[...] = inverse * (grad - unit * jnp.sum(unit * grad, axis=1, keepdims=True))
    cols = tail_sum((a0, a1, a2, a3), ROWS)
    rows = tail_sum((b0, b1, b2, b3), ROWS)
    loss_out[0] = jnp.sum(cols[0] + rows[0]) / (2 * batch)
    temp_out[0] = jnp.sum(cols[1] + rows[1]) / (2 * batch)


def gathered(value, moves):
    return [value] + [shifted(value, moves(by)) for by in OFFS[1:]]


def scattered(parts, moves):
    return [parts[0]] + [shifted(p, moves(-by)) for p, by in zip(parts[1:], OFFS[1:])]


def across(place, far):
    return 3 - place if far else place ^ 1


def pair_z(far):
    return lambda z, k, x, y: (across(z, far), k, x, y)


def on_device(images, texts, partner, log_scale):
    row, col = lax.axis_index("row"), lax.axis_index("col")
    ids = jnp.stack([row, col]).astype(jnp.int32)
    scale = jnp.exp(log_scale)
    unit = shape((ROWS, WIDTH), BF16)
    anywhere = pl.BlockSpec(memory_space=pl.ANY)
    anywhere = pl.BlockSpec(memory_space=pl.ANY)
    token = shape((8, ROWS), F32)
    unit_img = call(unit_kernel, unit, images)
    unit_txt = call(unit_kernel, unit, texts, unit_img, specs=[VMEM, anywhere])
    img_own = jnp.concatenate(gathered(unit_img, ring_a), axis=0)
    txt0 = jnp.concatenate(gathered(unit_txt, ring_z), axis=0)
    imgs = gathered(img_own, ring_b)
    txt1 = shifted(txt0, other_core)
    arrived = call(after_kernel, token, *imgs[1:], specs=[VMEM] * 3)

    owner = partner // (16 * ROWS)
    steps = (row // 2 - owner // 2) % 4
    slot = steps ^ (steps // 2)
    core = jnp.where(owner % 2 == row % 2, 0, 1)
    pos = (core * 4 + slot) * ROWS + partner % ROWS
    pos = jnp.where(partner // ROWS % 16 == col, pos, -1)
    pos = jnp.broadcast_to(pos[:, None], (16 * ROWS, ROWS))

    row_shape = shape((40, ROWS), F32)
    common = (ids, scale, pos)
    in_place = [VMEM] * 6
    row_stat, col_stat = call(
        forward_kernel, [row_shape, shape((16, ROWS), F32)],
        *common, *imgs, txt0, txt1, arrived,
        specs=[SMEM, SMEM, VMEM] + in_place + [anywhere],
    )
    for row_moves, col_move in ((ring_a, pair_z(False)), (ring_b, pair_z(True))):
        row_stat, col_stat = call(
            merge_kernel, [row_shape, shape((16, ROWS), F32)],
            *gathered(row_stat, row_moves), col_stat, shifted(col_stat, col_move),
        )
    tail = shape((EXTRA, WIDTH), BF16)
    row_shift, col_shift, row_tail, col_tail = call(
        shifts_kernel, [shape((16, ROWS), F32), shape((1, 8 * ROWS), F32), tail, tail],
        ids, row_stat, col_stat, shifted(col_stat, other_core),
        specs=[SMEM] + [VMEM] * 3, scratch=[pltpu.VMEM((8, ROWS), F32)],
    )

    sent = shape((QUAD + EXTRA, WIDTH), BF16)
    *dlogits, txt_own, txt_other = call(
        dlogit_kernel, [shape((QUAD, 8 * ROWS), BF16)] * 4 + [sent] * 2,
        *common, row_shift, col_shift, row_tail, *imgs, txt0, txt1,
        specs=[SMEM, SMEM] + [VMEM] * 4 + in_place,
        scratch=[pltpu.VMEM((8 * ROWS, WIDTH), F32)],
    )
    small = [shape((ROWS + EXTRA, WIDTH), BF16)] * 4
    grads = [
        call(
            images_kernel, sent, scale, col_tail, txt0, txt1, d, specs=[SMEM] + [VMEM] * 4
        )
        for d in dlogits
    ]
    txt_parts = call(
        partial_kernel, small, txt_own, shifted(txt_other, other_core)
    )
    txt_parts = scattered(txt_parts, ring_z)
    img_parts = call(
        lambda _, *refs: partial_kernel(*refs), small, txt_parts[0], *scattered(grads, ring_b),
        specs=[anywhere] + [VMEM] * 4,
    )
    img_parts = scattered(img_parts, ring_a)
    whole = shape((ROWS, WIDTH), F32)
    one = shape((1,), F32)
    return pl.pallas_call(
        functools.partial(finish_kernel, 128 * ROWS),
        out_shape=(whole, whole, one, one),
        in_specs=[VMEM] * 10,
        out_specs=(VMEM, VMEM, SMEM, SMEM),
        compiler_params=PARAMS,
    )(images, texts, *img_parts, *txt_parts)


def solution(mesh):
    placed = (P(("row", "col"), None), P(("row", "col"), None), P("row"), P())
    return jax.shard_map(
        on_device,
        mesh=mesh,
        in_specs=placed,
        out_specs=(P(("row", "col"), None), P(("row", "col"), None), P(), P()),
        check_vma=False,
    )
```

time: 112 us -> 93.9 us (0.84)
  waiting for transfers between devices: 50.8 us -> 31.1 us
  starting transfers between devices: 38.3 us -> 39.9 us
    ppermute x30 -> x29, waiting for transfers between devices: 50.8 us -> 31.1 us  [shifted(): return lax.ppermute(value, RC, pairs)]
    ppermute x30 -> x29, starting transfers between devices: 38.3 us -> 39.9 us  [shifted(): return lax.ppermute(value, RC, pairs)]
    pallas_call x6 -> x14, Pallas kernels: 17.6 us -> 18.6 us  [call(): pl.pallas_call(kernel, out_shape=outs, in_specs=specs or [VMEM] * len(arg...]
  transfers between devices with their start and end apart: 30 -> 29, of which waited for: 17 -> 10; matrix products, arithmetic and copies ran while one was open for 0% -> 0% of each run, Pallas kernels for 0% -> 4%
where the time goes in v2:
time: 93.9 us; the launch traced here: 93.7 us
  starting transfers between devices  39.9 us (42%)
  waiting for transfers between devices  31.1 us (33%)
  Pallas kernels  19.6 us (21%)
  between operations  1.67 us (2%)
  local copies, waits for them, and re-layouts  1.27 us (1%)
    ppermute x29, starting transfers between devices, shifted(): return lax.ppermute(value, RC, pairs)  39.9 us
    ppermute x29, waiting for transfers between devices, shifted(): return lax.ppermute(value, RC, pairs)  31.1 us
    pallas_call x14, Pallas kernels, call(): pl.pallas_call(kernel, out_shape=outs, in_specs=specs or [VMEM] * len(arg...  18.6 us
  transfers between devices with their start and end apart: 29, of which 10 were waited for; matrix products, arithmetic and copies ran while one was open for 0% of the time, Pallas kernels for 4%

profile of v2, /device:TPU:0, one launch (start us, length us, event | category | flops | bytes accessed | tf_op | source)
XLA Modules:
  0.0 93.7 jit_solution(6548005381120937841)
XLA Ops:
  0.6 0.0 copy-start.1
  0.7 0.9 copy-done.1
  1.6 0.1 shard_map.75.refs_0_
  1.7 3.2 %collective-permute-start.2 = (bf16[128,512]{1,0:T(8,128)(2,1)S(1)}, bf16[128,512]{1,0:T(8,128)(2,1)S(1)}, u32[]{:S(2)}, u32[]{:S(2)}) collective-permute-start(bf16[128,512]{1,0:T(8,128)(2,1)S(1)} %shard_map.75.refs_0_), channel_id=1, source_target_pairs={{0,8},{1,9},{2,10},{3,11},{4,12},{5,13},{6,14},{7,15},{8,0},{9,1},... | collective-permute-start | bytes 393224 | tf_op jit(solution)/shard_map/ppermute | solution.py:36
  4.9 1.1 %collective-permute-start.1 = (bf16[128,512]{1,0:T(8,128)(2,1)S(1)}, bf16[128,512]{1,0:T(8,128)(2,1)S(1)}, u32[]{:S(2)}, u32[]{:S(2)}) collective-permute-start(bf16[128,512]{1,0:T(8,128)(2,1)S(1)} %shard_map.75.refs_0_), channel_id=1, source_target_pairs={{0,12},{1,13},{2,14},{3,15},{4,0},{5,1},{6,2},{7,3},{8,4},{9,5},{1... | collective-permute-start | bytes 393224 | tf_op jit(solution)/shard_map/ppermute | solution.py:36
  6.0 0.9 collective-permute-start
  6.9 0.1 shard_map.76
  7.0 4.0 %collective-permute-start.8 = (bf16[128,512]{1,0:T(8,128)(2,1)S(1)}, bf16[128,512]{1,0:T(8,128)(2,1)S(1)}, u32[]{:S(2)}, u32[]{:S(2)}) collective-permute-start(bf16[128,512]{1,0:T(8,128)(2,1)S(1)} %shard_map.76), channel_id=1, source_target_pairs={{0,64},{1,65},{2,66},{3,67},{4,68},{5,69},{6,70},{7,71},{8,72},{9,... | collective-permute-start | bytes 393224 | tf_op jit(solution)/shard_map/ppermute | solution.py:36
  11.0 0.7 collective-permute-start.7
  11.7 1.3 %collective-permute-start.6 = (bf16[128,512]{1,0:T(8,128)(2,1)S(1)}, bf16[128,512]{1,0:T(8,128)(2,1)S(1)}, u32[]{:S(2)}, u32[]{:S(2)}) collective-permute-start(bf16[128,512]{1,0:T(8,128)(2,1)S(1)} %shard_map.76), channel_id=1, source_target_pairs={{0,32},{1,33},{2,34},{3,35},{4,36},{5,37},{6,38},{7,39},{8,40},{9,... | collective-permute-start | bytes 393224 | tf_op jit(solution)/shard_map/ppermute | solution.py:36
  13.1 3.3 %collective-permute-start.5 = (bf16[512,512]{1,0:T(8,128)(2,1)S(1)}, bf16[512,512]{1,0:T(8,128)(2,1)S(1)}, u32[]{:S(2)}, u32[]{:S(2)}) collective-permute-start(bf16[512,512]{1,0:T(8,128)(2,1)S(1)} %pad_maximum_fusion.i0), channel_id=1, source_target_pairs={{0,2},{1,3},{2,0},{3,1},{4,6},{5,7},{6,4},{7,5},{8,10},{9,11},{10,... | collective-permute-start | bytes 1572872 | tf_op jit(solution)/shard_map/ppermute | solution.py:36
  16.3 1.1 %collective-permute-start.4 = (bf16[512,512]{1,0:T(8,128)(2,1)S(1)}, bf16[512,512]{1,0:T(8,128)(2,1)S(1)}, u32[]{:S(2)}, u32[]{:S(2)}) collective-permute-start(bf16[512,512]{1,0:T(8,128)(2,1)S(1)} %pad_maximum_fusion.i0), channel_id=1, source_target_pairs={{0,3},{1,0},{2,1},{3,2},{4,7},{5,4},{6,5},{7,6},{8,11},{9,8},{10,9... | collective-permute-start | bytes 1572872 | tf_op jit(solution)/shard_map/ppermute | solution.py:36
  17.4 0.0 collective-permute-done.8
  17.4 1.0 %collective-permute-start.3 = (bf16[512,512]{1,0:T(8,128)(2,1)S(1)}, bf16[512,512]{1,0:T(8,128)(2,1)S(1)}, u32[]{:S(2)}, u32[]{:S(2)}) collective-permute-start(bf16[512,512]{1,0:T(8,128)(2,1)S(1)} %pad_maximum_fusion.i0), channel_id=1, source_target_pairs={{0,1},{1,2},{2,3},{3,0},{4,5},{5,6},{6,7},{7,4},{8,9},{9,10},{10,1... | collective-permute-start | bytes 1572872 | tf_op jit(solution)/shard_map/ppermute | solution.py:36
  18.4 0.0 collective-permute-done.7
  18.4 0.0 collective-permute-done.6
  18.4 0.1 collective-permute-start.9
  18.5 0.0 copy-start.3
  19.2 0.1 pad_add_fusion.ids_ref
  19.4 4.6 %collective-permute-done.5.refs_2_.i3 = bf16[512,512]{1,0:T(8,128)(2,1)S(1)} collective-permute-done((bf16[512,512]{1,0:T(8,128)(2,1)S(1)}, bf16[512,512]{1,0:T(8,128)(2,1)S(1)}, u32[]{:S(2)}, u32[]{:S(2)}) %collective-permute-start.5) | collective-permute-done | bytes 524320 | tf_op jit(solution)/shard_map/ppermute | solution.py:36
  23.9 5.9 %collective-permute-done.4.refs_1_.i2 = bf16[512,512]{1,0:T(8,128)(2,1)S(1)} collective-permute-done((bf16[512,512]{1,0:T(8,128)(2,1)S(1)}, bf16[512,512]{1,0:T(8,128)(2,1)S(1)}, u32[]{:S(2)}, u32[]{:S(2)}) %collective-permute-start.4) | collective-permute-done | bytes 524320 | tf_op jit(solution)/shard_map/ppermute | solution.py:36
  29.8 0.0 collective-permute-done.3.refs_0_.i1
  29.8 0.0 collective-permute-done.9.t1
  29.8 0.3 broadcast_in_dim.8.pos_ref
  30.2 6.9 %shard_map.78 = (f32[40,128]{1,0:T(8,128)S(1)}, f32[16,128]{1,0:T(8,128)S(1)}) custom-call(s32[2]{0:T(128)S(1)} %pad_add_fusion.ids_ref, f32[1]{0:T(128)S(6)} %exp.3.scale_ref, s32[2048,128]{1,0:T(8,128)S(1)} %broadcast_in_dim.8.pos_ref, bf16[512,512]{1,0:T(8,128)(2,1)S(1)} %pad_maximum_fusion.i0, bf16[512,512]{1,0:T(8,128)(2,1)S(1)} %collective-permute-done.3.refs_0_.i1, ...), custom_call_target="tpu_custom_call" | custom-call | tf_op jit(solution)/shard_map/pallas_call | solution.py:56
  37.0 0.7 collective-permute-start.12
  37.7 2.6 %collective-permute-start.11 = (f32[40,128]{1,0:T(8,128)S(1)}, f32[40,128]{1,0:T(8,128)S(1)}, u32[]{:S(2)}, u32[]{:S(2)}) collective-permute-start(f32[40,128]{1,0:T(8,128)S(1)} %get-tuple-element.28.r0), channel_id=1, source_target_pairs={{0,12},{1,13},{2,14},{3,15},{4,0},{5,1},{6,2},{7,3},{8,4},{9,5},{1... | collective-permute-start | bytes 61448 | tf_op jit(solution)/shard_map/ppermute | solution.py:36
  40.4 0.0 collective-permute-start.10
  40.4 1.0 %collective-permute-start.13 = (f32[16,128]{1,0:T(8,128)S(1)}, f32[16,128]{1,0:T(8,128)S(1)}, u32[]{:S(2)}, u32[]{:S(2)}) collective-permute-start(f32[16,128]{1,0:T(8,128)S(1)} %get-tuple-element.29.c0), channel_id=1, source_target_pairs={{0,32},{1,33},{2,34},{3,35},{4,36},{5,37},{6,38},{7,39},{8,40},{9,... | collective-permute-start | bytes 24584 | tf_op jit(solution)/shard_map/ppermute | solution.py:36
  41.4 2.6 %collective-permute-done.13.c1 = f32[16,128]{1,0:T(8,128)S(1)} collective-permute-done((f32[16,128]{1,0:T(8,128)S(1)}, f32[16,128]{1,0:T(8,128)S(1)}, u32[]{:S(2)}, u32[]{:S(2)}) %collective-permute-start.13) | collective-permute-done | bytes 8224 | tf_op jit(solution)/shard_map/ppermute | solution.py:36
  44.0 0.0 collective-permute-done.12.r3
  44.0 0.0 collective-permute-done.11.r2
  44.0 1.6 %collective-permute-done.10.r1 = f32[40,128]{1,0:T(8,128)S(1)} collective-permute-done((f32[40,128]{1,0:T(8,128)S(1)}, f32[40,128]{1,0:T(8,128)S(1)}, u32[]{:S(2)}, u32[]{:S(2)}) %collective-permute-start.10) | collective-permute-done | bytes 20512 | tf_op jit(solution)/shard_map/ppermute | solution.py:36
  45.6 2.7 %collective-permute-start.16 = (f32[40,128]{1,0:T(8,128)S(1)}, f32[40,128]{1,0:T(8,128)S(1)}, u32[]{:S(2)}, u32[]{:S(2)}) collective-permute-start(f32[40,128]{1,0:T(8,128)S(1)} %get-tuple-element.30.r0), channel_id=1, source_target_pairs={{0,2},{1,3},{2,0},{3,1},{4,6},{5,7},{6,4},{7,5},{8,10},{9,11},{10,... | collective-permute-start | bytes 61448 | tf_op jit(solution)/shard_map/ppermute | solution.py:36
  48.3 1.2 %collective-permute-start.15 = (f32[40,128]{1,0:T(8,128)S(1)}, f32[40,128]{1,0:T(8,128)S(1)}, u32[]{:S(2)}, u32[]{:S(2)}) collective-permute-start(f32[40,128]{1,0:T(8,128)S(1)} %get-tuple-element.30.r0), channel_id=1, source_target_pairs={{0,3},{1,0},{2,1},{3,2},{4,7},{5,4},{6,5},{7,6},{8,11},{9,8},{10,9... | collective-permute-start | bytes 61448 | tf_op jit(solution)/shard_map/ppermute | solution.py:36
  49.5 0.8 collective-permute-start.14
  50.3 2.3 %collective-permute-start.17 = (f32[16,128]{1,0:T(8,128)S(1)}, f32[16,128]{1,0:T(8,128)S(1)}, u32[]{:S(2)}, u32[]{:S(2)}) collective-permute-start(f32[16,128]{1,0:T(8,128)S(1)} %get-tuple-element.31.c0), channel_id=1, source_target_pairs={{0,96},{1,97},{2,98},{3,99},{4,100},{5,101},{6,102},{7,103},{8,104... | collective-permute-start | bytes 24584 | tf_op jit(solution)/shard_map/ppermute | solution.py:36
  52.6 2.6 %collective-permute-done.17.c1 = f32[16,128]{1,0:T(8,128)S(1)} collective-permute-done((f32[16,128]{1,0:T(8,128)S(1)}, f32[16,128]{1,0:T(8,128)S(1)}, u32[]{:S(2)}, u32[]{:S(2)}) %collective-permute-start.17) | collective-permute-done | bytes 8224 | tf_op jit(solution)/shard_map/ppermute | solution.py:36
  55.2 0.0 collective-permute-done.16.r3
  55.2 0.1 collective-permute-start.18
  55.3 1.2 %collective-permute-done.18.c1 = f32[16,128]{1,0:T(8,128)S(1)} collective-permute-done((f32[16,128]{1,0:T(8,128)S(1)}, f32[16,128]{1,0:T(8,128)S(1)}, u32[]{:S(2)}, u32[]{:S(2)}) %collective-permute-start.18) | collective-permute-done | bytes 8224 | tf_op jit(solution)/shard_map/ppermute | solution.py:36
  56.5 0.7 shard_map.81
  57.2 7.3 %shard_map.82 = (bf16[512,1024]{1,0:T(8,128)(2,1)S(1)}, bf16[512,1024]{1,0:T(8,128)(2,1)S(1)}, bf16[512,1024]{1,0:T(8,128)(2,1)S(1)}, bf16[512,1024]{1,0:T(8,128...) custom-call(s32[2]{0:T(128)S(1)} %pad_add_fusion.ids_ref, f32[1]{0:T(128)S(6)} %exp.3.scale_ref, ...), custom_call_target="tpu_custom_call" | custom-call | tf_op jit(solution)/shard_map/pallas_call | solution.py:56
  64.5 0.2 collective-permute-start.19
  64.8 0.7 shard_map.87
  65.5 1.0 %collective-permute-start.22 = (bf16[528,512]{1,0:T(8,128)(2,1)S(1)}, bf16[528,512]{1,0:T(8,128)(2,1)S(1)}, u32[]{:S(2)}, u32[]{:S(2)}) collective-permute-start(bf16[528,512]{1,0:T(8,128)(2,1)S(1)} %shard_map.87), channel_id=1, source_target_pairs={{0,2},{1,3},{2,0},{3,1},{4,6},{5,7},{6,4},{7,5},{8,10},{9,11},{10,... | collective-permute-start | bytes 1622024 | tf_op jit(solution)/shard_map/ppermute | solution.py:36
  66.5 0.7 shard_map.86
  67.2 2.4 %collective-permute-start.21 = (bf16[528,512]{1,0:T(8,128)(2,1)S(1)}, bf16[528,512]{1,0:T(8,128)(2,1)S(1)}, u32[]{:S(2)}, u32[]{:S(2)}) collective-permute-start(bf16[528,512]{1,0:T(8,128)(2,1)S(1)} %shard_map.86), channel_id=1, source_target_pairs={{0,1},{1,2},{2,3},{3,0},{4,5},{5,6},{6,7},{7,4},{8,9},{9,10},{10,1... | collective-permute-start | bytes 1622024 | tf_op jit(solution)/shard_map/ppermute | solution.py:36
  69.6 0.7 shard_map.85
  70.4 1.0 %collective-permute-start.20 = (bf16[528,512]{1,0:T(8,128)(2,1)S(1)}, bf16[528,512]{1,0:T(8,128)(2,1)S(1)}, u32[]{:S(2)}, u32[]{:S(2)}) collective-permute-start(bf16[528,512]{1,0:T(8,128)(2,1)S(1)} %shard_map.85), channel_id=1, source_target_pairs={{0,3},{1,0},{2,1},{3,2},{4,7},{5,4},{6,5},{7,6},{8,11},{9,8},{10,9... | collective-permute-start | bytes 1622024 | tf_op jit(solution)/shard_map/ppermute | solution.py:36
  71.3 0.2 shard_map.83
  71.5 2.2 %collective-permute-start.26 = (bf16[144,512]{1,0:T(8,128)(2,1)S(1)}, bf16[144,512]{1,0:T(8,128)(2,1)S(1)}, u32[]{:S(2)}, u32[]{:S(2)}) collective-permute-start(bf16[144,512]{1,0:T(8,128)(2,1)S(1)} %get-tuple-element.49), channel_id=1, source_target_pairs={{0,96},{1,97},{2,98},{3,99},{4,100},{5,101},{6,102},{7,103},{8,104... | collective-permute-start | bytes 442376 | tf_op jit(solution)/shard_map/ppermute | solution.py:36
  73.7 0.7 shard_map.84.refs_0_
  74.4 0.1 collective-permute-start.27
  74.5 2.1 %collective-permute-done.22.refs_3_ = bf16[528,512]{1,0:T(8,128)(2,1)S(1)} collective-permute-done((bf16[528,512]{1,0:T(8,128)(2,1)S(1)}, bf16[528,512]{1,0:T(8,128)(2,1)S(1)}, u32[]{:S(2)}, u32[]{:S(2)}) %collective-permute-start.22) | collective-permute-done | bytes 540704 | tf_op jit(solution)/shard_map/ppermute | solution.py:36
  76.5 1.5 %collective-permute-start.28 = (bf16[144,512]{1,0:T(8,128)(2,1)S(1)}, bf16[144,512]{1,0:T(8,128)(2,1)S(1)}, u32[]{:S(2)}, u32[]{:S(2)}) collective-permute-start(bf16[144,512]{1,0:T(8,128)(2,1)S(1)} %get-tuple-element.51), channel_id=1, source_target_pairs={{0,64},{1,65},{2,66},{3,67},{4,68},{5,69},{6,70},{7,71},{8,72},{9,... | collective-permute-start | bytes 442376 | tf_op jit(solution)/shard_map/ppermute | solution.py:36
  78.0 4.2 %collective-permute-done.21.refs_2_ = bf16[528,512]{1,0:T(8,128)(2,1)S(1)} collective-permute-done((bf16[528,512]{1,0:T(8,128)(2,1)S(1)}, bf16[528,512]{1,0:T(8,128)(2,1)S(1)}, u32[]{:S(2)}, u32[]{:S(2)}) %collective-permute-start.21) | collective-permute-done | bytes 540704 | tf_op jit(solution)/shard_map/ppermute | solution.py:36
  82.2 0.4 shard_map.88
  82.6 2.0 %collective-permute-start.23 = (bf16[144,512]{1,0:T(8,128)(2,1)S(1)}, bf16[144,512]{1,0:T(8,128)(2,1)S(1)}, u32[]{:S(2)}, u32[]{:S(2)}) collective-permute-start(bf16[144,512]{1,0:T(8,128)(2,1)S(1)} %get-tuple-element.46), channel_id=1, source_target_pairs={{0,12},{1,13},{2,14},{3,15},{4,0},{5,1},{6,2},{7,3},{8,4},{9,5},{1... | collective-permute-start | bytes 442376 | tf_op jit(solution)/shard_map/ppermute | solution.py:36
  84.6 0.1 collective-permute-start.24
  84.7 1.4 %collective-permute-start.25 = (bf16[144,512]{1,0:T(8,128)(2,1)S(1)}, bf16[144,512]{1,0:T(8,128)(2,1)S(1)}, u32[]{:S(2)}, u32[]{:S(2)}) collective-permute-start(bf16[144,512]{1,0:T(8,128)(2,1)S(1)} %get-tuple-element.48), channel_id=1, source_target_pairs={{0,8},{1,9},{2,10},{3,11},{4,12},{5,13},{6,14},{7,15},{8,0},{9,1},... | collective-permute-start | bytes 442376 | tf_op jit(solution)/shard_map/ppermute | solution.py:36
  86.1 1.7 %collective-permute-done.23.a1 = bf16[144,512]{1,0:T(8,128)(2,1)S(1)} collective-permute-done((bf16[144,512]{1,0:T(8,128)(2,1)S(1)}, bf16[144,512]{1,0:T(8,128)(2,1)S(1)}, u32[]{:S(2)}, u32[]{:S(2)}) %collective-permute-start.23) | collective-permute-done | bytes 147488 | tf_op jit(solution)/shard_map/ppermute | solution.py:36
  87.8 4.7 %collective-permute-done.24.a2 = bf16[144,512]{1,0:T(8,128)(2,1)S(1)} collective-permute-done((bf16[144,512]{1,0:T(8,128)(2,1)S(1)}, bf16[144,512]{1,0:T(8,128)(2,1)S(1)}, u32[]{:S(2)}, u32[]{:S(2)}) %collective-permute-start.24) | collective-permute-done | bytes 147488 | tf_op jit(solution)/shard_map/ppermute | solution.py:36
  92.5 1.1 %shard_map.89 = (f32[128,512]{1,0:T(8,128)}, f32[128,512]{1,0:T(8,128)}, f32[1]{0:T(128)}, f32[1]{0:T(128)}) custom-call(bf16[128,512]{1,0:T(8,128)(2,1)S(1)} %copy-done.2, bf16[128,512]{1,0:T(8,128)(2,1)S(1)} %copy-done, bf16[144,512]{1,0:T(8,128)(2,1)S(1)} %get-tuple-element.45.a0, bf16[144,512]{1,0:T(8,128)(2,1)S(1)} %collective-permute-done.23.a1, ...), custom_call_target="tpu_custom_call" | custom-call | tf_op jit(solution)/shard_map/pallas_call | solution.py:363
  (22 shorter events, 0.2 us)
Async XLA Ops:
  0.6 6.3 %copy-start = (bf16[128,512]{1,0:T(8,128)(2,1)S(1)}, bf16[128,512]{1,0:T(8,128)(2,1)}, u32[]{:S(2)}) copy-start(bf16[128,512]{1,0:T(8,128)(2,1)} %txt_ref.1) | copy-start | bytes 393220
  0.6 0.9 %copy-start.1 = (bf16[128,512]{1,0:T(8,128)(2,1)S(1)}, bf16[128,512]{1,0:T(8,128)(2,1)}, u32[]{:S(2)}) copy-start(bf16[128,512]{1,0:T(8,128)(2,1)} %img_ref.1) | copy-start | bytes 393220
  1.7 10.0 %collective-permute-start.2 = (bf16[128,512]{1,0:T(8,128)(2,1)S(1)}, bf16[128,512]{1,0:T(8,128)(2,1)S(1)}, u32[]{:S(2)}, u32[]{:S(2)}) collective-permute-start(bf16[128,512]{1,0:T(8,128)(2,1)S(1)} %shard_map.75.refs_0_), channel_id=1, source_target_pairs={{0,8},{1,9},{2,10},{3,11},{4,12},{5,13},{6,14},{7,15},{8,0},{9,1},... | collective-permute-start | bytes 393224 | tf_op jit(solution)/shard_map/ppermute | solution.py:36
  4.9 8.1 %collective-permute-start.1 = (bf16[128,512]{1,0:T(8,128)(2,1)S(1)}, bf16[128,512]{1,0:T(8,128)(2,1)S(1)}, u32[]{:S(2)}, u32[]{:S(2)}) collective-permute-start(bf16[128,512]{1,0:T(8,128)(2,1)S(1)} %shard_map.75.refs_0_), channel_id=1, source_target_pairs={{0,12},{1,13},{2,14},{3,15},{4,0},{5,1},{6,2},{7,3},{8,4},{9,5},{1... | collective-permute-start | bytes 393224 | tf_op jit(solution)/shard_map/ppermute | solution.py:36
  6.0 7.0 %collective-permute-start = (bf16[128,512]{1,0:T(8,128)(2,1)S(1)}, bf16[128,512]{1,0:T(8,128)(2,1)S(1)}, u32[]{:S(2)}, u32[]{:S(2)}) collective-permute-start(bf16[128,512]{1,0:T(8,128)(2,1)S(1)} %shard_map.75.refs_0_), channel_id=1, source_target_pairs={{0,4},{1,5},{2,6},{3,7},{4,8},{5,9},{6,10},{7,11},{8,12},{9,13},{1... | collective-permute-start | bytes 393224 | tf_op jit(solution)/shard_map/ppermute | solution.py:36
  7.0 10.4 %collective-permute-start.8 = (bf16[128,512]{1,0:T(8,128)(2,1)S(1)}, bf16[128,512]{1,0:T(8,128)(2,1)S(1)}, u32[]{:S(2)}, u32[]{:S(2)}) collective-permute-start(bf16[128,512]{1,0:T(8,128)(2,1)S(1)} %shard_map.76), channel_id=1, source_target_pairs={{0,64},{1,65},{2,66},{3,67},{4,68},{5,69},{6,70},{7,71},{8,72},{9,... | collective-permute-start | bytes 393224 | tf_op jit(solution)/shard_map/ppermute | solution.py:36
  11.0 7.4 %collective-permute-start.7 = (bf16[128,512]{1,0:T(8,128)(2,1)S(1)}, bf16[128,512]{1,0:T(8,128)(2,1)S(1)}, u32[]{:S(2)}, u32[]{:S(2)}) collective-permute-start(bf16[128,512]{1,0:T(8,128)(2,1)S(1)} %shard_map.76), channel_id=1, source_target_pairs={{0,96},{1,97},{2,98},{3,99},{4,100},{5,101},{6,102},{7,103},{8,104... | collective-permute-start | bytes 393224 | tf_op jit(solution)/shard_map/ppermute | solution.py:36
  11.7 6.7 %collective-permute-start.6 = (bf16[128,512]{1,0:T(8,128)(2,1)S(1)}, bf16[128,512]{1,0:T(8,128)(2,1)S(1)}, u32[]{:S(2)}, u32[]{:S(2)}) collective-permute-start(bf16[128,512]{1,0:T(8,128)(2,1)S(1)} %shard_map.76), channel_id=1, source_target_pairs={{0,32},{1,33},{2,34},{3,35},{4,36},{5,37},{6,38},{7,39},{8,40},{9,... | collective-permute-start | bytes 393224 | tf_op jit(solution)/shard_map/ppermute | solution.py:36
  13.1 10.9 %collective-permute-start.5 = (bf16[512,512]{1,0:T(8,128)(2,1)S(1)}, bf16[512,512]{1,0:T(8,128)(2,1)S(1)}, u32[]{:S(2)}, u32[]{:S(2)}) collective-permute-start(bf16[512,512]{1,0:T(8,128)(2,1)S(1)} %pad_maximum_fusion.i0), channel_id=1, source_target_pairs={{0,2},{1,3},{2,0},{3,1},{4,6},{5,7},{6,4},{7,5},{8,10},{9,11},{10,... | collective-permute-start | bytes 1572872 | tf_op jit(solution)/shard_map/ppermute | solution.py:36
  16.3 13.5 %collective-permute-start.4 = (bf16[512,512]{1,0:T(8,128)(2,1)S(1)}, bf16[512,512]{1,0:T(8,128)(2,1)S(1)}, u32[]{:S(2)}, u32[]{:S(2)}) collective-permute-start(bf16[512,512]{1,0:T(8,128)(2,1)S(1)} %pad_maximum_fusion.i0), channel_id=1, source_target_pairs={{0,3},{1,0},{2,1},{3,2},{4,7},{5,4},{6,5},{7,6},{8,11},{9,8},{10,9... | collective-permute-start | bytes 1572872 | tf_op jit(solution)/shard_map/ppermute | solution.py:36
  17.4 12.4 %collective-permute-start.3 = (bf16[512,512]{1,0:T(8,128)(2,1)S(1)}, bf16[512,512]{1,0:T(8,128)(2,1)S(1)}, u32[]{:S(2)}, u32[]{:S(2)}) collective-permute-start(bf16[512,512]{1,0:T(8,128)(2,1)S(1)} %pad_maximum_fusion.i0), channel_id=1, source_target_pairs={{0,1},{1,2},{2,3},{3,0},{4,5},{5,6},{6,7},{7,4},{8,9},{9,10},{10,1... | collective-permute-start | bytes 1572872 | tf_op jit(solution)/shard_map/ppermute | solution.py:36
  18.4 11.4 %collective-permute-start.9 = (bf16[512,512]{1,0:T(8,128)(2,1)S(1)}, bf16[512,512]{1,0:T(8,128)(2,1)S(1)}, u32[]{:S(2)}, u32[]{:S(2)}) collective-permute-start(bf16[512,512]{1,0:T(8,128)(2,1)S(1)} %pad_maximum_fusion.1.t0), channel_id=1, source_target_pairs={{0,16},{1,17},{2,18},{3,19},{4,20},{5,21},{6,22},{7,23},{8,24},{9,... | collective-permute-start | bytes 1572872 | tf_op jit(solution)/shard_map/ppermute | solution.py:36
  18.5 0.8 copy-start.3
  37.0 7.0 %collective-permute-start.12 = (f32[40,128]{1,0:T(8,128)S(1)}, f32[40,128]{1,0:T(8,128)S(1)}, u32[]{:S(2)}, u32[]{:S(2)}) collective-permute-start(f32[40,128]{1,0:T(8,128)S(1)} %get-tuple-element.28.r0), channel_id=1, source_target_pairs={{0,8},{1,9},{2,10},{3,11},{4,12},{5,13},{6,14},{7,15},{8,0},{9,1},... | collective-permute-start | bytes 61448 | tf_op jit(solution)/shard_map/ppermute | solution.py:36
  37.7 6.3 %collective-permute-start.11 = (f32[40,128]{1,0:T(8,128)S(1)}, f32[40,128]{1,0:T(8,128)S(1)}, u32[]{:S(2)}, u32[]{:S(2)}) collective-permute-start(f32[40,128]{1,0:T(8,128)S(1)} %get-tuple-element.28.r0), channel_id=1, source_target_pairs={{0,12},{1,13},{2,14},{3,15},{4,0},{5,1},{6,2},{7,3},{8,4},{9,5},{1... | collective-permute-start | bytes 61448 | tf_op jit(solution)/shard_map/ppermute | solution.py:36
  40.4 5.2 %collective-permute-start.10 = (f32[40,128]{1,0:T(8,128)S(1)}, f32[40,128]{1,0:T(8,128)S(1)}, u32[]{:S(2)}, u32[]{:S(2)}) collective-permute-start(f32[40,128]{1,0:T(8,128)S(1)} %get-tuple-element.28.r0), channel_id=1, source_target_pairs={{0,4},{1,5},{2,6},{3,7},{4,8},{5,9},{6,10},{7,11},{8,12},{9,13},{1... | collective-permute-start | bytes 61448 | tf_op jit(solution)/shard_map/ppermute | solution.py:36
  40.4 3.7 %collective-permute-start.13 = (f32[16,128]{1,0:T(8,128)S(1)}, f32[16,128]{1,0:T(8,128)S(1)}, u32[]{:S(2)}, u32[]{:S(2)}) collective-permute-start(f32[16,128]{1,0:T(8,128)S(1)} %get-tuple-element.29.c0), channel_id=1, source_target_pairs={{0,32},{1,33},{2,34},{3,35},{4,36},{5,37},{6,38},{7,39},{8,40},{9,... | collective-permute-start | bytes 24584 | tf_op jit(solution)/shard_map/ppermute | solution.py:36
  45.6 9.6 %collective-permute-start.16 = (f32[40,128]{1,0:T(8,128)S(1)}, f32[40,128]{1,0:T(8,128)S(1)}, u32[]{:S(2)}, u32[]{:S(2)}) collective-permute-start(f32[40,128]{1,0:T(8,128)S(1)} %get-tuple-element.30.r0), channel_id=1, source_target_pairs={{0,2},{1,3},{2,0},{3,1},{4,6},{5,7},{6,4},{7,5},{8,10},{9,11},{10,... | collective-permute-start | bytes 61448 | tf_op jit(solution)/shard_map/ppermute | solution.py:36
  48.3 6.9 %collective-permute-start.15 = (f32[40,128]{1,0:T(8,128)S(1)}, f32[40,128]{1,0:T(8,128)S(1)}, u32[]{:S(2)}, u32[]{:S(2)}) collective-permute-start(f32[40,128]{1,0:T(8,128)S(1)} %get-tuple-element.30.r0), channel_id=1, source_target_pairs={{0,3},{1,0},{2,1},{3,2},{4,7},{5,4},{6,5},{7,6},{8,11},{9,8},{10,9... | collective-permute-start | bytes 61448 | tf_op jit(solution)/shard_map/ppermute | solution.py:36
  49.5 5.7 %collective-permute-start.14 = (f32[40,128]{1,0:T(8,128)S(1)}, f32[40,128]{1,0:T(8,128)S(1)}, u32[]{:S(2)}, u32[]{:S(2)}) collective-permute-start(f32[40,128]{1,0:T(8,128)S(1)} %get-tuple-element.30.r0), channel_id=1, source_target_pairs={{0,1},{1,2},{2,3},{3,0},{4,5},{5,6},{6,7},{7,4},{8,9},{9,10},{10,1... | collective-permute-start | bytes 61448 | tf_op jit(solution)/shard_map/ppermute | solution.py:36
  50.3 4.9 %collective-permute-start.17 = (f32[16,128]{1,0:T(8,128)S(1)}, f32[16,128]{1,0:T(8,128)S(1)}, u32[]{:S(2)}, u32[]{:S(2)}) collective-permute-start(f32[16,128]{1,0:T(8,128)S(1)} %get-tuple-element.31.c0), channel_id=1, source_target_pairs={{0,96},{1,97},{2,98},{3,99},{4,100},{5,101},{6,102},{7,103},{8,104... | collective-permute-start | bytes 24584 | tf_op jit(solution)/shard_map/ppermute | solution.py:36
  55.2 1.3 %collective-permute-start.18 = (f32[16,128]{1,0:T(8,128)S(1)}, f32[16,128]{1,0:T(8,128)S(1)}, u32[]{:S(2)}, u32[]{:S(2)}) collective-permute-start(f32[16,128]{1,0:T(8,128)S(1)} %get-tuple-element.33.c0), channel_id=1, source_target_pairs={{0,16},{1,17},{2,18},{3,19},{4,20},{5,21},{6,22},{7,23},{8,24},{9,... | collective-permute-start | bytes 24584 | tf_op jit(solution)/shard_map/ppermute | solution.py:36
  64.5 6.8 %collective-permute-start.19 = (bf16[528,512]{1,0:T(8,128)(2,1)S(1)}, bf16[528,512]{1,0:T(8,128)(2,1)S(1)}, u32[]{:S(2)}, u32[]{:S(2)}) collective-permute-start(bf16[528,512]{1,0:T(8,128)(2,1)S(1)} %get-tuple-element.38), channel_id=1, source_target_pairs={{0,16},{1,17},{2,18},{3,19},{4,20},{5,21},{6,22},{7,23},{8,24},{9,... | collective-permute-start | bytes 1622024 | tf_op jit(solution)/shard_map/ppermute | solution.py:36
  65.5 11.0 %collective-permute-start.22 = (bf16[528,512]{1,0:T(8,128)(2,1)S(1)}, bf16[528,512]{1,0:T(8,128)(2,1)S(1)}, u32[]{:S(2)}, u32[]{:S(2)}) collective-permute-start(bf16[528,512]{1,0:T(8,128)(2,1)S(1)} %shard_map.87), channel_id=1, source_target_pairs={{0,2},{1,3},{2,0},{3,1},{4,6},{5,7},{6,4},{7,5},{8,10},{9,11},{10,... | collective-permute-start | bytes 1622024 | tf_op jit(solution)/shard_map/ppermute | solution.py:36
  67.2 15.0 %collective-permute-start.21 = (bf16[528,512]{1,0:T(8,128)(2,1)S(1)}, bf16[528,512]{1,0:T(8,128)(2,1)S(1)}, u32[]{:S(2)}, u32[]{:S(2)}) collective-permute-start(bf16[528,512]{1,0:T(8,128)(2,1)S(1)} %shard_map.86), channel_id=1, source_target_pairs={{0,1},{1,2},{2,3},{3,0},{4,5},{5,6},{6,7},{7,4},{8,9},{9,10},{10,1... | collective-permute-start | bytes 1622024 | tf_op jit(solution)/shard_map/ppermute | solution.py:36
  70.4 11.9 %collective-permute-start.20 = (bf16[528,512]{1,0:T(8,128)(2,1)S(1)}, bf16[528,512]{1,0:T(8,128)(2,1)S(1)}, u32[]{:S(2)}, u32[]{:S(2)}) collective-permute-start(bf16[528,512]{1,0:T(8,128)(2,1)S(1)} %shard_map.85), channel_id=1, source_target_pairs={{0,3},{1,0},{2,1},{3,2},{4,7},{5,4},{6,5},{7,6},{8,11},{9,8},{10,9... | collective-permute-start | bytes 1622024 | tf_op jit(solution)/shard_map/ppermute | solution.py:36
  71.5 13.2 %collective-permute-start.26 = (bf16[144,512]{1,0:T(8,128)(2,1)S(1)}, bf16[144,512]{1,0:T(8,128)(2,1)S(1)}, u32[]{:S(2)}, u32[]{:S(2)}) collective-permute-start(bf16[144,512]{1,0:T(8,128)(2,1)S(1)} %get-tuple-element.49), channel_id=1, source_target_pairs={{0,96},{1,97},{2,98},{3,99},{4,100},{5,101},{6,102},{7,103},{8,104... | collective-permute-start | bytes 442376 | tf_op jit(solution)/shard_map/ppermute | solution.py:36
  74.4 11.7 %collective-permute-start.27 = (bf16[144,512]{1,0:T(8,128)(2,1)S(1)}, bf16[144,512]{1,0:T(8,128)(2,1)S(1)}, u32[]{:S(2)}, u32[]{:S(2)}) collective-permute-start(bf16[144,512]{1,0:T(8,128)(2,1)S(1)} %get-tuple-element.50), channel_id=1, source_target_pairs={{0,32},{1,33},{2,34},{3,35},{4,36},{5,37},{6,38},{7,39},{8,40},{9,... | collective-permute-start | bytes 442376 | tf_op jit(solution)/shard_map/ppermute | solution.py:36
  76.5 9.6 %collective-permute-start.28 = (bf16[144,512]{1,0:T(8,128)(2,1)S(1)}, bf16[144,512]{1,0:T(8,128)(2,1)S(1)}, u32[]{:S(2)}, u32[]{:S(2)}) collective-permute-start(bf16[144,512]{1,0:T(8,128)(2,1)S(1)} %get-tuple-element.51), channel_id=1, source_target_pairs={{0,64},{1,65},{2,66},{3,67},{4,68},{5,69},{6,70},{7,71},{8,72},{9,... | collective-permute-start | bytes 442376 | tf_op jit(solution)/shard_map/ppermute | solution.py:36
  82.2 10.3 %copy-start.2 = (bf16[128,512]{1,0:T(8,128)(2,1)S(1)}, bf16[128,512]{1,0:T(8,128)(2,1)}, u32[]{:S(2)}) copy-start(bf16[128,512]{1,0:T(8,128)(2,1)} %img_ref.1) | copy-start | bytes 393220
  82.6 5.2 %collective-permute-start.23 = (bf16[144,512]{1,0:T(8,128)(2,1)S(1)}, bf16[144,512]{1,0:T(8,128)(2,1)S(1)}, u32[]{:S(2)}, u32[]{:S(2)}) collective-permute-start(bf16[144,512]{1,0:T(8,128)(2,1)S(1)} %get-tuple-element.46), channel_id=1, source_target_pairs={{0,12},{1,13},{2,14},{3,15},{4,0},{5,1},{6,2},{7,3},{8,4},{9,5},{1... | collective-permute-start | bytes 442376 | tf_op jit(solution)/shard_map/ppermute | solution.py:36
  84.6 7.9 %collective-permute-start.24 = (bf16[144,512]{1,0:T(8,128)(2,1)S(1)}, bf16[144,512]{1,0:T(8,128)(2,1)S(1)}, u32[]{:S(2)}, u32[]{:S(2)}) collective-permute-start(bf16[144,512]{1,0:T(8,128)(2,1)S(1)} %get-tuple-element.47), channel_id=1, source_target_pairs={{0,4},{1,5},{2,6},{3,7},{4,8},{5,9},{6,10},{7,11},{8,12},{9,13},{1... | collective-permute-start | bytes 442376 | tf_op jit(solution)/shard_map/ppermute | solution.py:36
  84.7 7.8 %collective-permute-start.25 = (bf16[144,512]{1,0:T(8,128)(2,1)S(1)}, bf16[144,512]{1,0:T(8,128)(2,1)S(1)}, u32[]{:S(2)}, u32[]{:S(2)}) collective-permute-start(bf16[144,512]{1,0:T(8,128)(2,1)S(1)} %get-tuple-element.48), channel_id=1, source_target_pairs={{0,8},{1,9},{2,10},{3,11},{4,12},{5,13},{6,14},{7,15},{8,0},{9,1},... | collective-permute-start | bytes 442376 | tf_op jit(solution)/shard_map/ppermute | solution.py:36

commit v3 on v2

--- a/solution.py
+++ b/solution.py
@@ -19,6 +19,7 @@
 BF16 = jnp.bfloat16
 VMEM = pl.BlockSpec(memory_space=pltpu.VMEM)
 SMEM = pl.BlockSpec(memory_space=pltpu.SMEM)
+BUSY = pl.CostEstimate(flops=10**10, bytes_accessed=10**6, transcendentals=0)
 PARAMS = pltpu.CompilerParams(vmem_limit_bytes=24 * 1024 * 1024)
 
 
@@ -114,15 +115,19 @@
 CHUNK = 256
 
 
-def forward_kernel(
-    ids_ref, scale_ref, pos_ref, i0, i1, i2, i3, t0, t1, _, row_out, col_out
-):
+def forward_kernel(last, places_of, ids_ref, scale_ref, pos_ref, i0, i1, t0, t1, *refs):
     scale2 = scale_ref[0] * LOG2E
     col_of, row_of = places(ids_ref)
     lanes = lax.broadcasted_iota(jnp.int32, (CHUNK, 8 * ROWS), 1)
-    col_high = jnp.full((1, 8 * ROWS), -jnp.inf, F32)
-    col_total = col_weighted = picked = jnp.zeros((1, 8 * ROWS), F32)
-    for q, rows_ref in enumerate((i0, i1, i2, i3)):
+    if last:
+        row_in, state_in, row_out, col_out = refs
+        row_out[...] = row_in[...]
+        col_high, col_total, col_weighted, picked = (state_in[i : i + 1, :] for i in range(4))
+    else:
+        _, row_out, state_out = refs
+        col_high = jnp.full((1, 8 * ROWS), -jnp.inf, F32)
+        col_total = col_weighted = picked = jnp.zeros((1, 8 * ROWS), F32)
+    for q, rows_ref in zip(places_of, (i0, i1)):
         for h in range(QUAD // CHUNK):
             logits = logits2(rows_ref[h * CHUNK : (h + 1) * CHUNK, :], t0, t1, scale2)
             high = jnp.max(logits, axis=1, keepdims=True)
@@ -145,6 +150,10 @@
             weights = jnp.exp2(logits - col_high)
             col_total = col_total * rescale + jnp.sum(weights, axis=0, keepdims=True)
             col_weighted = col_weighted * rescale + jnp.sum(weights * logits, axis=0, keepdims=True)
+    if not last:
+        for i, value in enumerate((col_high, col_total, col_weighted, picked)):
+            state_out[i : i + 1, :] = value
+        return
     row_out[32:40, :] = jnp.broadcast_to(jnp.sum(picked, axis=1, keepdims=True), (8, ROWS))
     col_lse = col_high + jnp.log2(col_total)
     col_mean = col_weighted / col_total
@@ -205,12 +214,17 @@
     )
 
 
+def images_grad(scale_ref, col_tail, t0, t1, d_ref, g_ref):
+    product = jnp.dot(d_ref[:, :QUAD], t0[...], preferred_element_type=F32)
+    product += jnp.dot(d_ref[:, QUAD:], t1[...], preferred_element_type=F32)
+    g_ref[0:QUAD, :] = (scale_ref[0] * product).astype(BF16)
+    g_ref[QUAD : QUAD + EXTRA, :] = col_tail[...]
+
+
 def dlogit_kernel(
-    ids_ref, scale_ref, pos_ref, row_shift, col_shift, row_tail, i0, i1, i2, i3, t0, t1,
-    d0, d1, d2, d3, h0, h1, acc,
+    ids_ref, scale_ref, pos_ref, row_shift, col_shift, i0, i1, i2, i3, t0, t1, d0, d1, d2, d3
 ):
-    scale = scale_ref[0]
-    scale2 = scale * LOG2E
+    scale2 = scale_ref[0] * LOG2E
     col_of, row_of = places(ids_ref)
     columns = col_shift[...]
     lanes = lax.broadcasted_iota(jnp.int32, (ROWS, 8 * ROWS), 1)
@@ -228,25 +242,16 @@
                 part = logits[b * ROWS : (b + 1) * ROWS]
                 soft = jnp.exp2(part - shift) + jnp.exp2(part - columns)
                 pieces.append(jnp.where(pos == lanes, soft - 1.0, soft).astype(BF16))
-            grad = jnp.concatenate(pieces, axis=0)
-            d_ref[h * CHUNK : (h + 1) * CHUNK, :] = grad
-            update = lax.dot_general(
-                grad, rows, (((0,), (0,)), ((), ())), preferred_element_type=F32
-            )
-            if q == 0 and h == 0:
-                acc[...] = update
-            else:
-                acc[...] += update
-    for j, out in enumerate((h0, h1)):
-        out[0:QUAD, :] = (scale * acc[j * QUAD : (j + 1) * QUAD, :]).astype(BF16)
-        out[QUAD : QUAD + EXTRA, :] = row_tail[...]
-
-
-def images_kernel(scale_ref, col_tail, t0, t1, d_ref, g_ref):
-    product = jnp.dot(d_ref[:, :QUAD], t0[...], preferred_element_type=F32)
-    product += jnp.dot(d_ref[:, QUAD:], t1[...], preferred_element_type=F32)
-    g_ref[0:QUAD, :] = (scale_ref[0] * product).astype(BF16)
-    g_ref[QUAD : QUAD + EXTRA, :] = col_tail[...]
+            d_ref[h * CHUNK : (h + 1) * CHUNK, :] = jnp.concatenate(pieces, axis=0)
+
+
+def texts_grad_kernel(scale_ref, row_tail, i0, i1, i2, i3, d0, d1, d2, d3, *refs, j):
+    out = refs[-1]
+    rows = jnp.concatenate([r[...] for r in (i0, i1, i2, i3)], axis=0)
+    part = jnp.concatenate([d[:, j * QUAD : (j + 1) * QUAD] for d in (d0, d1, d2, d3)], axis=0)
+    update = lax.dot_general(rows, part, (((0,), (0,)), ((), ())), preferred_element_type=F32)
+    out[0:QUAD, :] = (scale_ref[0] * jnp.transpose(update)).astype(BF16)
+    out[QUAD : QUAD + EXTRA, :] = row_tail[...]
 
 
 def tail_sum(refs, first):
@@ -305,7 +310,7 @@
     txt0 = jnp.concatenate(gathered(unit_txt, ring_z), axis=0)
     imgs = gathered(img_own, ring_b)
     txt1 = shifted(txt0, other_core)
-    arrived = call(after_kernel, token, *imgs[1:], specs=[VMEM] * 3)
+    arrived = call(after_kernel, token, imgs[3])
 
     owner = partner // (16 * ROWS)
     steps = (row // 2 - owner // 2) % 4
@@ -317,11 +322,13 @@
 
     row_shape = shape((40, ROWS), F32)
     common = (ids, scale, pos)
-    in_place = [VMEM] * 6
+    stats = call(
+        functools.partial(forward_kernel, False, (0, 3)), [row_shape, shape((8, 8 * ROWS), F32)],
+        *common, imgs[0], imgs[3], txt0, txt1, arrived, specs=[SMEM, SMEM] + [VMEM] * 6,
+    )
     row_stat, col_stat = call(
-        forward_kernel, [row_shape, shape((16, ROWS), F32)],
-        *common, *imgs, txt0, txt1, arrived,
-        specs=[SMEM, SMEM, VMEM] + in_place + [anywhere],
+        functools.partial(forward_kernel, True, (2, 1)), [row_shape, shape((16, ROWS), F32)],
+        *common, imgs[2], imgs[1], txt0, txt1, *stats, specs=[SMEM, SMEM] + [VMEM] * 7,
     )
     for row_moves, col_move in ((ring_a, pair_z(False)), (ring_b, pair_z(True))):
         row_stat, col_stat = call(
@@ -336,19 +343,24 @@
     )
 
     sent = shape((QUAD + EXTRA, WIDTH), BF16)
-    *dlogits, txt_own, txt_other = call(
-        dlogit_kernel, [shape((QUAD, 8 * ROWS), BF16)] * 4 + [sent] * 2,
-        *common, row_shift, col_shift, row_tail, *imgs, txt0, txt1,
-        specs=[SMEM, SMEM] + [VMEM] * 4 + in_place,
-        scratch=[pltpu.VMEM((8 * ROWS, WIDTH), F32)],
-    )
     small = [shape((ROWS + EXTRA, WIDTH), BF16)] * 4
+    dlogits = call(
+        dlogit_kernel, [shape((QUAD, 8 * ROWS), BF16)] * 4,
+        *common, row_shift, col_shift, *imgs, txt0, txt1, cost=BUSY, specs=[SMEM, SMEM] + [VMEM] * 9,
+    )
     grads = [
-        call(
-            images_kernel, sent, scale, col_tail, txt0, txt1, d, specs=[SMEM] + [VMEM] * 4
-        )
+        call(images_grad, sent, scale, col_tail, txt0, txt1, d, cost=BUSY, specs=[SMEM] + [VMEM] * 4)
         for d in dlogits
     ]
+    texts_args = (scale, row_tail, *imgs, *dlogits)
+    txt_other = call(
+        functools.partial(texts_grad_kernel, j=1), sent, *texts_args, *grads[1:],
+        cost=BUSY, specs=[SMEM] + [VMEM] * 12,
+    )
+    txt_own = call(
+        functools.partial(texts_grad_kernel, j=0), sent, *texts_args, txt_other,
+        cost=BUSY, specs=[SMEM] + [VMEM] * 10,
+    )
     txt_parts = call(
         partial_kernel, small, txt_own, shifted(txt_other, other_core)
     )

time: 93.9 us -> 87.5 us (0.932)
  waiting for transfers between devices: 31.1 us -> 21.9 us
  starting transfers between devices: 39.9 us -> 41.6 us
  Pallas kernels: 19.6 us -> 20.6 us
    ppermute x29, waiting for transfers between devices: 31.1 us -> 21.9 us  [shifted(): return lax.ppermute(value, RC, pairs)]
    ppermute x29, starting transfers between devices: 39.9 us -> 41.6 us  [shifted(): return lax.ppermute(value, RC, pairs)]
    pallas_call x14 -> x17, Pallas kernels: 18.6 us -> 19.5 us  [call(): pl.pallas_call(kernel, out_shape=outs, in_specs=specs or [VMEM] * len(arg...]
  transfers between devices with their start and end apart: 29 -> 29, of which waited for: 10 -> 13; matrix products, arithmetic and copies ran while one was open for 0% -> 1% of each run, Pallas kernels for 4% -> 11%
where the time goes in v3:
time: 87.5 us; the launch traced here: 87.3 us
  starting transfers between devices  41.6 us (48%)
  waiting for transfers between devices  21.9 us (25%)
  Pallas kernels  20.6 us (24%)
  between operations  1.68 us (2%)
  local copies, waits for them, and re-layouts  1.27 us (1%)
    ppermute x29, starting transfers between devices, shifted(): return lax.ppermute(value, RC, pairs)  41.6 us
    ppermute x29, waiting for transfers between devices, shifted(): return lax.ppermute(value, RC, pairs)  21.9 us
    pallas_call x17, Pallas kernels, call(): pl.pallas_call(kernel, out_shape=outs, in_specs=specs or [VMEM] * len(arg...  19.5 us
  transfers between devices with their start and end apart: 29, of which 13 were waited for; matrix products, arithmetic and copies ran while one was open for 1% of the time, Pallas kernels for 11%

profile of v3, /device:TPU:0, one launch (start us, length us, event | category | flops | bytes accessed | tf_op | source)
XLA Modules:
  0.0 87.3 jit_solution(12129396274128387385)
XLA Ops:
  0.6 0.0 copy-start.1
  0.7 0.9 %copy-done.1 = bf16[128,512]{1,0:T(8,128)(2,1)S(1)} copy-done((bf16[128,512]{1,0:T(8,128)(2,1)S(1)}, bf16[128,512]{1,0:T(8,128)(2,1)}, u32[]{:S(2)}) %copy-start.1) | copy-done | bytes 131096
  1.6 0.1 shard_map.75.refs_0_
  1.7 3.2 %collective-permute-start.2 = (bf16[128,512]{1,0:T(8,128)(2,1)S(1)}, bf16[128,512]{1,0:T(8,128)(2,1)S(1)}, u32[]{:S(2)}, u32[]{:S(2)}) collective-permute-start(bf16[128,512]{1,0:T(8,128)(2,1)S(1)} %shard_map.75.refs_0_), channel_id=1, source_target_pairs={{0,8},{1,9},{2,10},{3,11},{4,12},{5,13},{6,14},{7,15},{8,0},{9,1},... | collective-permute-start | bytes 393224 | tf_op jit(solution)/shard_map/ppermute | solution.py:37
  4.9 1.1 %collective-permute-start.1 = (bf16[128,512]{1,0:T(8,128)(2,1)S(1)}, bf16[128,512]{1,0:T(8,128)(2,1)S(1)}, u32[]{:S(2)}, u32[]{:S(2)}) collective-permute-start(bf16[128,512]{1,0:T(8,128)(2,1)S(1)} %shard_map.75.refs_0_), channel_id=1, source_target_pairs={{0,12},{1,13},{2,14},{3,15},{4,0},{5,1},{6,2},{7,3},{8,4},{9,5},{1... | collective-permute-start | bytes 393224 | tf_op jit(solution)/shard_map/ppermute | solution.py:37
  6.0 0.9 %collective-permute-start = (bf16[128,512]{1,0:T(8,128)(2,1)S(1)}, bf16[128,512]{1,0:T(8,128)(2,1)S(1)}, u32[]{:S(2)}, u32[]{:S(2)}) collective-permute-start(bf16[128,512]{1,0:T(8,128)(2,1)S(1)} %shard_map.75.refs_0_), channel_id=1, source_target_pairs={{0,4},{1,5},{2,6},{3,7},{4,8},{5,9},{6,10},{7,11},{8,12},{9,13},{1... | collective-permute-start | bytes 393224 | tf_op jit(solution)/shard_map/ppermute | solution.py:37
  6.9 0.1 shard_map.76
  7.0 4.0 %collective-permute-start.7 = (bf16[128,512]{1,0:T(8,128)(2,1)S(1)}, bf16[128,512]{1,0:T(8,128)(2,1)S(1)}, u32[]{:S(2)}, u32[]{:S(2)}) collective-permute-start(bf16[128,512]{1,0:T(8,128)(2,1)S(1)} %shard_map.76), channel_id=1, source_target_pairs={{0,64},{1,65},{2,66},{3,67},{4,68},{5,69},{6,70},{7,71},{8,72},{9,... | collective-permute-start | bytes 393224 | tf_op jit(solution)/shard_map/ppermute | solution.py:37
  11.0 0.7 collective-permute-start.6
  11.7 0.0 collective-permute-done.2
  11.7 1.3 %collective-permute-start.5 = (bf16[128,512]{1,0:T(8,128)(2,1)S(1)}, bf16[128,512]{1,0:T(8,128)(2,1)S(1)}, u32[]{:S(2)}, u32[]{:S(2)}) collective-permute-start(bf16[128,512]{1,0:T(8,128)(2,1)S(1)} %shard_map.76), channel_id=1, source_target_pairs={{0,32},{1,33},{2,34},{3,35},{4,36},{5,37},{6,38},{7,39},{8,40},{9,... | collective-permute-start | bytes 393224 | tf_op jit(solution)/shard_map/ppermute | solution.py:37
  13.0 0.0 collective-permute-done
  13.1 3.3 %collective-permute-start.9 = (bf16[512,512]{1,0:T(8,128)(2,1)S(1)}, bf16[512,512]{1,0:T(8,128)(2,1)S(1)}, u32[]{:S(2)}, u32[]{:S(2)}) collective-permute-start(bf16[512,512]{1,0:T(8,128)(2,1)S(1)} %pad_maximum_fusion.i0), channel_id=1, source_target_pairs={{0,2},{1,3},{2,0},{3,1},{4,6},{5,7},{6,4},{7,5},{8,10},{9,11},{10,... | collective-permute-start | bytes 1572872 | tf_op jit(solution)/shard_map/ppermute | solution.py:37
  16.3 1.1 %collective-permute-done.6 = bf16[128,512]{1,0:T(8,128)(2,1)S(1)} collective-permute-done((bf16[128,512]{1,0:T(8,128)(2,1)S(1)}, bf16[128,512]{1,0:T(8,128)(2,1)S(1)}, u32[]{:S(2)}, u32[]{:S(2)}) %collective-permute-start.6) | collective-permute-done | bytes 131104 | tf_op jit(solution)/shard_map/ppermute | solution.py:37
  17.4 0.5 collective-permute-done.5
  17.9 0.1 collective-permute-start.8
  18.0 1.6 %collective-permute-start.4 = (bf16[512,512]{1,0:T(8,128)(2,1)S(1)}, bf16[512,512]{1,0:T(8,128)(2,1)S(1)}, u32[]{:S(2)}, u32[]{:S(2)}) collective-permute-start(bf16[512,512]{1,0:T(8,128)(2,1)S(1)} %pad_maximum_fusion.i0), channel_id=1, source_target_pairs={{0,1},{1,2},{2,3},{3,0},{4,5},{5,6},{6,7},{7,4},{8,9},{9,10},{10,1... | collective-permute-start | bytes 1572872 | tf_op jit(solution)/shard_map/ppermute | solution.py:37
  19.7 1.7 %collective-permute-start.3 = (bf16[512,512]{1,0:T(8,128)(2,1)S(1)}, bf16[512,512]{1,0:T(8,128)(2,1)S(1)}, u32[]{:S(2)}, u32[]{:S(2)}) collective-permute-start(bf16[512,512]{1,0:T(8,128)(2,1)S(1)} %pad_maximum_fusion.i0), channel_id=1, source_target_pairs={{0,3},{1,0},{2,1},{3,2},{4,7},{5,4},{6,5},{7,6},{8,11},{9,8},{10,9... | collective-permute-start | bytes 1572872 | tf_op jit(solution)/shard_map/ppermute | solution.py:37
  22.0 0.1 pad_add_fusion.ids_ref
  22.2 1.8 %collective-permute-done.9.refs_0_.i1.i3 = bf16[512,512]{1,0:T(8,128)(2,1)S(1)} collective-permute-done((bf16[512,512]{1,0:T(8,128)(2,1)S(1)}, bf16[512,512]{1,0:T(8,128)(2,1)S(1)}, u32[]{:S(2)}, u32[]{:S(2)}) %collective-permute-start.9) | collective-permute-done | bytes 524320 | tf_op jit(solution)/shard_map/ppermute | solution.py:37
  23.9 0.0 collective-permute-done.8.t1
  23.9 0.3 broadcast_in_dim.8.pos_ref
  24.3 4.0 %shard_map.78 = (f32[40,128]{1,0:T(8,128)S(1)}, f32[8,1024]{1,0:T(8,128)S(1)}) custom-call(s32[2]{0:T(128)S(1)} %pad_add_fusion.ids_ref, f32[1]{0:T(128)S(6)} %exp.3.scale_ref, s32[2048,128]{1,0:T(8,128)S(1)} %broadcast_in_dim.8.pos_ref, bf16[512,512]{1,0:T(8,128)(2,1)S(1)} %pad_maximum_fusion.i0, bf16[512,512]{1,0:T(8,128)(2,1)S(1)} %collective-permute-done.9.refs_0_.i1.i3, ...), custom_call_target="tpu_custom_call" | custom-call | tf_op jit(solution)/shard_map/pallas_call | solution.py:57
  28.2 1.2 %collective-permute-done.4.i1 = bf16[512,512]{1,0:T(8,128)(2,1)S(1)} collective-permute-done((bf16[512,512]{1,0:T(8,128)(2,1)S(1)}, bf16[512,512]{1,0:T(8,128)(2,1)S(1)}, u32[]{:S(2)}, u32[]{:S(2)}) %collective-permute-start.4) | collective-permute-done | bytes 524320 | tf_op jit(solution)/shard_map/ppermute | solution.py:37
  29.4 0.3 collective-permute-done.3.i0.i2
  29.8 4.1 %shard_map.79 = (f32[40,128]{1,0:T(8,128)S(1)}, f32[16,128]{1,0:T(8,128)S(1)}) custom-call(s32[2]{0:T(128)S(1)} %pad_add_fusion.ids_ref, f32[1]{0:T(128)S(6)} %exp.3.scale_ref, s32[2048,128]{1,0:T(8,128)S(1)} %broadcast_in_dim.8.pos_ref, bf16[512,512]{1,0:T(8,128)(2,1)S(1)} %collective-permute-done.3.i0.i2, bf16[512,512]{1,0:T(8,128)(2,1)S(1)} %collective-permute-done.4.i1, ...), custom_call_target="tpu_custom_call" | custom-call | tf_op jit(solution)/shard_map/pallas_call | solution.py:57
  33.9 0.8 collective-permute-start.12
  34.7 2.5 %collective-permute-start.11 = (f32[40,128]{1,0:T(8,128)S(1)}, f32[40,128]{1,0:T(8,128)S(1)}, u32[]{:S(2)}, u32[]{:S(2)}) collective-permute-start(f32[40,128]{1,0:T(8,128)S(1)} %get-tuple-element.30.r0), channel_id=1, source_target_pairs={{0,12},{1,13},{2,14},{3,15},{4,0},{5,1},{6,2},{7,3},{8,4},{9,5},{1... | collective-permute-start | bytes 61448 | tf_op jit(solution)/shard_map/ppermute | solution.py:37
  37.2 0.0 collective-permute-start.10
  37.2 1.0 %collective-permute-start.13 = (f32[16,128]{1,0:T(8,128)S(1)}, f32[16,128]{1,0:T(8,128)S(1)}, u32[]{:S(2)}, u32[]{:S(2)}) collective-permute-start(f32[16,128]{1,0:T(8,128)S(1)} %get-tuple-element.31.c0), channel_id=1, source_target_pairs={{0,32},{1,33},{2,34},{3,35},{4,36},{5,37},{6,38},{7,39},{8,40},{9,... | collective-permute-start | bytes 24584 | tf_op jit(solution)/shard_map/ppermute | solution.py:37
  38.3 2.6 %collective-permute-done.13.c1 = f32[16,128]{1,0:T(8,128)S(1)} collective-permute-done((f32[16,128]{1,0:T(8,128)S(1)}, f32[16,128]{1,0:T(8,128)S(1)}, u32[]{:S(2)}, u32[]{:S(2)}) %collective-permute-start.13) | collective-permute-done | bytes 8224 | tf_op jit(solution)/shard_map/ppermute | solution.py:37
  40.9 1.3 %collective-permute-done.10.r1 = f32[40,128]{1,0:T(8,128)S(1)} collective-permute-done((f32[40,128]{1,0:T(8,128)S(1)}, f32[40,128]{1,0:T(8,128)S(1)}, u32[]{:S(2)}, u32[]{:S(2)}) %collective-permute-start.10) | collective-permute-done | bytes 20512 | tf_op jit(solution)/shard_map/ppermute | solution.py:37
  42.3 3.1 %collective-permute-start.16 = (f32[40,128]{1,0:T(8,128)S(1)}, f32[40,128]{1,0:T(8,128)S(1)}, u32[]{:S(2)}, u32[]{:S(2)}) collective-permute-start(f32[40,128]{1,0:T(8,128)S(1)} %get-tuple-element.32.r0), channel_id=1, source_target_pairs={{0,2},{1,3},{2,0},{3,1},{4,6},{5,7},{6,4},{7,5},{8,10},{9,11},{10,... | collective-permute-start | bytes 61448 | tf_op jit(solution)/shard_map/ppermute | solution.py:37
  45.4 1.2 %collective-permute-start.15 = (f32[40,128]{1,0:T(8,128)S(1)}, f32[40,128]{1,0:T(8,128)S(1)}, u32[]{:S(2)}, u32[]{:S(2)}) collective-permute-start(f32[40,128]{1,0:T(8,128)S(1)} %get-tuple-element.32.r0), channel_id=1, source_target_pairs={{0,3},{1,0},{2,1},{3,2},{4,7},{5,4},{6,5},{7,6},{8,11},{9,8},{10,9... | collective-permute-start | bytes 61448 | tf_op jit(solution)/shard_map/ppermute | solution.py:37
  46.6 0.8 collective-permute-start.14
  47.4 2.3 %collective-permute-start.17 = (f32[16,128]{1,0:T(8,128)S(1)}, f32[16,128]{1,0:T(8,128)S(1)}, u32[]{:S(2)}, u32[]{:S(2)}) collective-permute-start(f32[16,128]{1,0:T(8,128)S(1)} %get-tuple-element.33.c0), channel_id=1, source_target_pairs={{0,96},{1,97},{2,98},{3,99},{4,100},{5,101},{6,102},{7,103},{8,104... | collective-permute-start | bytes 24584 | tf_op jit(solution)/shard_map/ppermute | solution.py:37
  49.7 2.6 %collective-permute-done.17.c1 = f32[16,128]{1,0:T(8,128)S(1)} collective-permute-done((f32[16,128]{1,0:T(8,128)S(1)}, f32[16,128]{1,0:T(8,128)S(1)}, u32[]{:S(2)}, u32[]{:S(2)}) %collective-permute-start.17) | collective-permute-done | bytes 8224 | tf_op jit(solution)/shard_map/ppermute | solution.py:37
  52.3 0.1 collective-permute-start.18
  52.4 1.2 %collective-permute-done.18.c1 = f32[16,128]{1,0:T(8,128)S(1)} collective-permute-done((f32[16,128]{1,0:T(8,128)S(1)}, f32[16,128]{1,0:T(8,128)S(1)}, u32[]{:S(2)}, u32[]{:S(2)}) %collective-permute-start.18) | collective-permute-done | bytes 8224 | tf_op jit(solution)/shard_map/ppermute | solution.py:37
  53.6 0.7 shard_map.82
  54.3 4.0 %shard_map.83 = (bf16[512,1024]{1,0:T(8,128)(2,1)S(1)}, bf16[512,1024]{1,0:T(8,128)(2,1)S(1)}, bf16[512,1024]{1,0:T(8,128)(2,1)S(1)}, bf16[512,1024]{1,0:T(8,128)(2,1)S(1)}) custom-call(s32[2]{0:T(128)S(1)} %pad_add_fusion.ids_ref, f32[1]{0:T(128)S(6)} %exp.3.scale_ref, s32[2048,128]{1,0:T(8,128)S(1)} %broadcast_in_dim.8.pos_ref, ...), custom_call_target="tpu_custom_call" | custom-call | flops 10000000000 | bytes 1000000 | tf_op jit(solution)/shard_map/pallas_call | solution.py:57
  58.3 0.7 shard_map.86.refs_2_
  59.0 0.8 collective-permute-start.22
  59.8 0.7 shard_map.85.refs_1_
  60.5 2.6 %collective-permute-start.21 = (bf16[528,512]{1,0:T(8,128)(2,1)S(1)}, bf16[528,512]{1,0:T(8,128)(2,1)S(1)}, u32[]{:S(2)}, u32[]{:S(2)}) collective-permute-start(bf16[528,512]{1,0:T(8,128)(2,1)S(1)} %shard_map.85.refs_1_), channel_id=1, source_target_pairs={{0,1},{1,2},{2,3},{3,0},{4,5},{5,6},{6,7},{7,4},{8,9},{9,10},{10,1... | collective-permute-start | bytes 1622024 | tf_op jit(solution)/shard_map/ppermute | solution.py:37
  63.2 0.7 shard_map.84.refs_0_
  63.9 0.7 collective-permute-start.20
  64.6 1.5 %shard_map.87.refs_0_ = bf16[528,512]{1,0:T(8,128)(2,1)S(1)} custom-call(f32[1]{0:T(128)S(6)} %exp.3.scale_ref, bf16[16,512]{1,0:T(8,128)(2,1)S(1)} %get-tuple-element.36.row_tail, bf16[512,512]{1,0:T(8,128)(2,1)S(1)} %pad_maximum_fusion.i0, bf16[512,512]{1,0:T(8,128)(2,1)S(1)} %collective-permute-done.4.i1, ...), custom_call_target="tpu_custom_call" | custom-call | flops 10000000000 | bytes 1000000 | tf_op jit(solution)/shard_map/pallas_call | solution.py:57
  66.2 0.1 collective-permute-start.19
  66.2 1.5 %shard_map.88.refs_0_ = bf16[528,512]{1,0:T(8,128)(2,1)S(1)} custom-call(f32[1]{0:T(128)S(6)} %exp.3.scale_ref, bf16[16,512]{1,0:T(8,128)(2,1)S(1)} %get-tuple-element.36.row_tail, bf16[512,512]{1,0:T(8,128)(2,1)S(1)} %pad_maximum_fusion.i0, bf16[512,512]{1,0:T(8,128)(2,1)S(1)} %collective-permute-done.4.i1, ...), custom_call_target="tpu_custom_call" | custom-call | flops 10000000000 | bytes 1000000 | tf_op jit(solution)/shard_map/pallas_call | solution.py:57
  67.8 0.4 collective-permute-done.19.refs_1_
  68.2 0.2 shard_map.89
  68.3 2.5 %collective-permute-start.26 = (bf16[144,512]{1,0:T(8,128)(2,1)S(1)}, bf16[144,512]{1,0:T(8,128)(2,1)S(1)}, u32[]{:S(2)}, u32[]{:S(2)}) collective-permute-start(bf16[144,512]{1,0:T(8,128)(2,1)S(1)} %get-tuple-element.49), channel_id=1, source_target_pairs={{0,96},{1,97},{2,98},{3,99},{4,100},{5,101},{6,102},{7,103},{8,104... | collective-permute-start | bytes 442376 | tf_op jit(solution)/shard_map/ppermute | solution.py:37
  70.9 0.7 shard_map.90.refs_0_
  71.6 0.1 collective-permute-start.27
  71.7 1.5 %collective-permute-start.28 = (bf16[144,512]{1,0:T(8,128)(2,1)S(1)}, bf16[144,512]{1,0:T(8,128)(2,1)S(1)}, u32[]{:S(2)}, u32[]{:S(2)}) collective-permute-start(bf16[144,512]{1,0:T(8,128)(2,1)S(1)} %get-tuple-element.51), channel_id=1, source_target_pairs={{0,64},{1,65},{2,66},{3,67},{4,68},{5,69},{6,70},{7,71},{8,72},{9,... | collective-permute-start | bytes 442376 | tf_op jit(solution)/shard_map/ppermute | solution.py:37
  73.2 2.6 %collective-permute-done.21.refs_2_ = bf16[528,512]{1,0:T(8,128)(2,1)S(1)} collective-permute-done((bf16[528,512]{1,0:T(8,128)(2,1)S(1)}, bf16[528,512]{1,0:T(8,128)(2,1)S(1)}, u32[]{:S(2)}, u32[]{:S(2)}) %collective-permute-start.21) | collective-permute-done | bytes 540704 | tf_op jit(solution)/shard_map/ppermute | solution.py:37
  75.7 0.4 shard_map.91
  76.1 2.0 %collective-permute-start.23 = (bf16[144,512]{1,0:T(8,128)(2,1)S(1)}, bf16[144,512]{1,0:T(8,128)(2,1)S(1)}, u32[]{:S(2)}, u32[]{:S(2)}) collective-permute-start(bf16[144,512]{1,0:T(8,128)(2,1)S(1)} %get-tuple-element.46), channel_id=1, source_target_pairs={{0,12},{1,13},{2,14},{3,15},{4,0},{5,1},{6,2},{7,3},{8,4},{9,5},{1... | collective-permute-start | bytes 442376 | tf_op jit(solution)/shard_map/ppermute | solution.py:37
  78.1 0.1 collective-permute-start.24
  78.2 1.5 %collective-permute-start.25 = (bf16[144,512]{1,0:T(8,128)(2,1)S(1)}, bf16[144,512]{1,0:T(8,128)(2,1)S(1)}, u32[]{:S(2)}, u32[]{:S(2)}) collective-permute-start(bf16[144,512]{1,0:T(8,128)(2,1)S(1)} %get-tuple-element.48), channel_id=1, source_target_pairs={{0,8},{1,9},{2,10},{3,11},{4,12},{5,13},{6,14},{7,15},{8,0},{9,1},... | collective-permute-start | bytes 442376 | tf_op jit(solution)/shard_map/ppermute | solution.py:37
  79.7 2.2 %collective-permute-done.27.b2 = bf16[144,512]{1,0:T(8,128)(2,1)S(1)} collective-permute-done((bf16[144,512]{1,0:T(8,128)(2,1)S(1)}, bf16[144,512]{1,0:T(8,128)(2,1)S(1)}, u32[]{:S(2)}, u32[]{:S(2)}) %collective-permute-start.27) | collective-permute-done | bytes 147488 | tf_op jit(solution)/shard_map/ppermute | solution.py:37
  81.8 4.2 %collective-permute-done.24.a2 = bf16[144,512]{1,0:T(8,128)(2,1)S(1)} collective-permute-done((bf16[144,512]{1,0:T(8,128)(2,1)S(1)}, bf16[144,512]{1,0:T(8,128)(2,1)S(1)}, u32[]{:S(2)}, u32[]{:S(2)}) %collective-permute-start.24) | collective-permute-done | bytes 147488 | tf_op jit(solution)/shard_map/ppermute | solution.py:37
  86.1 1.1 %shard_map.92 = (f32[128,512]{1,0:T(8,128)}, f32[128,512]{1,0:T(8,128)}, f32[1]{0:T(128)}, f32[1]{0:T(128)}) custom-call(bf16[128,512]{1,0:T(8,128)(2,1)S(1)} %copy-done.2, bf16[128,512]{1,0:T(8,128)(2,1)S(1)} %copy-done, bf16[144,512]{1,0:T(8,128)(2,1)S(1)} %get-tuple-element.45.a0, bf16[144,512]{1,0:T(8,128)(2,1)S(1)} %collective-permute-done.23.a1, ...), custom_call_target="tpu_custom_call" | custom-call | tf_op jit(solution)/shard_map/pallas_call | solution.py:375
  (25 shorter events, 0.2 us)
Async XLA Ops:
  0.6 6.3 %copy-start = (bf16[128,512]{1,0:T(8,128)(2,1)S(1)}, bf16[128,512]{1,0:T(8,128)(2,1)}, u32[]{:S(2)}) copy-start(bf16[128,512]{1,0:T(8,128)(2,1)} %txt_ref.1) | copy-start | bytes 393220
  0.6 0.9 %copy-start.1 = (bf16[128,512]{1,0:T(8,128)(2,1)S(1)}, bf16[128,512]{1,0:T(8,128)(2,1)}, u32[]{:S(2)}) copy-start(bf16[128,512]{1,0:T(8,128)(2,1)} %img_ref.1) | copy-start | bytes 393220
  1.7 10.0 %collective-permute-start.2 = (bf16[128,512]{1,0:T(8,128)(2,1)S(1)}, bf16[128,512]{1,0:T(8,128)(2,1)S(1)}, u32[]{:S(2)}, u32[]{:S(2)}) collective-permute-start(bf16[128,512]{1,0:T(8,128)(2,1)S(1)} %shard_map.75.refs_0_), channel_id=1, source_target_pairs={{0,8},{1,9},{2,10},{3,11},{4,12},{5,13},{6,14},{7,15},{8,0},{9,1},... | collective-permute-start | bytes 393224 | tf_op jit(solution)/shard_map/ppermute | solution.py:37
  4.9 8.1 %collective-permute-start.1 = (bf16[128,512]{1,0:T(8,128)(2,1)S(1)}, bf16[128,512]{1,0:T(8,128)(2,1)S(1)}, u32[]{:S(2)}, u32[]{:S(2)}) collective-permute-start(bf16[128,512]{1,0:T(8,128)(2,1)S(1)} %shard_map.75.refs_0_), channel_id=1, source_target_pairs={{0,12},{1,13},{2,14},{3,15},{4,0},{5,1},{6,2},{7,3},{8,4},{9,5},{1... | collective-permute-start | bytes 393224 | tf_op jit(solution)/shard_map/ppermute | solution.py:37
  6.0 7.0 %collective-permute-start = (bf16[128,512]{1,0:T(8,128)(2,1)S(1)}, bf16[128,512]{1,0:T(8,128)(2,1)S(1)}, u32[]{:S(2)}, u32[]{:S(2)}) collective-permute-start(bf16[128,512]{1,0:T(8,128)(2,1)S(1)} %shard_map.75.refs_0_), channel_id=1, source_target_pairs={{0,4},{1,5},{2,6},{3,7},{4,8},{5,9},{6,10},{7,11},{8,12},{9,13},{1... | collective-permute-start | bytes 393224 | tf_op jit(solution)/shard_map/ppermute | solution.py:37
  7.0 9.3 %collective-permute-start.7 = (bf16[128,512]{1,0:T(8,128)(2,1)S(1)}, bf16[128,512]{1,0:T(8,128)(2,1)S(1)}, u32[]{:S(2)}, u32[]{:S(2)}) collective-permute-start(bf16[128,512]{1,0:T(8,128)(2,1)S(1)} %shard_map.76), channel_id=1, source_target_pairs={{0,64},{1,65},{2,66},{3,67},{4,68},{5,69},{6,70},{7,71},{8,72},{9,... | collective-permute-start | bytes 393224 | tf_op jit(solution)/shard_map/ppermute | solution.py:37
  11.0 6.4 %collective-permute-start.6 = (bf16[128,512]{1,0:T(8,128)(2,1)S(1)}, bf16[128,512]{1,0:T(8,128)(2,1)S(1)}, u32[]{:S(2)}, u32[]{:S(2)}) collective-permute-start(bf16[128,512]{1,0:T(8,128)(2,1)S(1)} %shard_map.76), channel_id=1, source_target_pairs={{0,96},{1,97},{2,98},{3,99},{4,100},{5,101},{6,102},{7,103},{8,104... | collective-permute-start | bytes 393224 | tf_op jit(solution)/shard_map/ppermute | solution.py:37
  11.7 6.2 %collective-permute-start.5 = (bf16[128,512]{1,0:T(8,128)(2,1)S(1)}, bf16[128,512]{1,0:T(8,128)(2,1)S(1)}, u32[]{:S(2)}, u32[]{:S(2)}) collective-permute-start(bf16[128,512]{1,0:T(8,128)(2,1)S(1)} %shard_map.76), channel_id=1, source_target_pairs={{0,32},{1,33},{2,34},{3,35},{4,36},{5,37},{6,38},{7,39},{8,40},{9,... | collective-permute-start | bytes 393224 | tf_op jit(solution)/shard_map/ppermute | solution.py:37
  13.1 10.9 %collective-permute-start.9 = (bf16[512,512]{1,0:T(8,128)(2,1)S(1)}, bf16[512,512]{1,0:T(8,128)(2,1)S(1)}, u32[]{:S(2)}, u32[]{:S(2)}) collective-permute-start(bf16[512,512]{1,0:T(8,128)(2,1)S(1)} %pad_maximum_fusion.i0), channel_id=1, source_target_pairs={{0,2},{1,3},{2,0},{3,1},{4,6},{5,7},{6,4},{7,5},{8,10},{9,11},{10,... | collective-permute-start | bytes 1572872 | tf_op jit(solution)/shard_map/ppermute | solution.py:37
  17.9 6.0 %collective-permute-start.8 = (bf16[512,512]{1,0:T(8,128)(2,1)S(1)}, bf16[512,512]{1,0:T(8,128)(2,1)S(1)}, u32[]{:S(2)}, u32[]{:S(2)}) collective-permute-start(bf16[512,512]{1,0:T(8,128)(2,1)S(1)} %pad_maximum_fusion.1.t0), channel_id=1, source_target_pairs={{0,16},{1,17},{2,18},{3,19},{4,20},{5,21},{6,22},{7,23},{8,24},{9,... | collective-permute-start | bytes 1572872 | tf_op jit(solution)/shard_map/ppermute | solution.py:37
  18.0 11.4 %collective-permute-start.4 = (bf16[512,512]{1,0:T(8,128)(2,1)S(1)}, bf16[512,512]{1,0:T(8,128)(2,1)S(1)}, u32[]{:S(2)}, u32[]{:S(2)}) collective-permute-start(bf16[512,512]{1,0:T(8,128)(2,1)S(1)} %pad_maximum_fusion.i0), channel_id=1, source_target_pairs={{0,1},{1,2},{2,3},{3,0},{4,5},{5,6},{6,7},{7,4},{8,9},{9,10},{10,1... | collective-permute-start | bytes 1572872 | tf_op jit(solution)/shard_map/ppermute | solution.py:37
  19.7 10.1 %collective-permute-start.3 = (bf16[512,512]{1,0:T(8,128)(2,1)S(1)}, bf16[512,512]{1,0:T(8,128)(2,1)S(1)}, u32[]{:S(2)}, u32[]{:S(2)}) collective-permute-start(bf16[512,512]{1,0:T(8,128)(2,1)S(1)} %pad_maximum_fusion.i0), channel_id=1, source_target_pairs={{0,3},{1,0},{2,1},{3,2},{4,7},{5,4},{6,5},{7,6},{8,11},{9,8},{10,9... | collective-permute-start | bytes 1572872 | tf_op jit(solution)/shard_map/ppermute | solution.py:37
  21.3 0.8 copy-start.3
  33.9 7.0 %collective-permute-start.12 = (f32[40,128]{1,0:T(8,128)S(1)}, f32[40,128]{1,0:T(8,128)S(1)}, u32[]{:S(2)}, u32[]{:S(2)}) collective-permute-start(f32[40,128]{1,0:T(8,128)S(1)} %get-tuple-element.30.r0), channel_id=1, source_target_pairs={{0,8},{1,9},{2,10},{3,11},{4,12},{5,13},{6,14},{7,15},{8,0},{9,1},... | collective-permute-start | bytes 61448 | tf_op jit(solution)/shard_map/ppermute | solution.py:37
  34.7 6.2 %collective-permute-start.11 = (f32[40,128]{1,0:T(8,128)S(1)}, f32[40,128]{1,0:T(8,128)S(1)}, u32[]{:S(2)}, u32[]{:S(2)}) collective-permute-start(f32[40,128]{1,0:T(8,128)S(1)} %get-tuple-element.30.r0), channel_id=1, source_target_pairs={{0,12},{1,13},{2,14},{3,15},{4,0},{5,1},{6,2},{7,3},{8,4},{9,5},{1... | collective-permute-start | bytes 61448 | tf_op jit(solution)/shard_map/ppermute | solution.py:37
  37.2 5.0 %collective-permute-start.10 = (f32[40,128]{1,0:T(8,128)S(1)}, f32[40,128]{1,0:T(8,128)S(1)}, u32[]{:S(2)}, u32[]{:S(2)}) collective-permute-start(f32[40,128]{1,0:T(8,128)S(1)} %get-tuple-element.30.r0), channel_id=1, source_target_pairs={{0,4},{1,5},{2,6},{3,7},{4,8},{5,9},{6,10},{7,11},{8,12},{9,13},{1... | collective-permute-start | bytes 61448 | tf_op jit(solution)/shard_map/ppermute | solution.py:37
  37.2 3.7 %collective-permute-start.13 = (f32[16,128]{1,0:T(8,128)S(1)}, f32[16,128]{1,0:T(8,128)S(1)}, u32[]{:S(2)}, u32[]{:S(2)}) collective-permute-start(f32[16,128]{1,0:T(8,128)S(1)} %get-tuple-element.31.c0), channel_id=1, source_target_pairs={{0,32},{1,33},{2,34},{3,35},{4,36},{5,37},{6,38},{7,39},{8,40},{9,... | collective-permute-start | bytes 24584 | tf_op jit(solution)/shard_map/ppermute | solution.py:37
  42.3 10.0 %collective-permute-start.16 = (f32[40,128]{1,0:T(8,128)S(1)}, f32[40,128]{1,0:T(8,128)S(1)}, u32[]{:S(2)}, u32[]{:S(2)}) collective-permute-start(f32[40,128]{1,0:T(8,128)S(1)} %get-tuple-element.32.r0), channel_id=1, source_target_pairs={{0,2},{1,3},{2,0},{3,1},{4,6},{5,7},{6,4},{7,5},{8,10},{9,11},{10,... | collective-permute-start | bytes 61448 | tf_op jit(solution)/shard_map/ppermute | solution.py:37
  45.4 6.9 %collective-permute-start.15 = (f32[40,128]{1,0:T(8,128)S(1)}, f32[40,128]{1,0:T(8,128)S(1)}, u32[]{:S(2)}, u32[]{:S(2)}) collective-permute-start(f32[40,128]{1,0:T(8,128)S(1)} %get-tuple-element.32.r0), channel_id=1, source_target_pairs={{0,3},{1,0},{2,1},{3,2},{4,7},{5,4},{6,5},{7,6},{8,11},{9,8},{10,9... | collective-permute-start | bytes 61448 | tf_op jit(solution)/shard_map/ppermute | solution.py:37
  46.6 5.7 %collective-permute-start.14 = (f32[40,128]{1,0:T(8,128)S(1)}, f32[40,128]{1,0:T(8,128)S(1)}, u32[]{:S(2)}, u32[]{:S(2)}) collective-permute-start(f32[40,128]{1,0:T(8,128)S(1)} %get-tuple-element.32.r0), channel_id=1, source_target_pairs={{0,1},{1,2},{2,3},{3,0},{4,5},{5,6},{6,7},{7,4},{8,9},{9,10},{10,1... | collective-permute-start | bytes 61448 | tf_op jit(solution)/shard_map/ppermute | solution.py:37
  47.4 4.9 %collective-permute-start.17 = (f32[16,128]{1,0:T(8,128)S(1)}, f32[16,128]{1,0:T(8,128)S(1)}, u32[]{:S(2)}, u32[]{:S(2)}) collective-permute-start(f32[16,128]{1,0:T(8,128)S(1)} %get-tuple-element.33.c0), channel_id=1, source_target_pairs={{0,96},{1,97},{2,98},{3,99},{4,100},{5,101},{6,102},{7,103},{8,104... | collective-permute-start | bytes 24584 | tf_op jit(solution)/shard_map/ppermute | solution.py:37
  52.3 1.3 %collective-permute-start.18 = (f32[16,128]{1,0:T(8,128)S(1)}, f32[16,128]{1,0:T(8,128)S(1)}, u32[]{:S(2)}, u32[]{:S(2)}) collective-permute-start(f32[16,128]{1,0:T(8,128)S(1)} %get-tuple-element.35.c0), channel_id=1, source_target_pairs={{0,16},{1,17},{2,18},{3,19},{4,20},{5,21},{6,22},{7,23},{8,24},{9,... | collective-permute-start | bytes 24584 | tf_op jit(solution)/shard_map/ppermute | solution.py:37
  59.0 12.7 %collective-permute-start.22 = (bf16[528,512]{1,0:T(8,128)(2,1)S(1)}, bf16[528,512]{1,0:T(8,128)(2,1)S(1)}, u32[]{:S(2)}, u32[]{:S(2)}) collective-permute-start(bf16[528,512]{1,0:T(8,128)(2,1)S(1)} %shard_map.86.refs_2_), channel_id=1, source_target_pairs={{0,2},{1,3},{2,0},{3,1},{4,6},{5,7},{6,4},{7,5},{8,10},{9,11},{10,... | collective-permute-start | bytes 1622024 | tf_op jit(solution)/shard_map/ppermute | solution.py:37
  60.5 15.2 %collective-permute-start.21 = (bf16[528,512]{1,0:T(8,128)(2,1)S(1)}, bf16[528,512]{1,0:T(8,128)(2,1)S(1)}, u32[]{:S(2)}, u32[]{:S(2)}) collective-permute-start(bf16[528,512]{1,0:T(8,128)(2,1)S(1)} %shard_map.85.refs_1_), channel_id=1, source_target_pairs={{0,1},{1,2},{2,3},{3,0},{4,5},{5,6},{6,7},{7,4},{8,9},{9,10},{10,1... | collective-permute-start | bytes 1622024 | tf_op jit(solution)/shard_map/ppermute | solution.py:37
  63.9 11.9 %collective-permute-start.20 = (bf16[528,512]{1,0:T(8,128)(2,1)S(1)}, bf16[528,512]{1,0:T(8,128)(2,1)S(1)}, u32[]{:S(2)}, u32[]{:S(2)}) collective-permute-start(bf16[528,512]{1,0:T(8,128)(2,1)S(1)} %shard_map.84.refs_0_), channel_id=1, source_target_pairs={{0,3},{1,0},{2,1},{3,2},{4,7},{5,4},{6,5},{7,6},{8,11},{9,8},{10,9... | collective-permute-start | bytes 1622024 | tf_op jit(solution)/shard_map/ppermute | solution.py:37
  66.2 2.0 %collective-permute-start.19 = (bf16[528,512]{1,0:T(8,128)(2,1)S(1)}, bf16[528,512]{1,0:T(8,128)(2,1)S(1)}, u32[]{:S(2)}, u32[]{:S(2)}) collective-permute-start(bf16[528,512]{1,0:T(8,128)(2,1)S(1)} %shard_map.87.refs_0_), channel_id=1, source_target_pairs={{0,16},{1,17},{2,18},{3,19},{4,20},{5,21},{6,22},{7,23},{8,24},{9,... | collective-permute-start | bytes 1622024 | tf_op jit(solution)/shard_map/ppermute | solution.py:37
  68.3 9.9 %collective-permute-start.26 = (bf16[144,512]{1,0:T(8,128)(2,1)S(1)}, bf16[144,512]{1,0:T(8,128)(2,1)S(1)}, u32[]{:S(2)}, u32[]{:S(2)}) collective-permute-start(bf16[144,512]{1,0:T(8,128)(2,1)S(1)} %get-tuple-element.49), channel_id=1, source_target_pairs={{0,96},{1,97},{2,98},{3,99},{4,100},{5,101},{6,102},{7,103},{8,104... | collective-permute-start | bytes 442376 | tf_op jit(solution)/shard_map/ppermute | solution.py:37
  71.6 10.2 %collective-permute-start.27 = (bf16[144,512]{1,0:T(8,128)(2,1)S(1)}, bf16[144,512]{1,0:T(8,128)(2,1)S(1)}, u32[]{:S(2)}, u32[]{:S(2)}) collective-permute-start(bf16[144,512]{1,0:T(8,128)(2,1)S(1)} %get-tuple-element.50), channel_id=1, source_target_pairs={{0,32},{1,33},{2,34},{3,35},{4,36},{5,37},{6,38},{7,39},{8,40},{9,... | collective-permute-start | bytes 442376 | tf_op jit(solution)/shard_map/ppermute | solution.py:37
  71.7 10.1 %collective-permute-start.28 = (bf16[144,512]{1,0:T(8,128)(2,1)S(1)}, bf16[144,512]{1,0:T(8,128)(2,1)S(1)}, u32[]{:S(2)}, u32[]{:S(2)}) collective-permute-start(bf16[144,512]{1,0:T(8,128)(2,1)S(1)} %get-tuple-element.51), channel_id=1, source_target_pairs={{0,64},{1,65},{2,66},{3,67},{4,68},{5,69},{6,70},{7,71},{8,72},{9,... | collective-permute-start | bytes 442376 | tf_op jit(solution)/shard_map/ppermute | solution.py:37
  75.7 10.3 %copy-start.2 = (bf16[128,512]{1,0:T(8,128)(2,1)S(1)}, bf16[128,512]{1,0:T(8,128)(2,1)}, u32[]{:S(2)}) copy-start(bf16[128,512]{1,0:T(8,128)(2,1)} %img_ref.1) | copy-start | bytes 393220
  76.1 5.7 %collective-permute-start.23 = (bf16[144,512]{1,0:T(8,128)(2,1)S(1)}, bf16[144,512]{1,0:T(8,128)(2,1)S(1)}, u32[]{:S(2)}, u32[]{:S(2)}) collective-permute-start(bf16[144,512]{1,0:T(8,128)(2,1)S(1)} %get-tuple-element.46), channel_id=1, source_target_pairs={{0,12},{1,13},{2,14},{3,15},{4,0},{5,1},{6,2},{7,3},{8,4},{9,5},{1... | collective-permute-start | bytes 442376 | tf_op jit(solution)/shard_map/ppermute | solution.py:37
  78.1 7.9 %collective-permute-start.24 = (bf16[144,512]{1,0:T(8,128)(2,1)S(1)}, bf16[144,512]{1,0:T(8,128)(2,1)S(1)}, u32[]{:S(2)}, u32[]{:S(2)}) collective-permute-start(bf16[144,512]{1,0:T(8,128)(2,1)S(1)} %get-tuple-element.47), channel_id=1, source_target_pairs={{0,4},{1,5},{2,6},{3,7},{4,8},{5,9},{6,10},{7,11},{8,12},{9,13},{1... | collective-permute-start | bytes 442376 | tf_op jit(solution)/shard_map/ppermute | solution.py:37
  78.2 7.9 %collective-permute-start.25 = (bf16[144,512]{1,0:T(8,128)(2,1)S(1)}, bf16[144,512]{1,0:T(8,128)(2,1)S(1)}, u32[]{:S(2)}, u32[]{:S(2)}) collective-permute-start(bf16[144,512]{1,0:T(8,128)(2,1)S(1)} %get-tuple-element.48), channel_id=1, source_target_pairs={{0,8},{1,9},{2,10},{3,11},{4,12},{5,13},{6,14},{7,15},{8,0},{9,1},... | collective-permute-start | bytes 442376 | tf_op jit(solution)/shard_map/ppermute | solution.py:37

commit v4 on v3

--- a/solution.py
+++ b/solution.py
@@ -115,41 +115,72 @@
 CHUNK = 256
 
 
-def forward_kernel(last, places_of, ids_ref, scale_ref, pos_ref, i0, i1, t0, t1, *refs):
+def either_way(scale_ref, part):
+    bounded = scale_ref[0] * (LOG2E * 1.01) <= 100.0
+    pl.when(bounded)(functools.partial(part, True))
+    pl.when(jnp.logical_not(bounded))(functools.partial(part, False))
+
+
+def forward_kernel(last, places_of, ids_ref, scale_ref, *refs):
+    either_way(
+        scale_ref, lambda bounded: forward_part(bounded, last, places_of, ids_ref, scale_ref, *refs)
+    )
+
+
+def lane_sums(values):
+    part = sum(values[:, c * ROWS : (c + 1) * ROWS] for c in range(8))
+    return jnp.sum(jnp.transpose(part), axis=0, keepdims=True)
+
+
+def forward_part(bounded, last, places_of, ids_ref, scale_ref, pos_ref, i0, i1, t0, t1, *refs):
     scale2 = scale_ref[0] * LOG2E
     col_of, row_of = places(ids_ref)
-    lanes = lax.broadcasted_iota(jnp.int32, (CHUNK, 8 * ROWS), 1)
+    lanes = lax.broadcasted_iota(jnp.int32, (1, 8 * ROWS), 1)
     if last:
         row_in, state_in, row_out, col_out = refs
         row_out[...] = row_in[...]
         col_high, col_total, col_weighted, picked = (state_in[i : i + 1, :] for i in range(4))
     else:
         _, row_out, state_out = refs
-        col_high = jnp.full((1, 8 * ROWS), -jnp.inf, F32)
+        col_high = jnp.full((1, 8 * ROWS), 0.0 if bounded else -jnp.inf, F32)
         col_total = col_weighted = picked = jnp.zeros((1, 8 * ROWS), F32)
     for q, rows_ref in zip(places_of, (i0, i1)):
         for h in range(QUAD // CHUNK):
             logits = logits2(rows_ref[h * CHUNK : (h + 1) * CHUNK, :], t0, t1, scale2)
-            high = jnp.max(logits, axis=1, keepdims=True)
-            weights = jnp.exp2(logits - high)
-            total = jnp.sum(weights, axis=1, keepdims=True)
-            mean = jnp.sum(weights * logits, axis=1, keepdims=True) / total
-            lse = high + jnp.log2(total)
+            if bounded:
+                weights = jnp.exp2(logits)
+                weighted = weights * logits
+                col_total += jnp.sum(weights, axis=0, keepdims=True)
+                col_weighted += jnp.sum(weighted, axis=0, keepdims=True)
+            else:
+                high = jnp.max(logits, axis=1, keepdims=True)
+                weights = jnp.exp2(logits - high)
+                total = jnp.sum(weights, axis=1, keepdims=True)
+                mean = jnp.sum(weights * logits, axis=1, keepdims=True) / total
+                lse = high + jnp.log2(total)
+                old = col_high
+                col_high = jnp.maximum(old, jnp.max(logits, axis=0, keepdims=True))
+                rescale = jnp.exp2(old - col_high)
+                weights = jnp.exp2(logits - col_high)
+                col_total = col_total * rescale + jnp.sum(weights, axis=0, keepdims=True)
+                col_weighted = col_weighted * rescale + jnp.sum(
+                    weights * logits, axis=0, keepdims=True
+                )
             pos = []
             for b in range(CHUNK // ROWS):
                 place = col_of(q, h * (CHUNK // ROWS) + b)
-                row_out[pl.ds(place, 1), :] = to_lanes(lse[b * ROWS : (b + 1) * ROWS])
-                row_out[pl.ds(16 + place, 1), :] = to_lanes(mean[b * ROWS : (b + 1) * ROWS])
+                block = slice(b * ROWS, (b + 1) * ROWS)
+                if bounded:
+                    total = lane_sums(weights[block])
+                    row_out[pl.ds(place, 1), :] = jnp.log2(total)
+                    row_out[pl.ds(16 + place, 1), :] = lane_sums(weighted[block]) / total
+                else:
+                    row_out[pl.ds(place, 1), :] = to_lanes(lse[block])
+                    row_out[pl.ds(16 + place, 1), :] = to_lanes(mean[block])
                 pos.append(pos_ref[pl.ds(pl.multiple_of(place * ROWS, ROWS), ROWS), :])
             pos = jnp.concatenate(pos, axis=0)
             pos = jnp.concatenate([pos] * 8, axis=1)
             picked += jnp.sum(jnp.where(pos == lanes, logits, 0.0), axis=0, keepdims=True)
-            old = col_high
-            col_high = jnp.maximum(old, jnp.max(logits, axis=0, keepdims=True))
-            rescale = jnp.exp2(old - col_high)
-            weights = jnp.exp2(logits - col_high)
-            col_total = col_total * rescale + jnp.sum(weights, axis=0, keepdims=True)
-            col_weighted = col_weighted * rescale + jnp.sum(weights * logits, axis=0, keepdims=True)
     if not last:
         for i, value in enumerate((col_high, col_total, col_weighted, picked)):
             state_out[i : i + 1, :] = value
@@ -174,8 +205,8 @@
     return high + jnp.log2(total), mean
 
 
-def merge_kernel(r0, r1, r2, r3, c0, c1, row_out, col_out):
-    refs = (r0, r1, r2, r3)
+def merge_kernel(*refs):
+    *refs, c0, c1, row_out, col_out = refs
     row_out[0:16, :], row_out[16:32, :] = merged(refs, 16)
     row_out[32:40, :] = sum(r[32:40, :] for r in refs)
     col_out[0:8, :], col_out[8:16, :] = merged((c0, c1), 8)
@@ -195,11 +226,11 @@
     return jnp.where(part == 2, low.astype(F32), out).astype(BF16)
 
 
-def shifts_kernel(ids_ref, row_ref, c0, c1, row_shift, columns, row_tail, col_tail, col_shift):
+def shifts_kernel(ids_ref, r0, r1, c0, c1, row_shift, columns, row_tail, col_tail, col_shift):
     _, row_of = places(ids_ref)
-    row_lse, row_mean = row_ref[0:16, :], row_ref[16:32, :]
+    row_lse, row_mean = merged((r0, r1), 16)
     col_lse, col_mean = merged((c0, c1), 8)
-    picked = row_ref[32:33, 0:1]
+    picked = r0[32:33, 0:1] + r1[32:33, 0:1]
     row_shift[...] = row_lse + 1.0
     col_shift[...] = col_lse + 1.0
     columns[...] = jnp.concatenate(
@@ -221,13 +252,18 @@
     g_ref[QUAD : QUAD + EXTRA, :] = col_tail[...]
 
 
-def dlogit_kernel(
-    ids_ref, scale_ref, pos_ref, row_shift, col_shift, i0, i1, i2, i3, t0, t1, d0, d1, d2, d3
+def dlogit_kernel(ids_ref, scale_ref, *refs):
+    either_way(scale_ref, lambda bounded: dlogit_part(bounded, ids_ref, scale_ref, *refs))
+
+
+def dlogit_part(
+    bounded, ids_ref, scale_ref, pos_ref, row_shift, col_shift, i0, i1, i2, i3, t0, t1,
+    d0, d1, d2, d3,
 ):
     scale2 = scale_ref[0] * LOG2E
     col_of, row_of = places(ids_ref)
-    columns = col_shift[...]
-    lanes = lax.broadcasted_iota(jnp.int32, (ROWS, 8 * ROWS), 1)
+    columns = jnp.exp2(-col_shift[...]) if bounded else col_shift[...]
+    lanes = lax.broadcasted_iota(jnp.int32, (1, 8 * ROWS), 1)
     for q, (rows_ref, d_ref) in enumerate(zip((i0, i1, i2, i3), (d0, d1, d2, d3))):
         for h in range(QUAD // CHUNK):
             rows = rows_ref[h * CHUNK : (h + 1) * CHUNK, :]
@@ -235,12 +271,17 @@
             pieces = []
             for b in range(CHUNK // ROWS):
                 place = col_of(q, h * (CHUNK // ROWS) + b)
-                shift = jnp.transpose(jnp.broadcast_to(row_shift[pl.ds(place, 1), :], (ROWS, ROWS)))
+                shift = row_shift[pl.ds(place, 1), :]
+                shift = jnp.exp2(-shift) if bounded else shift
+                shift = jnp.transpose(jnp.broadcast_to(shift, (ROWS, ROWS)))
                 pos = pos_ref[pl.ds(pl.multiple_of(place * ROWS, ROWS), ROWS), :]
                 shift = jnp.concatenate([shift] * 8, axis=1)
                 pos = jnp.concatenate([pos] * 8, axis=1)
                 part = logits[b * ROWS : (b + 1) * ROWS]
-                soft = jnp.exp2(part - shift) + jnp.exp2(part - columns)
+                if bounded:
+                    soft = jnp.exp2(part) * (shift + columns)
+                else:
+                    soft = jnp.exp2(part - shift) + jnp.exp2(part - columns)
                 pieces.append(jnp.where(pos == lanes, soft - 1.0, soft).astype(BF16))
             d_ref[h * CHUNK : (h + 1) * CHUNK, :] = jnp.concatenate(pieces, axis=0)
 
@@ -290,6 +331,10 @@
 
 def across(place, far):
     return 3 - place if far else place ^ 1
+
+
+def pair_b(far):
+    return lambda z, k, x, y: (z, k, across(x, far), y) if k else (z, k, x, across(y, far))
 
 
 def pair_z(far):
@@ -330,16 +375,20 @@
         functools.partial(forward_kernel, True, (2, 1)), [row_shape, shape((16, ROWS), F32)],
         *common, imgs[2], imgs[1], txt0, txt1, *stats, specs=[SMEM, SMEM] + [VMEM] * 7,
     )
-    for row_moves, col_move in ((ring_a, pair_z(False)), (ring_b, pair_z(True))):
-        row_stat, col_stat = call(
-            merge_kernel, [row_shape, shape((16, ROWS), F32)],
-            *gathered(row_stat, row_moves), col_stat, shifted(col_stat, col_move),
-        )
+    col_shape = shape((16, ROWS), F32)
+    row_stat, col_stat = call(
+        merge_kernel, [row_shape, col_shape],
+        *gathered(row_stat, ring_a), col_stat, shifted(col_stat, other_core),
+    )
+    row_stat, col_stat = call(
+        merge_kernel, [row_shape, col_shape],
+        row_stat, shifted(row_stat, pair_b(False)), col_stat, shifted(col_stat, pair_z(False)),
+    )
     tail = shape((EXTRA, WIDTH), BF16)
     row_shift, col_shift, row_tail, col_tail = call(
         shifts_kernel, [shape((16, ROWS), F32), shape((1, 8 * ROWS), F32), tail, tail],
-        ids, row_stat, col_stat, shifted(col_stat, other_core),
-        specs=[SMEM] + [VMEM] * 3, scratch=[pltpu.VMEM((8, ROWS), F32)],
+        ids, row_stat, shifted(row_stat, pair_b(True)), col_stat, shifted(col_stat, pair_z(True)),
+        specs=[SMEM] + [VMEM] * 4, scratch=[pltpu.VMEM((8, ROWS), F32)],
     )
 
     sent = shape((QUAD + EXTRA, WIDTH), BF16)

time: 87.5 us -> 87.6 us (level)
  starting transfers between devices: 41.6 us -> 39.2 us
  waiting for transfers between devices: 21.9 us -> 23.9 us
    ppermute x29 -> x28, starting transfers between devices: 41.6 us -> 39.2 us  [shifted(): return lax.ppermute(value, RC, pairs)]
    ppermute x29 -> x28, waiting for transfers between devices: 21.9 us -> 23.9 us  [shifted(): return lax.ppermute(value, RC, pairs)]
  transfers between devices with their start and end apart: 29 -> 28, of which waited for: 13 -> 15; matrix products, arithmetic and copies ran while one was open for 1% -> 1% of each run, Pallas kernels for 11% -> 11%
where the time goes in v4:
time: 87.6 us; the launch traced here: 87.4 us
  starting transfers between devices  39.2 us (45%)
  waiting for transfers between devices  23.9 us (27%)
  Pallas kernels  21.1 us (24%)
  between operations  1.7 us (2%)
  local copies, waits for them, and re-layouts  1.27 us (1%)
    ppermute x28, starting transfers between devices, shifted(): return lax.ppermute(value, RC, pairs)  39.2 us
    ppermute x28, waiting for transfers between devices, shifted(): return lax.ppermute(value, RC, pairs)  23.9 us
    pallas_call x17, Pallas kernels, call(): pl.pallas_call(kernel, out_shape=outs, in_specs=specs or [VMEM] * len(arg...  20 us
  transfers between devices with their start and end apart: 28, of which 15 were waited for; matrix products, arithmetic and copies ran while one was open for 1% of the time, Pallas kernels for 11%

profile of v4, /device:TPU:0, one launch (start us, length us, event | category | flops | bytes accessed | tf_op | source)
XLA Modules:
  0.0 87.4 jit_solution(12435162917126319478)
XLA Ops:
  0.6 0.0 copy-start.1
  0.7 0.9 %copy-done.1 = bf16[128,512]{1,0:T(8,128)(2,1)S(1)} copy-done((bf16[128,512]{1,0:T(8,128)(2,1)S(1)}, bf16[128,512]{1,0:T(8,128)(2,1)}, u32[]{:S(2)}) %copy-start.1) | copy-done | bytes 131096
  1.6 0.1 shard_map.75.refs_0_
  1.7 3.2 %collective-permute-start.2 = (bf16[128,512]{1,0:T(8,128)(2,1)S(1)}, bf16[128,512]{1,0:T(8,128)(2,1)S(1)}, u32[]{:S(2)}, u32[]{:S(2)}) collective-permute-start(bf16[128,512]{1,0:T(8,128)(2,1)S(1)} %shard_map.75.refs_0_), channel_id=1, source_target_pairs={{0,8},{1,9},{2,10},{3,11},{4,12},{5,13},{6,14},{7,15},{8,0},{9,1},... | collective-permute-start | bytes 393224 | tf_op jit(solution)/shard_map/ppermute | solution.py:37
  4.9 1.1 %collective-permute-start.1 = (bf16[128,512]{1,0:T(8,128)(2,1)S(1)}, bf16[128,512]{1,0:T(8,128)(2,1)S(1)}, u32[]{:S(2)}, u32[]{:S(2)}) collective-permute-start(bf16[128,512]{1,0:T(8,128)(2,1)S(1)} %shard_map.75.refs_0_), channel_id=1, source_target_pairs={{0,12},{1,13},{2,14},{3,15},{4,0},{5,1},{6,2},{7,3},{8,4},{9,5},{1... | collective-permute-start | bytes 393224 | tf_op jit(solution)/shard_map/ppermute | solution.py:37
  6.0 0.9 %collective-permute-start = (bf16[128,512]{1,0:T(8,128)(2,1)S(1)}, bf16[128,512]{1,0:T(8,128)(2,1)S(1)}, u32[]{:S(2)}, u32[]{:S(2)}) collective-permute-start(bf16[128,512]{1,0:T(8,128)(2,1)S(1)} %shard_map.75.refs_0_), channel_id=1, source_target_pairs={{0,4},{1,5},{2,6},{3,7},{4,8},{5,9},{6,10},{7,11},{8,12},{9,13},{1... | collective-permute-start | bytes 393224 | tf_op jit(solution)/shard_map/ppermute | solution.py:37
  6.9 0.1 shard_map.76
  7.0 4.0 %collective-permute-start.7 = (bf16[128,512]{1,0:T(8,128)(2,1)S(1)}, bf16[128,512]{1,0:T(8,128)(2,1)S(1)}, u32[]{:S(2)}, u32[]{:S(2)}) collective-permute-start(bf16[128,512]{1,0:T(8,128)(2,1)S(1)} %shard_map.76), channel_id=1, source_target_pairs={{0,64},{1,65},{2,66},{3,67},{4,68},{5,69},{6,70},{7,71},{8,72},{9,... | collective-permute-start | bytes 393224 | tf_op jit(solution)/shard_map/ppermute | solution.py:37
  11.0 0.7 collective-permute-start.6
  11.7 0.0 collective-permute-done.2
  11.7 1.3 %collective-permute-start.5 = (bf16[128,512]{1,0:T(8,128)(2,1)S(1)}, bf16[128,512]{1,0:T(8,128)(2,1)S(1)}, u32[]{:S(2)}, u32[]{:S(2)}) collective-permute-start(bf16[128,512]{1,0:T(8,128)(2,1)S(1)} %shard_map.76), channel_id=1, source_target_pairs={{0,32},{1,33},{2,34},{3,35},{4,36},{5,37},{6,38},{7,39},{8,40},{9,... | collective-permute-start | bytes 393224 | tf_op jit(solution)/shard_map/ppermute | solution.py:37
  13.0 0.0 collective-permute-done.1
  13.0 0.0 collective-permute-done
  13.1 3.3 %collective-permute-start.9 = (bf16[512,512]{1,0:T(8,128)(2,1)S(1)}, bf16[512,512]{1,0:T(8,128)(2,1)S(1)}, u32[]{:S(2)}, u32[]{:S(2)}) collective-permute-start(bf16[512,512]{1,0:T(8,128)(2,1)S(1)} %pad_maximum_fusion.refs_1_.refs_3_.i0), channel_id=1, source_target_pairs={{0,2},{1,3},{2,0},{3,1},{4,6},{5,7},{6,4},{7,5},{8,10},{9,11},{10,... | collective-permute-start | bytes 1572872 | tf_op jit(solution)/shard_map/ppermute | solution.py:37
  16.3 0.0 collective-permute-done.7
  16.3 1.1 %collective-permute-done.6 = bf16[128,512]{1,0:T(8,128)(2,1)S(1)} collective-permute-done((bf16[128,512]{1,0:T(8,128)(2,1)S(1)}, bf16[128,512]{1,0:T(8,128)(2,1)S(1)}, u32[]{:S(2)}, u32[]{:S(2)}) %collective-permute-start.6) | collective-permute-done | bytes 131104 | tf_op jit(solution)/shard_map/ppermute | solution.py:37
  17.4 0.5 collective-permute-done.5
  17.9 0.1 collective-permute-start.8
  18.0 1.6 %collective-permute-start.4 = (bf16[512,512]{1,0:T(8,128)(2,1)S(1)}, bf16[512,512]{1,0:T(8,128)(2,1)S(1)}, u32[]{:S(2)}, u32[]{:S(2)}) collective-permute-start(bf16[512,512]{1,0:T(8,128)(2,1)S(1)} %pad_maximum_fusion.refs_1_.refs_3_.i0), channel_id=1, source_target_pairs={{0,1},{1,2},{2,3},{3,0},{4,5},{5,6},{6,7},{7,4},{8,9},{9,10},{10,1... | collective-permute-start | bytes 1572872 | tf_op jit(solution)/shard_map/ppermute | solution.py:37
  19.7 1.7 %collective-permute-start.3 = (bf16[512,512]{1,0:T(8,128)(2,1)S(1)}, bf16[512,512]{1,0:T(8,128)(2,1)S(1)}, u32[]{:S(2)}, u32[]{:S(2)}) collective-permute-start(bf16[512,512]{1,0:T(8,128)(2,1)S(1)} %pad_maximum_fusion.refs_1_.refs_3_.i0), channel_id=1, source_target_pairs={{0,3},{1,0},{2,1},{3,2},{4,7},{5,4},{6,5},{7,6},{8,11},{9,8},{10,9... | collective-permute-start | bytes 1572872 | tf_op jit(solution)/shard_map/ppermute | solution.py:37
  22.0 0.1 pad_add_fusion.ids_ref
  22.2 1.8 %collective-permute-done.9.refs_0_.refs_2_.refs_6_.i3 = bf16[512,512]{1,0:T(8,128)(2,1)S(1)} collective-permute-done((bf16[512,512]{1,0:T(8,128)(2,1)S(1)}, bf16[512,512]{1,0:T(8,128)(2,1)S(1)}, u32[]{:S(2)}, u32[]{:S(2)}) %collective-permute-start.9) | collective-permute-done | bytes 524320 | tf_op jit(solution)/shard_map/ppermute | solution.py:37
  23.9 0.3 broadcast_in_dim.8.refs_0_
  24.3 4.0 %shard_map.78 = (f32[40,128]{1,0:T(8,128)S(1)}, f32[8,1024]{1,0:T(8,128)S(1)}) custom-call(s32[2]{0:T(128)S(1)} %pad_add_fusion.ids_ref, f32[1]{0:T(128)S(6)} %exp.3.scale_ref, s32[2048,128]{1,0:T(8,128)S(1)} %broadcast_in_dim.8.refs_0_, bf16[512,512]{1,0:T(8,128)(2,1)S(1)} %pad_maximum_fusion.refs_1_.refs_3_.i0, ...), custom_call_target="tpu_custom_call" | custom-call | tf_op jit(solution)/shard_map/pallas_call | solution.py:57
  28.3 1.2 %collective-permute-done.4.refs_2_.refs_4_.i1 = bf16[512,512]{1,0:T(8,128)(2,1)S(1)} collective-permute-done((bf16[512,512]{1,0:T(8,128)(2,1)S(1)}, bf16[512,512]{1,0:T(8,128)(2,1)S(1)}, u32[]{:S(2)}, u32[]{:S(2)}) %collective-permute-start.4) | collective-permute-done | bytes 524320 | tf_op jit(solution)/shard_map/ppermute | solution.py:37
  29.4 0.3 collective-permute-done.3.refs_1_.refs_5_.i2
  29.8 4.3 %shard_map.79 = (f32[40,128]{1,0:T(8,128)S(1)}, f32[16,128]{1,0:T(8,128)S(1)}) custom-call(s32[2]{0:T(128)S(1)} %pad_add_fusion.ids_ref, f32[1]{0:T(128)S(6)} %exp.3.scale_ref, s32[2048,128]{1,0:T(8,128)S(1)} %broadcast_in_dim.8.refs_0_, bf16[512,512]{1,0:T(8,128)(2,1)S(1)} %collective-permute-done.3.refs_1_.refs_5_.i2, ...), custom_call_target="tpu_custom_call" | custom-call | tf_op jit(solution)/shard_map/pallas_call | solution.py:57
  34.1 0.8 collective-permute-start.12
  34.9 2.5 %collective-permute-start.11 = (f32[40,128]{1,0:T(8,128)S(1)}, f32[40,128]{1,0:T(8,128)S(1)}, u32[]{:S(2)}, u32[]{:S(2)}) collective-permute-start(f32[40,128]{1,0:T(8,128)S(1)} %get-tuple-element.30.refs_0_), channel_id=1, source_target_pairs={{0,12},{1,13},{2,14},{3,15},{4,0},{5,1},{6,2},{7,3},{8,4},{9,5},{1... | collective-permute-start | bytes 61448 | tf_op jit(solution)/shard_map/ppermute | solution.py:37
  37.4 1.2 %collective-permute-done.13.refs_5_ = f32[16,128]{1,0:T(8,128)S(1)} collective-permute-done((f32[16,128]{1,0:T(8,128)S(1)}, f32[16,128]{1,0:T(8,128)S(1)}, u32[]{:S(2)}, u32[]{:S(2)}) %collective-permute-start.13) | collective-permute-done | bytes 8224 | tf_op jit(solution)/shard_map/ppermute | solution.py:37
  38.6 0.8 collective-permute-done.12.refs_3_
  39.5 3.0 %collective-permute-done.10.refs_1_ = f32[40,128]{1,0:T(8,128)S(1)} collective-permute-done((f32[40,128]{1,0:T(8,128)S(1)}, f32[40,128]{1,0:T(8,128)S(1)}, u32[]{:S(2)}, u32[]{:S(2)}) %collective-permute-start.10) | collective-permute-done | bytes 20512 | tf_op jit(solution)/shard_map/ppermute | solution.py:37
  42.5 1.5 %collective-permute-start.14 = (f32[40,128]{1,0:T(8,128)S(1)}, f32[40,128]{1,0:T(8,128)S(1)}, u32[]{:S(2)}, u32[]{:S(2)}) collective-permute-start(f32[40,128]{1,0:T(8,128)S(1)} %get-tuple-element.32.refs_0_), channel_id=1, source_target_pairs={{0,1},{1,0},{2,3},{3,2},{4,5},{5,4},{6,7},{7,6},{8,9},{9,8},{10,11... | collective-permute-start | bytes 61448 | tf_op jit(solution)/shard_map/ppermute | solution.py:37
  43.9 1.0 %collective-permute-start.15 = (f32[16,128]{1,0:T(8,128)S(1)}, f32[16,128]{1,0:T(8,128)S(1)}, u32[]{:S(2)}, u32[]{:S(2)}) collective-permute-start(f32[16,128]{1,0:T(8,128)S(1)} %get-tuple-element.33.refs_2_), channel_id=1, source_target_pairs={{0,32},{1,33},{2,34},{3,35},{4,36},{5,37},{6,38},{7,39},{8,40},{9,... | collective-permute-start | bytes 24584 | tf_op jit(solution)/shard_map/ppermute | solution.py:37
  45.0 2.6 %collective-permute-done.15.refs_3_ = f32[16,128]{1,0:T(8,128)S(1)} collective-permute-done((f32[16,128]{1,0:T(8,128)S(1)}, f32[16,128]{1,0:T(8,128)S(1)}, u32[]{:S(2)}, u32[]{:S(2)}) %collective-permute-start.15) | collective-permute-done | bytes 8224 | tf_op jit(solution)/shard_map/ppermute | solution.py:37
  47.6 2.1 %collective-permute-start.16 = (f32[40,128]{1,0:T(8,128)S(1)}, f32[40,128]{1,0:T(8,128)S(1)}, u32[]{:S(2)}, u32[]{:S(2)}) collective-permute-start(f32[40,128]{1,0:T(8,128)S(1)} %get-tuple-element.34.r0), channel_id=1, source_target_pairs={{0,3},{1,2},{2,1},{3,0},{4,7},{5,6},{6,5},{7,4},{8,11},{9,10},{10,... | collective-permute-start | bytes 61448 | tf_op jit(solution)/shard_map/ppermute | solution.py:37
  49.7 2.3 %collective-permute-start.17 = (f32[16,128]{1,0:T(8,128)S(1)}, f32[16,128]{1,0:T(8,128)S(1)}, u32[]{:S(2)}, u32[]{:S(2)}) collective-permute-start(f32[16,128]{1,0:T(8,128)S(1)} %get-tuple-element.35.c0), channel_id=1, source_target_pairs={{0,96},{1,97},{2,98},{3,99},{4,100},{5,101},{6,102},{7,103},{8,104... | collective-permute-start | bytes 24584 | tf_op jit(solution)/shard_map/ppermute | solution.py:37
  52.0 2.6 %collective-permute-done.17.c1 = f32[16,128]{1,0:T(8,128)S(1)} collective-permute-done((f32[16,128]{1,0:T(8,128)S(1)}, f32[16,128]{1,0:T(8,128)S(1)}, u32[]{:S(2)}, u32[]{:S(2)}) %collective-permute-start.17) | collective-permute-done | bytes 8224 | tf_op jit(solution)/shard_map/ppermute | solution.py:37
  54.6 0.7 shard_map.82
  55.3 4.2 %shard_map.83 = (bf16[512,1024]{1,0:T(8,128)(2,1)S(1)}, bf16[512,1024]{1,0:T(8,128)(2,1)S(1)}, bf16[512,1024]{1,0:T(8,128)(2,1)S(1)}, bf16[512,1024]{1,0:T(8,128)(2,1)S(1)}) custom-call(s32[2]{0:T(128)S(1)} %pad_add_fusion.ids_ref, f32[1]{0:T(128)S(6)} %exp.3.scale_ref, s32[2048,128]{1,0:T(8,128)S(1)} %broadcast_in_dim.8.refs_0_, ...), custom_call_target="tpu_custom_call" | custom-call | flops 10000000000 | bytes 1000000 | tf_op jit(solution)/shard_map/pallas_call | solution.py:57
  59.6 0.7 shard_map.86.refs_2_
  60.3 0.9 %collective-permute-start.21 = (bf16[528,512]{1,0:T(8,128)(2,1)S(1)}, bf16[528,512]{1,0:T(8,128)(2,1)S(1)}, u32[]{:S(2)}, u32[]{:S(2)}) collective-permute-start(bf16[528,512]{1,0:T(8,128)(2,1)S(1)} %shard_map.86.refs_2_), channel_id=1, source_target_pairs={{0,2},{1,3},{2,0},{3,1},{4,6},{5,7},{6,4},{7,5},{8,10},{9,11},{10,... | collective-permute-start | bytes 1622024 | tf_op jit(solution)/shard_map/ppermute | solution.py:37
  61.2 0.7 shard_map.85.refs_1_
  61.9 1.3 %collective-permute-start.20 = (bf16[528,512]{1,0:T(8,128)(2,1)S(1)}, bf16[528,512]{1,0:T(8,128)(2,1)S(1)}, u32[]{:S(2)}, u32[]{:S(2)}) collective-permute-start(bf16[528,512]{1,0:T(8,128)(2,1)S(1)} %shard_map.85.refs_1_), channel_id=1, source_target_pairs={{0,1},{1,2},{2,3},{3,0},{4,5},{5,6},{6,7},{7,4},{8,9},{9,10},{10,1... | collective-permute-start | bytes 1622024 | tf_op jit(solution)/shard_map/ppermute | solution.py:37
  63.2 0.7 shard_map.84.refs_0_
  63.9 2.0 %collective-permute-start.19 = (bf16[528,512]{1,0:T(8,128)(2,1)S(1)}, bf16[528,512]{1,0:T(8,128)(2,1)S(1)}, u32[]{:S(2)}, u32[]{:S(2)}) collective-permute-start(bf16[528,512]{1,0:T(8,128)(2,1)S(1)} %shard_map.84.refs_0_), channel_id=1, source_target_pairs={{0,3},{1,0},{2,1},{3,2},{4,7},{5,4},{6,5},{7,6},{8,11},{9,8},{10,9... | collective-permute-start | bytes 1622024 | tf_op jit(solution)/shard_map/ppermute | solution.py:37
  66.0 1.5 %shard_map.87.refs_0_ = bf16[528,512]{1,0:T(8,128)(2,1)S(1)} custom-call(f32[1]{0:T(128)S(6)} %exp.3.scale_ref, bf16[16,512]{1,0:T(8,128)(2,1)S(1)} %get-tuple-element.36.row_tail, bf16[512,512]{1,0:T(8,128)(2,1)S(1)} %pad_maximum_fusion.refs_1_.refs_3_.i0, bf16[512,512]{1,0:T(8,128)(2,1)S(1)} %collective-permute-done.4.refs_2_.refs_4_.i1, ...), custom_call_target="tpu_custom_call" | custom-call | flops 10000000000 | bytes 1000000 | tf_op jit(solution)/shard_map/pallas_call | solution.py:57
  67.5 0.1 collective-permute-start.18
  67.6 1.5 %shard_map.88.refs_0_ = bf16[528,512]{1,0:T(8,128)(2,1)S(1)} custom-call(f32[1]{0:T(128)S(6)} %exp.3.scale_ref, bf16[16,512]{1,0:T(8,128)(2,1)S(1)} %get-tuple-element.36.row_tail, bf16[512,512]{1,0:T(8,128)(2,1)S(1)} %pad_maximum_fusion.refs_1_.refs_3_.i0, bf16[512,512]{1,0:T(8,128)(2,1)S(1)} %collective-permute-done.4.refs_2_.refs_4_.i1, ...), custom_call_target="tpu_custom_call" | custom-call | flops 10000000000 | bytes 1000000 | tf_op jit(solution)/shard_map/pallas_call | solution.py:57
  69.1 0.4 collective-permute-done.18.refs_1_
  69.5 0.2 shard_map.89
  69.7 2.4 %collective-permute-start.25 = (bf16[144,512]{1,0:T(8,128)(2,1)S(1)}, bf16[144,512]{1,0:T(8,128)(2,1)S(1)}, u32[]{:S(2)}, u32[]{:S(2)}) collective-permute-start(bf16[144,512]{1,0:T(8,128)(2,1)S(1)} %get-tuple-element.49), channel_id=1, source_target_pairs={{0,96},{1,97},{2,98},{3,99},{4,100},{5,101},{6,102},{7,103},{8,104... | collective-permute-start | bytes 442376 | tf_op jit(solution)/shard_map/ppermute | solution.py:37
  72.1 0.7 shard_map.90.refs_0_
  72.8 0.1 collective-permute-start.26
  72.9 1.5 %collective-permute-start.27 = (bf16[144,512]{1,0:T(8,128)(2,1)S(1)}, bf16[144,512]{1,0:T(8,128)(2,1)S(1)}, u32[]{:S(2)}, u32[]{:S(2)}) collective-permute-start(bf16[144,512]{1,0:T(8,128)(2,1)S(1)} %get-tuple-element.51), channel_id=1, source_target_pairs={{0,64},{1,65},{2,66},{3,67},{4,68},{5,69},{6,70},{7,71},{8,72},{9,... | collective-permute-start | bytes 442376 | tf_op jit(solution)/shard_map/ppermute | solution.py:37
  74.3 2.7 %collective-permute-done.20.refs_2_ = bf16[528,512]{1,0:T(8,128)(2,1)S(1)} collective-permute-done((bf16[528,512]{1,0:T(8,128)(2,1)S(1)}, bf16[528,512]{1,0:T(8,128)(2,1)S(1)}, u32[]{:S(2)}, u32[]{:S(2)}) %collective-permute-start.20) | collective-permute-done | bytes 540704 | tf_op jit(solution)/shard_map/ppermute | solution.py:37
  77.0 0.4 shard_map.91
  77.4 0.1 collective-permute-start.22
  77.5 2.0 %collective-permute-start.23 = (bf16[144,512]{1,0:T(8,128)(2,1)S(1)}, bf16[144,512]{1,0:T(8,128)(2,1)S(1)}, u32[]{:S(2)}, u32[]{:S(2)}) collective-permute-start(bf16[144,512]{1,0:T(8,128)(2,1)S(1)} %get-tuple-element.47), channel_id=1, source_target_pairs={{0,4},{1,5},{2,6},{3,7},{4,8},{5,9},{6,10},{7,11},{8,12},{9,13},{1... | collective-permute-start | bytes 442376 | tf_op jit(solution)/shard_map/ppermute | solution.py:37
  79.5 0.8 collective-permute-start.24
  80.3 2.6 %collective-permute-done.26.b2 = bf16[144,512]{1,0:T(8,128)(2,1)S(1)} collective-permute-done((bf16[144,512]{1,0:T(8,128)(2,1)S(1)}, bf16[144,512]{1,0:T(8,128)(2,1)S(1)}, u32[]{:S(2)}, u32[]{:S(2)}) %collective-permute-start.26) | collective-permute-done | bytes 147488 | tf_op jit(solution)/shard_map/ppermute | solution.py:37
  82.8 1.0 %collective-permute-done.23.a2 = bf16[144,512]{1,0:T(8,128)(2,1)S(1)} collective-permute-done((bf16[144,512]{1,0:T(8,128)(2,1)S(1)}, bf16[144,512]{1,0:T(8,128)(2,1)S(1)}, u32[]{:S(2)}, u32[]{:S(2)}) %collective-permute-start.23) | collective-permute-done | bytes 147488 | tf_op jit(solution)/shard_map/ppermute | solution.py:37
  83.9 2.2 %collective-permute-done.24.a3 = bf16[144,512]{1,0:T(8,128)(2,1)S(1)} collective-permute-done((bf16[144,512]{1,0:T(8,128)(2,1)S(1)}, bf16[144,512]{1,0:T(8,128)(2,1)S(1)}, u32[]{:S(2)}, u32[]{:S(2)}) %collective-permute-start.24) | collective-permute-done | bytes 147488 | tf_op jit(solution)/shard_map/ppermute | solution.py:37
  86.1 1.1 %shard_map.92 = (f32[128,512]{1,0:T(8,128)}, f32[128,512]{1,0:T(8,128)}, f32[1]{0:T(128)}, f32[1]{0:T(128)}) custom-call(bf16[128,512]{1,0:T(8,128)(2,1)S(1)} %copy-done.2, bf16[128,512]{1,0:T(8,128)(2,1)S(1)} %copy-done, bf16[144,512]{1,0:T(8,128)(2,1)S(1)} %get-tuple-element.45.a0, bf16[144,512]{1,0:T(8,128)(2,1)S(1)} %collective-permute-done.22.a1, ...), custom_call_target="tpu_custom_call" | custom-call | tf_op jit(solution)/shard_map/pallas_call | solution.py:424
  (23 shorter events, 0.2 us)
Async XLA Ops:
  0.6 6.3 %copy-start = (bf16[128,512]{1,0:T(8,128)(2,1)S(1)}, bf16[128,512]{1,0:T(8,128)(2,1)}, u32[]{:S(2)}) copy-start(bf16[128,512]{1,0:T(8,128)(2,1)} %txt_ref.1) | copy-start | bytes 393220
  0.6 0.9 %copy-start.1 = (bf16[128,512]{1,0:T(8,128)(2,1)S(1)}, bf16[128,512]{1,0:T(8,128)(2,1)}, u32[]{:S(2)}) copy-start(bf16[128,512]{1,0:T(8,128)(2,1)} %img_ref.1) | copy-start | bytes 393220
  1.7 10.0 %collective-permute-start.2 = (bf16[128,512]{1,0:T(8,128)(2,1)S(1)}, bf16[128,512]{1,0:T(8,128)(2,1)S(1)}, u32[]{:S(2)}, u32[]{:S(2)}) collective-permute-start(bf16[128,512]{1,0:T(8,128)(2,1)S(1)} %shard_map.75.refs_0_), channel_id=1, source_target_pairs={{0,8},{1,9},{2,10},{3,11},{4,12},{5,13},{6,14},{7,15},{8,0},{9,1},... | collective-permute-start | bytes 393224 | tf_op jit(solution)/shard_map/ppermute | solution.py:37
  4.9 8.1 %collective-permute-start.1 = (bf16[128,512]{1,0:T(8,128)(2,1)S(1)}, bf16[128,512]{1,0:T(8,128)(2,1)S(1)}, u32[]{:S(2)}, u32[]{:S(2)}) collective-permute-start(bf16[128,512]{1,0:T(8,128)(2,1)S(1)} %shard_map.75.refs_0_), channel_id=1, source_target_pairs={{0,12},{1,13},{2,14},{3,15},{4,0},{5,1},{6,2},{7,3},{8,4},{9,5},{1... | collective-permute-start | bytes 393224 | tf_op jit(solution)/shard_map/ppermute | solution.py:37
  6.0 7.0 %collective-permute-start = (bf16[128,512]{1,0:T(8,128)(2,1)S(1)}, bf16[128,512]{1,0:T(8,128)(2,1)S(1)}, u32[]{:S(2)}, u32[]{:S(2)}) collective-permute-start(bf16[128,512]{1,0:T(8,128)(2,1)S(1)} %shard_map.75.refs_0_), channel_id=1, source_target_pairs={{0,4},{1,5},{2,6},{3,7},{4,8},{5,9},{6,10},{7,11},{8,12},{9,13},{1... | collective-permute-start | bytes 393224 | tf_op jit(solution)/shard_map/ppermute | solution.py:37
  7.0 9.3 %collective-permute-start.7 = (bf16[128,512]{1,0:T(8,128)(2,1)S(1)}, bf16[128,512]{1,0:T(8,128)(2,1)S(1)}, u32[]{:S(2)}, u32[]{:S(2)}) collective-permute-start(bf16[128,512]{1,0:T(8,128)(2,1)S(1)} %shard_map.76), channel_id=1, source_target_pairs={{0,64},{1,65},{2,66},{3,67},{4,68},{5,69},{6,70},{7,71},{8,72},{9,... | collective-permute-start | bytes 393224 | tf_op jit(solution)/shard_map/ppermute | solution.py:37
  11.0 6.4 %collective-permute-start.6 = (bf16[128,512]{1,0:T(8,128)(2,1)S(1)}, bf16[128,512]{1,0:T(8,128)(2,1)S(1)}, u32[]{:S(2)}, u32[]{:S(2)}) collective-permute-start(bf16[128,512]{1,0:T(8,128)(2,1)S(1)} %shard_map.76), channel_id=1, source_target_pairs={{0,96},{1,97},{2,98},{3,99},{4,100},{5,101},{6,102},{7,103},{8,104... | collective-permute-start | bytes 393224 | tf_op jit(solution)/shard_map/ppermute | solution.py:37
  11.7 6.2 %collective-permute-start.5 = (bf16[128,512]{1,0:T(8,128)(2,1)S(1)}, bf16[128,512]{1,0:T(8,128)(2,1)S(1)}, u32[]{:S(2)}, u32[]{:S(2)}) collective-permute-start(bf16[128,512]{1,0:T(8,128)(2,1)S(1)} %shard_map.76), channel_id=1, source_target_pairs={{0,32},{1,33},{2,34},{3,35},{4,36},{5,37},{6,38},{7,39},{8,40},{9,... | collective-permute-start | bytes 393224 | tf_op jit(solution)/shard_map/ppermute | solution.py:37
  13.1 10.9 %collective-permute-start.9 = (bf16[512,512]{1,0:T(8,128)(2,1)S(1)}, bf16[512,512]{1,0:T(8,128)(2,1)S(1)}, u32[]{:S(2)}, u32[]{:S(2)}) collective-permute-start(bf16[512,512]{1,0:T(8,128)(2,1)S(1)} %pad_maximum_fusion.refs_1_.refs_3_.i0), channel_id=1, source_target_pairs={{0,2},{1,3},{2,0},{3,1},{4,6},{5,7},{6,4},{7,5},{8,10},{9,11},{10,... | collective-permute-start | bytes 1572872 | tf_op jit(solution)/shard_map/ppermute | solution.py:37
  17.9 6.0 %collective-permute-start.8 = (bf16[512,512]{1,0:T(8,128)(2,1)S(1)}, bf16[512,512]{1,0:T(8,128)(2,1)S(1)}, u32[]{:S(2)}, u32[]{:S(2)}) collective-permute-start(bf16[512,512]{1,0:T(8,128)(2,1)S(1)} %pad_maximum_fusion.1.refs_3_.refs_7_.t0), channel_id=1, source_target_pairs={{0,16},{1,17},{2,18},{3,19},{4,20},{5,21},{6,22},{7,23},{8,24},{9,... | collective-permute-start | bytes 1572872 | tf_op jit(solution)/shard_map/ppermute | solution.py:37
  18.0 11.4 %collective-permute-start.4 = (bf16[512,512]{1,0:T(8,128)(2,1)S(1)}, bf16[512,512]{1,0:T(8,128)(2,1)S(1)}, u32[]{:S(2)}, u32[]{:S(2)}) collective-permute-start(bf16[512,512]{1,0:T(8,128)(2,1)S(1)} %pad_maximum_fusion.refs_1_.refs_3_.i0), channel_id=1, source_target_pairs={{0,1},{1,2},{2,3},{3,0},{4,5},{5,6},{6,7},{7,4},{8,9},{9,10},{10,1... | collective-permute-start | bytes 1572872 | tf_op jit(solution)/shard_map/ppermute | solution.py:37
  19.7 10.1 %collective-permute-start.3 = (bf16[512,512]{1,0:T(8,128)(2,1)S(1)}, bf16[512,512]{1,0:T(8,128)(2,1)S(1)}, u32[]{:S(2)}, u32[]{:S(2)}) collective-permute-start(bf16[512,512]{1,0:T(8,128)(2,1)S(1)} %pad_maximum_fusion.refs_1_.refs_3_.i0), channel_id=1, source_target_pairs={{0,3},{1,0},{2,1},{3,2},{4,7},{5,4},{6,5},{7,6},{8,11},{9,8},{10,9... | collective-permute-start | bytes 1572872 | tf_op jit(solution)/shard_map/ppermute | solution.py:37
  21.3 0.8 copy-start.3
  34.1 5.3 %collective-permute-start.12 = (f32[40,128]{1,0:T(8,128)S(1)}, f32[40,128]{1,0:T(8,128)S(1)}, u32[]{:S(2)}, u32[]{:S(2)}) collective-permute-start(f32[40,128]{1,0:T(8,128)S(1)} %get-tuple-element.30.refs_0_), channel_id=1, source_target_pairs={{0,8},{1,9},{2,10},{3,11},{4,12},{5,13},{6,14},{7,15},{8,0},{9,1},... | collective-permute-start | bytes 61448 | tf_op jit(solution)/shard_map/ppermute | solution.py:37
  34.9 4.5 %collective-permute-start.11 = (f32[40,128]{1,0:T(8,128)S(1)}, f32[40,128]{1,0:T(8,128)S(1)}, u32[]{:S(2)}, u32[]{:S(2)}) collective-permute-start(f32[40,128]{1,0:T(8,128)S(1)} %get-tuple-element.30.refs_0_), channel_id=1, source_target_pairs={{0,12},{1,13},{2,14},{3,15},{4,0},{5,1},{6,2},{7,3},{8,4},{9,5},{1... | collective-permute-start | bytes 61448 | tf_op jit(solution)/shard_map/ppermute | solution.py:37
  37.4 5.0 %collective-permute-start.10 = (f32[40,128]{1,0:T(8,128)S(1)}, f32[40,128]{1,0:T(8,128)S(1)}, u32[]{:S(2)}, u32[]{:S(2)}) collective-permute-start(f32[40,128]{1,0:T(8,128)S(1)} %get-tuple-element.30.refs_0_), channel_id=1, source_target_pairs={{0,4},{1,5},{2,6},{3,7},{4,8},{5,9},{6,10},{7,11},{8,12},{9,13},{1... | collective-permute-start | bytes 61448 | tf_op jit(solution)/shard_map/ppermute | solution.py:37
  37.4 1.2 %collective-permute-start.13 = (f32[16,128]{1,0:T(8,128)S(1)}, f32[16,128]{1,0:T(8,128)S(1)}, u32[]{:S(2)}, u32[]{:S(2)}) collective-permute-start(f32[16,128]{1,0:T(8,128)S(1)} %get-tuple-element.31.refs_4_), channel_id=1, source_target_pairs={{0,16},{1,17},{2,18},{3,19},{4,20},{5,21},{6,22},{7,23},{8,24},{9,... | collective-permute-start | bytes 24584 | tf_op jit(solution)/shard_map/ppermute | solution.py:37
  42.5 5.1 %collective-permute-start.14 = (f32[40,128]{1,0:T(8,128)S(1)}, f32[40,128]{1,0:T(8,128)S(1)}, u32[]{:S(2)}, u32[]{:S(2)}) collective-permute-start(f32[40,128]{1,0:T(8,128)S(1)} %get-tuple-element.32.refs_0_), channel_id=1, source_target_pairs={{0,1},{1,0},{2,3},{3,2},{4,5},{5,4},{6,7},{7,6},{8,9},{9,8},{10,11... | collective-permute-start | bytes 61448 | tf_op jit(solution)/shard_map/ppermute | solution.py:37
  43.9 3.7 %collective-permute-start.15 = (f32[16,128]{1,0:T(8,128)S(1)}, f32[16,128]{1,0:T(8,128)S(1)}, u32[]{:S(2)}, u32[]{:S(2)}) collective-permute-start(f32[16,128]{1,0:T(8,128)S(1)} %get-tuple-element.33.refs_2_), channel_id=1, source_target_pairs={{0,32},{1,33},{2,34},{3,35},{4,36},{5,37},{6,38},{7,39},{8,40},{9,... | collective-permute-start | bytes 24584 | tf_op jit(solution)/shard_map/ppermute | solution.py:37
  47.6 7.0 %collective-permute-start.16 = (f32[40,128]{1,0:T(8,128)S(1)}, f32[40,128]{1,0:T(8,128)S(1)}, u32[]{:S(2)}, u32[]{:S(2)}) collective-permute-start(f32[40,128]{1,0:T(8,128)S(1)} %get-tuple-element.34.r0), channel_id=1, source_target_pairs={{0,3},{1,2},{2,1},{3,0},{4,7},{5,6},{6,5},{7,4},{8,11},{9,10},{10,... | collective-permute-start | bytes 61448 | tf_op jit(solution)/shard_map/ppermute | solution.py:37
  49.7 4.9 %collective-permute-start.17 = (f32[16,128]{1,0:T(8,128)S(1)}, f32[16,128]{1,0:T(8,128)S(1)}, u32[]{:S(2)}, u32[]{:S(2)}) collective-permute-start(f32[16,128]{1,0:T(8,128)S(1)} %get-tuple-element.35.c0), channel_id=1, source_target_pairs={{0,96},{1,97},{2,98},{3,99},{4,100},{5,101},{6,102},{7,103},{8,104... | collective-permute-start | bytes 24584 | tf_op jit(solution)/shard_map/ppermute | solution.py:37
  60.3 12.6 %collective-permute-start.21 = (bf16[528,512]{1,0:T(8,128)(2,1)S(1)}, bf16[528,512]{1,0:T(8,128)(2,1)S(1)}, u32[]{:S(2)}, u32[]{:S(2)}) collective-permute-start(bf16[528,512]{1,0:T(8,128)(2,1)S(1)} %shard_map.86.refs_2_), channel_id=1, source_target_pairs={{0,2},{1,3},{2,0},{3,1},{4,6},{5,7},{6,4},{7,5},{8,10},{9,11},{10,... | collective-permute-start | bytes 1622024 | tf_op jit(solution)/shard_map/ppermute | solution.py:37
  61.9 15.1 %collective-permute-start.20 = (bf16[528,512]{1,0:T(8,128)(2,1)S(1)}, bf16[528,512]{1,0:T(8,128)(2,1)S(1)}, u32[]{:S(2)}, u32[]{:S(2)}) collective-permute-start(bf16[528,512]{1,0:T(8,128)(2,1)S(1)} %shard_map.85.refs_1_), channel_id=1, source_target_pairs={{0,1},{1,2},{2,3},{3,0},{4,5},{5,6},{6,7},{7,4},{8,9},{9,10},{10,1... | collective-permute-start | bytes 1622024 | tf_op jit(solution)/shard_map/ppermute | solution.py:37
  63.9 13.1 %collective-permute-start.19 = (bf16[528,512]{1,0:T(8,128)(2,1)S(1)}, bf16[528,512]{1,0:T(8,128)(2,1)S(1)}, u32[]{:S(2)}, u32[]{:S(2)}) collective-permute-start(bf16[528,512]{1,0:T(8,128)(2,1)S(1)} %shard_map.84.refs_0_), channel_id=1, source_target_pairs={{0,3},{1,0},{2,1},{3,2},{4,7},{5,4},{6,5},{7,6},{8,11},{9,8},{10,9... | collective-permute-start | bytes 1622024 | tf_op jit(solution)/shard_map/ppermute | solution.py:37
  67.5 2.0 %collective-permute-start.18 = (bf16[528,512]{1,0:T(8,128)(2,1)S(1)}, bf16[528,512]{1,0:T(8,128)(2,1)S(1)}, u32[]{:S(2)}, u32[]{:S(2)}) collective-permute-start(bf16[528,512]{1,0:T(8,128)(2,1)S(1)} %shard_map.87.refs_0_), channel_id=1, source_target_pairs={{0,16},{1,17},{2,18},{3,19},{4,20},{5,21},{6,22},{7,23},{8,24},{9,... | collective-permute-start | bytes 1622024 | tf_op jit(solution)/shard_map/ppermute | solution.py:37
  69.7 9.8 %collective-permute-start.25 = (bf16[144,512]{1,0:T(8,128)(2,1)S(1)}, bf16[144,512]{1,0:T(8,128)(2,1)S(1)}, u32[]{:S(2)}, u32[]{:S(2)}) collective-permute-start(bf16[144,512]{1,0:T(8,128)(2,1)S(1)} %get-tuple-element.49), channel_id=1, source_target_pairs={{0,96},{1,97},{2,98},{3,99},{4,100},{5,101},{6,102},{7,103},{8,104... | collective-permute-start | bytes 442376 | tf_op jit(solution)/shard_map/ppermute | solution.py:37
  72.8 10.1 %collective-permute-start.26 = (bf16[144,512]{1,0:T(8,128)(2,1)S(1)}, bf16[144,512]{1,0:T(8,128)(2,1)S(1)}, u32[]{:S(2)}, u32[]{:S(2)}) collective-permute-start(bf16[144,512]{1,0:T(8,128)(2,1)S(1)} %get-tuple-element.50), channel_id=1, source_target_pairs={{0,32},{1,33},{2,34},{3,35},{4,36},{5,37},{6,38},{7,39},{8,40},{9,... | collective-permute-start | bytes 442376 | tf_op jit(solution)/shard_map/ppermute | solution.py:37
  72.9 10.0 %collective-permute-start.27 = (bf16[144,512]{1,0:T(8,128)(2,1)S(1)}, bf16[144,512]{1,0:T(8,128)(2,1)S(1)}, u32[]{:S(2)}, u32[]{:S(2)}) collective-permute-start(bf16[144,512]{1,0:T(8,128)(2,1)S(1)} %get-tuple-element.51), channel_id=1, source_target_pairs={{0,64},{1,65},{2,66},{3,67},{4,68},{5,69},{6,70},{7,71},{8,72},{9,... | collective-permute-start | bytes 442376 | tf_op jit(solution)/shard_map/ppermute | solution.py:37
  77.0 9.1 %copy-start.2 = (bf16[128,512]{1,0:T(8,128)(2,1)S(1)}, bf16[128,512]{1,0:T(8,128)(2,1)}, u32[]{:S(2)}) copy-start(bf16[128,512]{1,0:T(8,128)(2,1)} %img_ref.1) | copy-start | bytes 393220
  77.4 5.5 %collective-permute-start.22 = (bf16[144,512]{1,0:T(8,128)(2,1)S(1)}, bf16[144,512]{1,0:T(8,128)(2,1)S(1)}, u32[]{:S(2)}, u32[]{:S(2)}) collective-permute-start(bf16[144,512]{1,0:T(8,128)(2,1)S(1)} %get-tuple-element.46), channel_id=1, source_target_pairs={{0,12},{1,13},{2,14},{3,15},{4,0},{5,1},{6,2},{7,3},{8,4},{9,5},{1... | collective-permute-start | bytes 442376 | tf_op jit(solution)/shard_map/ppermute | solution.py:37
  77.5 6.4 %collective-permute-start.23 = (bf16[144,512]{1,0:T(8,128)(2,1)S(1)}, bf16[144,512]{1,0:T(8,128)(2,1)S(1)}, u32[]{:S(2)}, u32[]{:S(2)}) collective-permute-start(bf16[144,512]{1,0:T(8,128)(2,1)S(1)} %get-tuple-element.47), channel_id=1, source_target_pairs={{0,4},{1,5},{2,6},{3,7},{4,8},{5,9},{6,10},{7,11},{8,12},{9,13},{1... | collective-permute-start | bytes 442376 | tf_op jit(solution)/shard_map/ppermute | solution.py:37
  79.5 6.6 %collective-permute-start.24 = (bf16[144,512]{1,0:T(8,128)(2,1)S(1)}, bf16[144,512]{1,0:T(8,128)(2,1)S(1)}, u32[]{:S(2)}, u32[]{:S(2)}) collective-permute-start(bf16[144,512]{1,0:T(8,128)(2,1)S(1)} %get-tuple-element.48), channel_id=1, source_target_pairs={{0,8},{1,9},{2,10},{3,11},{4,12},{5,13},{6,14},{7,15},{8,0},{9,1},... | collective-permute-start | bytes 442376 | tf_op jit(solution)/shard_map/ppermute | solution.py:37

commit v5 on v4

--- a/solution.py
+++ b/solution.py
@@ -20,7 +20,7 @@
 VMEM = pl.BlockSpec(memory_space=pltpu.VMEM)
 SMEM = pl.BlockSpec(memory_space=pltpu.SMEM)
 BUSY = pl.CostEstimate(flops=10**10, bytes_accessed=10**6, transcendentals=0)
-PARAMS = pltpu.CompilerParams(vmem_limit_bytes=24 * 1024 * 1024)
+PARAMS = pltpu.CompilerParams(vmem_limit_bytes=12 * 1024 * 1024)
 
 
 def device(z, k, x, y):
@@ -137,22 +137,24 @@
     col_of, row_of = places(ids_ref)
     lanes = lax.broadcasted_iota(jnp.int32, (1, 8 * ROWS), 1)
     if last:
-        row_in, state_in, row_out, col_out = refs
+        row_in, state_in, row_out, col_out, *kept = refs
         row_out[...] = row_in[...]
         col_high, col_total, col_weighted, picked = (state_in[i : i + 1, :] for i in range(4))
     else:
-        _, row_out, state_out = refs
+        _, row_out, state_out, *kept = refs
         col_high = jnp.full((1, 8 * ROWS), 0.0 if bounded else -jnp.inf, F32)
         col_total = col_weighted = picked = jnp.zeros((1, 8 * ROWS), F32)
-    for q, rows_ref in zip(places_of, (i0, i1)):
+    for q, rows_ref, kept_ref in zip(places_of, (i0, i1), kept):
         for h in range(QUAD // CHUNK):
             logits = logits2(rows_ref[h * CHUNK : (h + 1) * CHUNK, :], t0, t1, scale2)
             if bounded:
                 weights = jnp.exp2(logits)
+                kept_ref[h * CHUNK : (h + 1) * CHUNK, :] = weights
                 weighted = weights * logits
                 col_total += jnp.sum(weights, axis=0, keepdims=True)
                 col_weighted += jnp.sum(weighted, axis=0, keepdims=True)
             else:
+                kept_ref[h * CHUNK : (h + 1) * CHUNK, :] = logits
                 high = jnp.max(logits, axis=1, keepdims=True)
                 weights = jnp.exp2(logits - high)
                 total = jnp.sum(weights, axis=1, keepdims=True)
@@ -252,22 +254,18 @@
     g_ref[QUAD : QUAD + EXTRA, :] = col_tail[...]
 
 
-def dlogit_kernel(ids_ref, scale_ref, *refs):
-    either_way(scale_ref, lambda bounded: dlogit_part(bounded, ids_ref, scale_ref, *refs))
-
-
-def dlogit_part(
-    bounded, ids_ref, scale_ref, pos_ref, row_shift, col_shift, i0, i1, i2, i3, t0, t1,
-    d0, d1, d2, d3,
-):
-    scale2 = scale_ref[0] * LOG2E
+def dlogit_kernel(pieces, ids_ref, scale_ref, *refs):
+    either_way(scale_ref, lambda bounded: dlogit_part(bounded, pieces, ids_ref, *refs))
+
+
+def dlogit_part(bounded, places_of, ids_ref, pos_ref, row_shift, col_shift, *refs):
+    count = len(places_of)
     col_of, row_of = places(ids_ref)
     columns = jnp.exp2(-col_shift[...]) if bounded else col_shift[...]
     lanes = lax.broadcasted_iota(jnp.int32, (1, 8 * ROWS), 1)
-    for q, (rows_ref, d_ref) in enumerate(zip((i0, i1, i2, i3), (d0, d1, d2, d3))):
+    for q, kept_ref, d_ref in zip(places_of, refs[:count], refs[count:]):
         for h in range(QUAD // CHUNK):
-            rows = rows_ref[h * CHUNK : (h + 1) * CHUNK, :]
-            logits = logits2(rows, t0, t1, scale2)
+            kept = kept_ref[h * CHUNK : (h + 1) * CHUNK, :]
             pieces = []
             for b in range(CHUNK // ROWS):
                 place = col_of(q, h * (CHUNK // ROWS) + b)
@@ -277,9 +275,9 @@
                 pos = pos_ref[pl.ds(pl.multiple_of(place * ROWS, ROWS), ROWS), :]
                 shift = jnp.concatenate([shift] * 8, axis=1)
                 pos = jnp.concatenate([pos] * 8, axis=1)
-                part = logits[b * ROWS : (b + 1) * ROWS]
+                part = kept[b * ROWS : (b + 1) * ROWS]
                 if bounded:
-                    soft = jnp.exp2(part) * (shift + columns)
+                    soft = part * (shift + columns)
                 else:
                     soft = jnp.exp2(part - shift) + jnp.exp2(part - columns)
                 pieces.append(jnp.where(pos == lanes, soft - 1.0, soft).astype(BF16))
@@ -367,14 +365,18 @@
 
     row_shape = shape((40, ROWS), F32)
     common = (ids, scale, pos)
-    stats = call(
-        functools.partial(forward_kernel, False, (0, 3)), [row_shape, shape((8, 8 * ROWS), F32)],
+    kept = shape((QUAD, 8 * ROWS), F32)
+    row_stat, state, *near_kept = call(
+        functools.partial(forward_kernel, False, (0, 3)),
+        [row_shape, shape((8, 8 * ROWS), F32), kept, kept],
         *common, imgs[0], imgs[3], txt0, txt1, arrived, specs=[SMEM, SMEM] + [VMEM] * 6,
     )
-    row_stat, col_stat = call(
-        functools.partial(forward_kernel, True, (2, 1)), [row_shape, shape((16, ROWS), F32)],
-        *common, imgs[2], imgs[1], txt0, txt1, *stats, specs=[SMEM, SMEM] + [VMEM] * 7,
-    )
+    row_stat, col_stat, *far_kept = call(
+        functools.partial(forward_kernel, True, (2, 1)),
+        [row_shape, shape((16, ROWS), F32), kept, kept],
+        *common, imgs[2], imgs[1], txt0, txt1, row_stat, state, specs=[SMEM, SMEM] + [VMEM] * 7,
+    )
+    kept = (near_kept[0], far_kept[1], far_kept[0], near_kept[1])
     col_shape = shape((16, ROWS), F32)
     row_stat, col_stat = call(
         merge_kernel, [row_shape, col_shape],
@@ -393,10 +395,15 @@
 
     sent = shape((QUAD + EXTRA, WIDTH), BF16)
     small = [shape((ROWS + EXTRA, WIDTH), BF16)] * 4
-    dlogits = call(
-        dlogit_kernel, [shape((QUAD, 8 * ROWS), BF16)] * 4,
-        *common, row_shift, col_shift, *imgs, txt0, txt1, cost=BUSY, specs=[SMEM, SMEM] + [VMEM] * 9,
-    )
+    dlogits = {}
+    for pieces in ((3,), (2, 1, 0)):
+        made = call(
+            functools.partial(dlogit_kernel, pieces), [shape((QUAD, 8 * ROWS), BF16)] * len(pieces),
+            *common, row_shift, col_shift, *(kept[q] for q in pieces),
+            cost=BUSY, specs=[SMEM, SMEM] + [VMEM] * (3 + len(pieces)),
+        )
+        dlogits.update(zip(pieces, made))
+    dlogits = [dlogits[q] for q in range(4)]
     grads = [
         call(images_grad, sent, scale, col_tail, txt0, txt1, d, cost=BUSY, specs=[SMEM] + [VMEM] * 4)
         for d in dlogits

time: 87.6 us -> 86.8 us (level)
  waiting for transfers between devices: 23.9 us -> 21.4 us
    ppermute x28, waiting for transfers between devices: 23.9 us -> 21.4 us  [shifted(): return lax.ppermute(value, RC, pairs)]
    unnamed x8 -> x10, local copies, waits for them, and re-layouts: 0.95 us -> 1.82 us
    pallas_call x17 -> x18, Pallas kernels: 20 us -> 20.6 us  [call(): pl.pallas_call(kernel, out_shape=outs, in_specs=specs or [VMEM] * len(arg...]
  transfers between devices with their start and end apart: 28 -> 28, of which waited for: 15 -> 13; matrix products, arithmetic and copies ran while one was open for 1% -> 1% of each run, Pallas kernels for 11% -> 15%
where the time goes in v5:
time: 86.8 us; the launch traced here: 86 us
  starting transfers between devices  39 us (45%)
  Pallas kernels  21.6 us (25%)
  waiting for transfers between devices  21.4 us (25%)
  local copies, waits for them, and re-layouts  2.14 us (2%)
  between operations  1.7 us (2%)
    ppermute x28, starting transfers between devices, shifted(): return lax.ppermute(value, RC, pairs)  39 us
    ppermute x28, waiting for transfers between devices, shifted(): return lax.ppermute(value, RC, pairs)  21.4 us
    pallas_call x18, Pallas kernels, call(): pl.pallas_call(kernel, out_shape=outs, in_specs=specs or [VMEM] * len(arg...  20.6 us
    unnamed x10, local copies, waits for them, and re-layouts  1.82 us
  transfers between devices with their start and end apart: 28, of which 13 were waited for; matrix products, arithmetic and copies ran while one was open for 1% of the time, Pallas kernels for 15%

profile of v5, /device:TPU:0, one launch (start us, length us, event | category | flops | bytes accessed | tf_op | source)
XLA Modules:
  0.0 86.0 jit_solution(8471181953881731061)
XLA Ops:
  0.6 0.0 copy-start.2
  0.6 0.9 %copy-done.2 = bf16[128,512]{1,0:T(8,128)(2,1)S(1)} copy-done((bf16[128,512]{1,0:T(8,128)(2,1)S(1)}, bf16[128,512]{1,0:T(8,128)(2,1)}, u32[]{:S(2)}) %copy-start.2) | copy-done | bytes 131096
  1.5 0.1 shard_map.75.refs_0_
  1.7 3.2 %collective-permute-start.2 = (bf16[128,512]{1,0:T(8,128)(2,1)S(1)}, bf16[128,512]{1,0:T(8,128)(2,1)S(1)}, u32[]{:S(2)}, u32[]{:S(2)}) collective-permute-start(bf16[128,512]{1,0:T(8,128)(2,1)S(1)} %shard_map.75.refs_0_), channel_id=1, source_target_pairs={{0,8},{1,9},{2,10},{3,11},{4,12},{5,13},{6,14},{7,15},{8,0},{9,1},... | collective-permute-start | bytes 393224 | tf_op jit(solution)/shard_map/ppermute | solution.py:37
  4.8 1.1 %collective-permute-start.1 = (bf16[128,512]{1,0:T(8,128)(2,1)S(1)}, bf16[128,512]{1,0:T(8,128)(2,1)S(1)}, u32[]{:S(2)}, u32[]{:S(2)}) collective-permute-start(bf16[128,512]{1,0:T(8,128)(2,1)S(1)} %shard_map.75.refs_0_), channel_id=1, source_target_pairs={{0,12},{1,13},{2,14},{3,15},{4,0},{5,1},{6,2},{7,3},{8,4},{9,5},{1... | collective-permute-start | bytes 393224 | tf_op jit(solution)/shard_map/ppermute | solution.py:37
  6.0 0.9 %collective-permute-start = (bf16[128,512]{1,0:T(8,128)(2,1)S(1)}, bf16[128,512]{1,0:T(8,128)(2,1)S(1)}, u32[]{:S(2)}, u32[]{:S(2)}) collective-permute-start(bf16[128,512]{1,0:T(8,128)(2,1)S(1)} %shard_map.75.refs_0_), channel_id=1, source_target_pairs={{0,4},{1,5},{2,6},{3,7},{4,8},{5,9},{6,10},{7,11},{8,12},{9,13},{1... | collective-permute-start | bytes 393224 | tf_op jit(solution)/shard_map/ppermute | solution.py:37
  6.9 0.9 %copy-done = bf16[128,512]{1,0:T(8,128)(2,1)S(1)} copy-done((bf16[128,512]{1,0:T(8,128)(2,1)S(1)}, bf16[128,512]{1,0:T(8,128)(2,1)}, u32[]{:S(2)}) %copy-start) | copy-done | bytes 131096
  7.8 0.1 shard_map.76
  7.9 4.0 %collective-permute-start.7 = (bf16[128,512]{1,0:T(8,128)(2,1)S(1)}, bf16[128,512]{1,0:T(8,128)(2,1)S(1)}, u32[]{:S(2)}, u32[]{:S(2)}) collective-permute-start(bf16[128,512]{1,0:T(8,128)(2,1)S(1)} %shard_map.76), channel_id=1, source_target_pairs={{0,64},{1,65},{2,66},{3,67},{4,68},{5,69},{6,70},{7,71},{8,72},{9,... | collective-permute-start | bytes 393224 | tf_op jit(solution)/shard_map/ppermute | solution.py:37
  11.8 0.7 collective-permute-start.6
  12.6 1.3 %collective-permute-start.5 = (bf16[128,512]{1,0:T(8,128)(2,1)S(1)}, bf16[128,512]{1,0:T(8,128)(2,1)S(1)}, u32[]{:S(2)}, u32[]{:S(2)}) collective-permute-start(bf16[128,512]{1,0:T(8,128)(2,1)S(1)} %shard_map.76), channel_id=1, source_target_pairs={{0,32},{1,33},{2,34},{3,35},{4,36},{5,37},{6,38},{7,39},{8,40},{9,... | collective-permute-start | bytes 393224 | tf_op jit(solution)/shard_map/ppermute | solution.py:37
  13.9 3.3 %collective-permute-start.9 = (bf16[512,512]{1,0:T(8,128)(2,1)S(1)}, bf16[512,512]{1,0:T(8,128)(2,1)S(1)}, u32[]{:S(2)}, u32[]{:S(2)}) collective-permute-start(bf16[512,512]{1,0:T(8,128)(2,1)S(1)} %pad_maximum_fusion.refs_1_.i0), channel_id=1, source_target_pairs={{0,2},{1,3},{2,0},{3,1},{4,6},{5,7},{6,4},{7,5},{8,10},{9,11},{10,... | collective-permute-start | bytes 1572872 | tf_op jit(solution)/shard_map/ppermute | solution.py:37
  17.2 0.0 collective-permute-done.7
  17.2 1.1 %collective-permute-done.6 = bf16[128,512]{1,0:T(8,128)(2,1)S(1)} collective-permute-done((bf16[128,512]{1,0:T(8,128)(2,1)S(1)}, bf16[128,512]{1,0:T(8,128)(2,1)S(1)}, u32[]{:S(2)}, u32[]{:S(2)}) %collective-permute-start.6) | collective-permute-done | bytes 131104 | tf_op jit(solution)/shard_map/ppermute | solution.py:37
  18.3 0.5 collective-permute-done.5
  18.8 0.1 collective-permute-start.8
  18.9 1.6 %collective-permute-start.4 = (bf16[512,512]{1,0:T(8,128)(2,1)S(1)}, bf16[512,512]{1,0:T(8,128)(2,1)S(1)}, u32[]{:S(2)}, u32[]{:S(2)}) collective-permute-start(bf16[512,512]{1,0:T(8,128)(2,1)S(1)} %pad_maximum_fusion.refs_1_.i0), channel_id=1, source_target_pairs={{0,1},{1,2},{2,3},{3,0},{4,5},{5,6},{6,7},{7,4},{8,9},{9,10},{10,1... | collective-permute-start | bytes 1572872 | tf_op jit(solution)/shard_map/ppermute | solution.py:37
  20.5 1.7 %collective-permute-start.3 = (bf16[512,512]{1,0:T(8,128)(2,1)S(1)}, bf16[512,512]{1,0:T(8,128)(2,1)S(1)}, u32[]{:S(2)}, u32[]{:S(2)}) collective-permute-start(bf16[512,512]{1,0:T(8,128)(2,1)S(1)} %pad_maximum_fusion.refs_1_.i0), channel_id=1, source_target_pairs={{0,3},{1,0},{2,1},{3,2},{4,7},{5,4},{6,5},{7,6},{8,11},{9,8},{10,9... | collective-permute-start | bytes 1572872 | tf_op jit(solution)/shard_map/ppermute | solution.py:37
  22.9 0.1 pad_add_fusion.ids_ref
  23.0 1.8 %collective-permute-done.9.refs_0_.refs_2_.i3 = bf16[512,512]{1,0:T(8,128)(2,1)S(1)} collective-permute-done((bf16[512,512]{1,0:T(8,128)(2,1)S(1)}, bf16[512,512]{1,0:T(8,128)(2,1)S(1)}, u32[]{:S(2)}, u32[]{:S(2)}) %collective-permute-start.9) | collective-permute-done | bytes 524320 | tf_op jit(solution)/shard_map/ppermute | solution.py:37
  24.8 0.3 broadcast_in_dim.8.refs_0_
  25.1 4.4 %shard_map.78 = (f32[40,128]{1,0:T(8,128)S(1)}, f32[8,1024]{1,0:T(8,128)S(1)}, f32[512,1024]{1,0:T(8,128)S(1)}, f32[512,1024]{1,0:T(8,128)S(1)}) custom-call(s32[2]{0:T(128)S(1)} %pad_add_fusion.ids_ref, f32[1]{0:T(128)S(6)} %exp.3.scale_ref, s32[2048,128]{1,0:T(8,128)S(1)} %broadcast_in_dim.8.refs_0_, bf16[512,512]{1,0:T(8,128)(2,1)S(1)} %pad_maximum_fusion.refs_1_.i0, ...), custom_call_target="tpu_custom_call" | custom-call | tf_op jit(solution)/shard_map/pallas_call | solution.py:57
  29.5 0.8 collective-permute-done.4.refs_2_.i1
  30.3 0.3 collective-permute-done.3.refs_1_.i2
  30.6 5.0 %shard_map.79 = (f32[40,128]{1,0:T(8,128)S(1)}, f32[16,128]{1,0:T(8,128)S(1)}, f32[512,1024]{1,0:T(8,128)S(1)}, f32[512,1024]{1,0:T(8,128)S(1)}) custom-call(s32[2]{0:T(128)S(1)} %pad_add_fusion.ids_ref, f32[1]{0:T(128)S(6)} %exp.3.scale_ref, s32[2048,128]{1,0:T(8,128)S(1)} %broadcast_in_dim.8.refs_0_, ...), custom_call_target="tpu_custom_call" | custom-call | tf_op jit(solution)/shard_map/pallas_call | solution.py:57
  35.6 0.8 collective-permute-start.12
  36.4 2.5 %collective-permute-start.11 = (f32[40,128]{1,0:T(8,128)S(1)}, f32[40,128]{1,0:T(8,128)S(1)}, u32[]{:S(2)}, u32[]{:S(2)}) collective-permute-start(f32[40,128]{1,0:T(8,128)S(1)} %get-tuple-element.33.refs_0_), channel_id=1, source_target_pairs={{0,12},{1,13},{2,14},{3,15},{4,0},{5,1},{6,2},{7,3},{8,4},{9,5},{1... | collective-permute-start | bytes 61448 | tf_op jit(solution)/shard_map/ppermute | solution.py:37
  38.9 1.2 %collective-permute-done.13.refs_5_ = f32[16,128]{1,0:T(8,128)S(1)} collective-permute-done((f32[16,128]{1,0:T(8,128)S(1)}, f32[16,128]{1,0:T(8,128)S(1)}, u32[]{:S(2)}, u32[]{:S(2)}) %collective-permute-start.13) | collective-permute-done | bytes 8224 | tf_op jit(solution)/shard_map/ppermute | solution.py:37
  40.1 0.8 collective-permute-done.12.refs_3_
  41.0 0.0 collective-permute-done.11.refs_2_
  41.0 3.0 %collective-permute-done.10.refs_1_ = f32[40,128]{1,0:T(8,128)S(1)} collective-permute-done((f32[40,128]{1,0:T(8,128)S(1)}, f32[40,128]{1,0:T(8,128)S(1)}, u32[]{:S(2)}, u32[]{:S(2)}) %collective-permute-start.10) | collective-permute-done | bytes 20512 | tf_op jit(solution)/shard_map/ppermute | solution.py:37
  44.0 1.5 %collective-permute-start.14 = (f32[40,128]{1,0:T(8,128)S(1)}, f32[40,128]{1,0:T(8,128)S(1)}, u32[]{:S(2)}, u32[]{:S(2)}) collective-permute-start(f32[40,128]{1,0:T(8,128)S(1)} %get-tuple-element.35.refs_0_), channel_id=1, source_target_pairs={{0,1},{1,0},{2,3},{3,2},{4,5},{5,4},{6,7},{7,6},{8,9},{9,8},{10,11... | collective-permute-start | bytes 61448 | tf_op jit(solution)/shard_map/ppermute | solution.py:37
  45.4 1.0 %collective-permute-start.15 = (f32[16,128]{1,0:T(8,128)S(1)}, f32[16,128]{1,0:T(8,128)S(1)}, u32[]{:S(2)}, u32[]{:S(2)}) collective-permute-start(f32[16,128]{1,0:T(8,128)S(1)} %get-tuple-element.36.refs_2_), channel_id=1, source_target_pairs={{0,32},{1,33},{2,34},{3,35},{4,36},{5,37},{6,38},{7,39},{8,40},{9,... | collective-permute-start | bytes 24584 | tf_op jit(solution)/shard_map/ppermute | solution.py:37
  46.5 2.6 %collective-permute-done.15.refs_3_ = f32[16,128]{1,0:T(8,128)S(1)} collective-permute-done((f32[16,128]{1,0:T(8,128)S(1)}, f32[16,128]{1,0:T(8,128)S(1)}, u32[]{:S(2)}, u32[]{:S(2)}) %collective-permute-start.15) | collective-permute-done | bytes 8224 | tf_op jit(solution)/shard_map/ppermute | solution.py:37
  49.1 2.1 %collective-permute-start.16 = (f32[40,128]{1,0:T(8,128)S(1)}, f32[40,128]{1,0:T(8,128)S(1)}, u32[]{:S(2)}, u32[]{:S(2)}) collective-permute-start(f32[40,128]{1,0:T(8,128)S(1)} %get-tuple-element.37.r0), channel_id=1, source_target_pairs={{0,3},{1,2},{2,1},{3,0},{4,7},{5,6},{6,5},{7,4},{8,11},{9,10},{10,... | collective-permute-start | bytes 61448 | tf_op jit(solution)/shard_map/ppermute | solution.py:37
  51.2 1.9 %collective-permute-start.17 = (f32[16,128]{1,0:T(8,128)S(1)}, f32[16,128]{1,0:T(8,128)S(1)}, u32[]{:S(2)}, u32[]{:S(2)}) collective-permute-start(f32[16,128]{1,0:T(8,128)S(1)} %get-tuple-element.38.c0), channel_id=1, source_target_pairs={{0,96},{1,97},{2,98},{3,99},{4,100},{5,101},{6,102},{7,103},{8,104... | collective-permute-start | bytes 24584 | tf_op jit(solution)/shard_map/ppermute | solution.py:37
  53.1 2.9 %collective-permute-done.17.c1 = f32[16,128]{1,0:T(8,128)S(1)} collective-permute-done((f32[16,128]{1,0:T(8,128)S(1)}, f32[16,128]{1,0:T(8,128)S(1)}, u32[]{:S(2)}, u32[]{:S(2)}) %collective-permute-start.17) | collective-permute-done | bytes 8224 | tf_op jit(solution)/shard_map/ppermute | solution.py:37
  56.1 0.7 shard_map.82
  56.8 1.3 %shard_map.84.d_ref.d3 = bf16[512,1024]{1,0:T(8,128)(2,1)S(1)} custom-call(s32[2]{0:T(128)S(1)} %pad_add_fusion.ids_ref, f32[1]{0:T(128)S(6)} %exp.3.scale_ref, s32[2048,128]{1,0:T(8,128)S(1)} %broadcast_in_dim.8.refs_0_, f32[16,128]{1,0:T(8,128)S(1)} %get-tuple-element.40.refs_1_, f32[1,1024]{1,0:T(1,128)S(1)} %get-tuple-element.41.refs_2_, ...), custom_call_target="tpu_custom_call" | custom-call | flops 10000000000 | bytes 1000000 | tf_op jit(solution)/shard_map/pallas_call | solution.py:57
  58.1 0.7 shard_map.87.refs_2_
  58.8 0.9 %collective-permute-start.21 = (bf16[528,512]{1,0:T(8,128)(2,1)S(1)}, bf16[528,512]{1,0:T(8,128)(2,1)S(1)}, u32[]{:S(2)}, u32[]{:S(2)}) collective-permute-start(bf16[528,512]{1,0:T(8,128)(2,1)S(1)} %shard_map.87.refs_2_), channel_id=1, source_target_pairs={{0,2},{1,3},{2,0},{3,1},{4,6},{5,7},{6,4},{7,5},{8,10},{9,11},{10,... | collective-permute-start | bytes 1622024 | tf_op jit(solution)/shard_map/ppermute | solution.py:37
  59.7 2.5 %shard_map.83 = (bf16[512,1024]{1,0:T(8,128)(2,1)S(1)}, bf16[512,1024]{1,0:T(8,128)(2,1)S(1)}, bf16[512,1024]{1,0:T(8,128)(2,1)S(1)}) custom-call(s32[2]{0:T(128)S(1)} %pad_add_fusion.ids_ref, f32[1]{0:T(128)S(6)} %exp.3.scale_ref, s32[2048,128]{1,0:T(8,128)S(1)} %broadcast_in_dim.8.refs_0_, f32[16,128]{1,0:T(8,128)S(1)} %get-tuple-element.40.refs_1_, ...), custom_call_target="tpu_custom_call" | custom-call | flops 10000000000 | bytes 1000000 | tf_op jit(solution)/shard_map/pallas_call | solution.py:57
  62.2 0.7 shard_map.86.refs_1_
  62.9 1.5 %collective-permute-start.20 = (bf16[528,512]{1,0:T(8,128)(2,1)S(1)}, bf16[528,512]{1,0:T(8,128)(2,1)S(1)}, u32[]{:S(2)}, u32[]{:S(2)}) collective-permute-start(bf16[528,512]{1,0:T(8,128)(2,1)S(1)} %shard_map.86.refs_1_), channel_id=1, source_target_pairs={{0,1},{1,2},{2,3},{3,0},{4,5},{5,6},{6,7},{7,4},{8,9},{9,10},{10,1... | collective-permute-start | bytes 1622024 | tf_op jit(solution)/shard_map/ppermute | solution.py:37
  64.5 0.7 shard_map.85.refs_0_
  65.2 2.0 %collective-permute-start.19 = (bf16[528,512]{1,0:T(8,128)(2,1)S(1)}, bf16[528,512]{1,0:T(8,128)(2,1)S(1)}, u32[]{:S(2)}, u32[]{:S(2)}) collective-permute-start(bf16[528,512]{1,0:T(8,128)(2,1)S(1)} %shard_map.85.refs_0_), channel_id=1, source_target_pairs={{0,3},{1,0},{2,1},{3,2},{4,7},{5,4},{6,5},{7,6},{8,11},{9,8},{10,9... | collective-permute-start | bytes 1622024 | tf_op jit(solution)/shard_map/ppermute | solution.py:37
  67.3 1.5 %shard_map.88.refs_0_ = bf16[528,512]{1,0:T(8,128)(2,1)S(1)} custom-call(f32[1]{0:T(128)S(6)} %exp.3.scale_ref, bf16[16,512]{1,0:T(8,128)(2,1)S(1)} %get-tuple-element.39.row_tail, bf16[512,512]{1,0:T(8,128)(2,1)S(1)} %pad_maximum_fusion.refs_1_.i0, bf16[512,512]{1,0:T(8,128)(2,1)S(1)} %collective-permute-done.4.refs_2_.i1, ...), custom_call_target="tpu_custom_call" | custom-call | flops 10000000000 | bytes 1000000 | tf_op jit(solution)/shard_map/pallas_call | solution.py:57
  68.8 0.1 collective-permute-start.18
  68.9 1.5 %shard_map.89.refs_0_ = bf16[528,512]{1,0:T(8,128)(2,1)S(1)} custom-call(f32[1]{0:T(128)S(6)} %exp.3.scale_ref, bf16[16,512]{1,0:T(8,128)(2,1)S(1)} %get-tuple-element.39.row_tail, bf16[512,512]{1,0:T(8,128)(2,1)S(1)} %pad_maximum_fusion.refs_1_.i0, bf16[512,512]{1,0:T(8,128)(2,1)S(1)} %collective-permute-done.4.refs_2_.i1, ...), custom_call_target="tpu_custom_call" | custom-call | flops 10000000000 | bytes 1000000 | tf_op jit(solution)/shard_map/pallas_call | solution.py:57
  70.4 0.4 collective-permute-done.18.refs_1_
  70.8 0.2 shard_map.90
  71.0 2.3 %collective-permute-start.25 = (bf16[144,512]{1,0:T(8,128)(2,1)S(1)}, bf16[144,512]{1,0:T(8,128)(2,1)S(1)}, u32[]{:S(2)}, u32[]{:S(2)}) collective-permute-start(bf16[144,512]{1,0:T(8,128)(2,1)S(1)} %get-tuple-element.55), channel_id=1, source_target_pairs={{0,96},{1,97},{2,98},{3,99},{4,100},{5,101},{6,102},{7,103},{8,104... | collective-permute-start | bytes 442376 | tf_op jit(solution)/shard_map/ppermute | solution.py:37
  73.3 0.7 shard_map.91.refs_0_
  74.0 0.0 copy-start.1
  74.0 0.0 copy-start.3
  74.1 0.1 collective-permute-start.26
  74.2 1.5 %collective-permute-start.27 = (bf16[144,512]{1,0:T(8,128)(2,1)S(1)}, bf16[144,512]{1,0:T(8,128)(2,1)S(1)}, u32[]{:S(2)}, u32[]{:S(2)}) collective-permute-start(bf16[144,512]{1,0:T(8,128)(2,1)S(1)} %get-tuple-element.57), channel_id=1, source_target_pairs={{0,64},{1,65},{2,66},{3,67},{4,68},{5,69},{6,70},{7,71},{8,72},{9,... | collective-permute-start | bytes 442376 | tf_op jit(solution)/shard_map/ppermute | solution.py:37
  75.6 0.4 shard_map.92
  76.0 0.1 collective-permute-start.22
  76.1 2.0 %collective-permute-start.23 = (bf16[144,512]{1,0:T(8,128)(2,1)S(1)}, bf16[144,512]{1,0:T(8,128)(2,1)S(1)}, u32[]{:S(2)}, u32[]{:S(2)}) collective-permute-start(bf16[144,512]{1,0:T(8,128)(2,1)S(1)} %get-tuple-element.53), channel_id=1, source_target_pairs={{0,4},{1,5},{2,6},{3,7},{4,8},{5,9},{6,10},{7,11},{8,12},{9,13},{1... | collective-permute-start | bytes 442376 | tf_op jit(solution)/shard_map/ppermute | solution.py:37
  78.1 0.7 collective-permute-start.24
  78.8 5.3 %collective-permute-done.26.b2 = bf16[144,512]{1,0:T(8,128)(2,1)S(1)} collective-permute-done((bf16[144,512]{1,0:T(8,128)(2,1)S(1)}, bf16[144,512]{1,0:T(8,128)(2,1)S(1)}, u32[]{:S(2)}, u32[]{:S(2)}) %collective-permute-start.26) | collective-permute-done | bytes 147488 | tf_op jit(solution)/shard_map/ppermute | solution.py:37
  84.1 0.6 collective-permute-done.24.a3
  84.7 1.1 %shard_map.93 = (f32[128,512]{1,0:T(8,128)}, f32[128,512]{1,0:T(8,128)}, f32[1]{0:T(128)}, f32[1]{0:T(128)}) custom-call(bf16[128,512]{1,0:T(8,128)(2,1)S(1)} %copy-done.3, bf16[128,512]{1,0:T(8,128)(2,1)S(1)} %copy-done.1, bf16[144,512]{1,0:T(8,128)(2,1)S(1)} %get-tuple-element.51.a0, bf16[144,512]{1,0:T(8,128)(2,1)S(1)} %collective-permute-done.22.a1, ...), custom_call_target="tpu_custom_call" | custom-call | tf_op jit(solution)/shard_map/pallas_call | solution.py:431
  (26 shorter events, 0.2 us)
Async XLA Ops:
  0.6 0.9 %copy-start.2 = (bf16[128,512]{1,0:T(8,128)(2,1)S(1)}, bf16[128,512]{1,0:T(8,128)(2,1)}, u32[]{:S(2)}) copy-start(bf16[128,512]{1,0:T(8,128)(2,1)} %img_ref.1) | copy-start | bytes 393220
  1.5 21.4 %copy-start.4 = (s32[2048]{0:T(1024)S(1)}, s32[2048]{0:T(1024)}, u32[]{:S(2)}) copy-start(s32[2048]{0:T(1024)} %param.6) | copy-start | bytes 24580
  1.7 10.9 %collective-permute-start.2 = (bf16[128,512]{1,0:T(8,128)(2,1)S(1)}, bf16[128,512]{1,0:T(8,128)(2,1)S(1)}, u32[]{:S(2)}, u32[]{:S(2)}) collective-permute-start(bf16[128,512]{1,0:T(8,128)(2,1)S(1)} %shard_map.75.refs_0_), channel_id=1, source_target_pairs={{0,8},{1,9},{2,10},{3,11},{4,12},{5,13},{6,14},{7,15},{8,0},{9,1},... | collective-permute-start | bytes 393224 | tf_op jit(solution)/shard_map/ppermute | solution.py:37
  4.8 9.0 %collective-permute-start.1 = (bf16[128,512]{1,0:T(8,128)(2,1)S(1)}, bf16[128,512]{1,0:T(8,128)(2,1)S(1)}, u32[]{:S(2)}, u32[]{:S(2)}) collective-permute-start(bf16[128,512]{1,0:T(8,128)(2,1)S(1)} %shard_map.75.refs_0_), channel_id=1, source_target_pairs={{0,12},{1,13},{2,14},{3,15},{4,0},{5,1},{6,2},{7,3},{8,4},{9,5},{1... | collective-permute-start | bytes 393224 | tf_op jit(solution)/shard_map/ppermute | solution.py:37
  6.0 7.9 %collective-permute-start = (bf16[128,512]{1,0:T(8,128)(2,1)S(1)}, bf16[128,512]{1,0:T(8,128)(2,1)S(1)}, u32[]{:S(2)}, u32[]{:S(2)}) collective-permute-start(bf16[128,512]{1,0:T(8,128)(2,1)S(1)} %shard_map.75.refs_0_), channel_id=1, source_target_pairs={{0,4},{1,5},{2,6},{3,7},{4,8},{5,9},{6,10},{7,11},{8,12},{9,13},{1... | collective-permute-start | bytes 393224 | tf_op jit(solution)/shard_map/ppermute | solution.py:37
  6.9 0.9 %copy-start = (bf16[128,512]{1,0:T(8,128)(2,1)S(1)}, bf16[128,512]{1,0:T(8,128)(2,1)}, u32[]{:S(2)}) copy-start(bf16[128,512]{1,0:T(8,128)(2,1)} %txt_ref.1) | copy-start | bytes 393220
  7.9 9.3 %collective-permute-start.7 = (bf16[128,512]{1,0:T(8,128)(2,1)S(1)}, bf16[128,512]{1,0:T(8,128)(2,1)S(1)}, u32[]{:S(2)}, u32[]{:S(2)}) collective-permute-start(bf16[128,512]{1,0:T(8,128)(2,1)S(1)} %shard_map.76), channel_id=1, source_target_pairs={{0,64},{1,65},{2,66},{3,67},{4,68},{5,69},{6,70},{7,71},{8,72},{9,... | collective-permute-start | bytes 393224 | tf_op jit(solution)/shard_map/ppermute | solution.py:37
  11.8 6.4 %collective-permute-start.6 = (bf16[128,512]{1,0:T(8,128)(2,1)S(1)}, bf16[128,512]{1,0:T(8,128)(2,1)S(1)}, u32[]{:S(2)}, u32[]{:S(2)}) collective-permute-start(bf16[128,512]{1,0:T(8,128)(2,1)S(1)} %shard_map.76), channel_id=1, source_target_pairs={{0,96},{1,97},{2,98},{3,99},{4,100},{5,101},{6,102},{7,103},{8,104... | collective-permute-start | bytes 393224 | tf_op jit(solution)/shard_map/ppermute | solution.py:37
  12.6 6.2 %collective-permute-start.5 = (bf16[128,512]{1,0:T(8,128)(2,1)S(1)}, bf16[128,512]{1,0:T(8,128)(2,1)S(1)}, u32[]{:S(2)}, u32[]{:S(2)}) collective-permute-start(bf16[128,512]{1,0:T(8,128)(2,1)S(1)} %shard_map.76), channel_id=1, source_target_pairs={{0,32},{1,33},{2,34},{3,35},{4,36},{5,37},{6,38},{7,39},{8,40},{9,... | collective-permute-start | bytes 393224 | tf_op jit(solution)/shard_map/ppermute | solution.py:37
  13.9 10.9 %collective-permute-start.9 = (bf16[512,512]{1,0:T(8,128)(2,1)S(1)}, bf16[512,512]{1,0:T(8,128)(2,1)S(1)}, u32[]{:S(2)}, u32[]{:S(2)}) collective-permute-start(bf16[512,512]{1,0:T(8,128)(2,1)S(1)} %pad_maximum_fusion.refs_1_.i0), channel_id=1, source_target_pairs={{0,2},{1,3},{2,0},{3,1},{4,6},{5,7},{6,4},{7,5},{8,10},{9,11},{10,... | collective-permute-start | bytes 1572872 | tf_op jit(solution)/shard_map/ppermute | solution.py:37
  18.8 6.0 %collective-permute-start.8 = (bf16[512,512]{1,0:T(8,128)(2,1)S(1)}, bf16[512,512]{1,0:T(8,128)(2,1)S(1)}, u32[]{:S(2)}, u32[]{:S(2)}) collective-permute-start(bf16[512,512]{1,0:T(8,128)(2,1)S(1)} %pad_maximum_fusion.1.refs_3_.t0), channel_id=1, source_target_pairs={{0,16},{1,17},{2,18},{3,19},{4,20},{5,21},{6,22},{7,23},{8,24},{9,... | collective-permute-start | bytes 1572872 | tf_op jit(solution)/shard_map/ppermute | solution.py:37
  18.9 11.4 %collective-permute-start.4 = (bf16[512,512]{1,0:T(8,128)(2,1)S(1)}, bf16[512,512]{1,0:T(8,128)(2,1)S(1)}, u32[]{:S(2)}, u32[]{:S(2)}) collective-permute-start(bf16[512,512]{1,0:T(8,128)(2,1)S(1)} %pad_maximum_fusion.refs_1_.i0), channel_id=1, source_target_pairs={{0,1},{1,2},{2,3},{3,0},{4,5},{5,6},{6,7},{7,4},{8,9},{9,10},{10,1... | collective-permute-start | bytes 1572872 | tf_op jit(solution)/shard_map/ppermute | solution.py:37
  20.5 10.1 %collective-permute-start.3 = (bf16[512,512]{1,0:T(8,128)(2,1)S(1)}, bf16[512,512]{1,0:T(8,128)(2,1)S(1)}, u32[]{:S(2)}, u32[]{:S(2)}) collective-permute-start(bf16[512,512]{1,0:T(8,128)(2,1)S(1)} %pad_maximum_fusion.refs_1_.i0), channel_id=1, source_target_pairs={{0,3},{1,0},{2,1},{3,2},{4,7},{5,4},{6,5},{7,6},{8,11},{9,8},{10,9... | collective-permute-start | bytes 1572872 | tf_op jit(solution)/shard_map/ppermute | solution.py:37
  35.6 5.3 %collective-permute-start.12 = (f32[40,128]{1,0:T(8,128)S(1)}, f32[40,128]{1,0:T(8,128)S(1)}, u32[]{:S(2)}, u32[]{:S(2)}) collective-permute-start(f32[40,128]{1,0:T(8,128)S(1)} %get-tuple-element.33.refs_0_), channel_id=1, source_target_pairs={{0,8},{1,9},{2,10},{3,11},{4,12},{5,13},{6,14},{7,15},{8,0},{9,1},... | collective-permute-start | bytes 61448 | tf_op jit(solution)/shard_map/ppermute | solution.py:37
  36.4 4.5 %collective-permute-start.11 = (f32[40,128]{1,0:T(8,128)S(1)}, f32[40,128]{1,0:T(8,128)S(1)}, u32[]{:S(2)}, u32[]{:S(2)}) collective-permute-start(f32[40,128]{1,0:T(8,128)S(1)} %get-tuple-element.33.refs_0_), channel_id=1, source_target_pairs={{0,12},{1,13},{2,14},{3,15},{4,0},{5,1},{6,2},{7,3},{8,4},{9,5},{1... | collective-permute-start | bytes 61448 | tf_op jit(solution)/shard_map/ppermute | solution.py:37
  38.9 5.0 %collective-permute-start.10 = (f32[40,128]{1,0:T(8,128)S(1)}, f32[40,128]{1,0:T(8,128)S(1)}, u32[]{:S(2)}, u32[]{:S(2)}) collective-permute-start(f32[40,128]{1,0:T(8,128)S(1)} %get-tuple-element.33.refs_0_), channel_id=1, source_target_pairs={{0,4},{1,5},{2,6},{3,7},{4,8},{5,9},{6,10},{7,11},{8,12},{9,13},{1... | collective-permute-start | bytes 61448 | tf_op jit(solution)/shard_map/ppermute | solution.py:37
  38.9 1.2 %collective-permute-start.13 = (f32[16,128]{1,0:T(8,128)S(1)}, f32[16,128]{1,0:T(8,128)S(1)}, u32[]{:S(2)}, u32[]{:S(2)}) collective-permute-start(f32[16,128]{1,0:T(8,128)S(1)} %get-tuple-element.34.refs_4_), channel_id=1, source_target_pairs={{0,16},{1,17},{2,18},{3,19},{4,20},{5,21},{6,22},{7,23},{8,24},{9,... | collective-permute-start | bytes 24584 | tf_op jit(solution)/shard_map/ppermute | solution.py:37
  44.0 5.1 %collective-permute-start.14 = (f32[40,128]{1,0:T(8,128)S(1)}, f32[40,128]{1,0:T(8,128)S(1)}, u32[]{:S(2)}, u32[]{:S(2)}) collective-permute-start(f32[40,128]{1,0:T(8,128)S(1)} %get-tuple-element.35.refs_0_), channel_id=1, source_target_pairs={{0,1},{1,0},{2,3},{3,2},{4,5},{5,4},{6,7},{7,6},{8,9},{9,8},{10,11... | collective-permute-start | bytes 61448 | tf_op jit(solution)/shard_map/ppermute | solution.py:37
  45.4 3.7 %collective-permute-start.15 = (f32[16,128]{1,0:T(8,128)S(1)}, f32[16,128]{1,0:T(8,128)S(1)}, u32[]{:S(2)}, u32[]{:S(2)}) collective-permute-start(f32[16,128]{1,0:T(8,128)S(1)} %get-tuple-element.36.refs_2_), channel_id=1, source_target_pairs={{0,32},{1,33},{2,34},{3,35},{4,36},{5,37},{6,38},{7,39},{8,40},{9,... | collective-permute-start | bytes 24584 | tf_op jit(solution)/shard_map/ppermute | solution.py:37
  49.1 7.0 %collective-permute-start.16 = (f32[40,128]{1,0:T(8,128)S(1)}, f32[40,128]{1,0:T(8,128)S(1)}, u32[]{:S(2)}, u32[]{:S(2)}) collective-permute-start(f32[40,128]{1,0:T(8,128)S(1)} %get-tuple-element.37.r0), channel_id=1, source_target_pairs={{0,3},{1,2},{2,1},{3,0},{4,7},{5,6},{6,5},{7,4},{8,11},{9,10},{10,... | collective-permute-start | bytes 61448 | tf_op jit(solution)/shard_map/ppermute | solution.py:37
  51.2 4.9 %collective-permute-start.17 = (f32[16,128]{1,0:T(8,128)S(1)}, f32[16,128]{1,0:T(8,128)S(1)}, u32[]{:S(2)}, u32[]{:S(2)}) collective-permute-start(f32[16,128]{1,0:T(8,128)S(1)} %get-tuple-element.38.c0), channel_id=1, source_target_pairs={{0,96},{1,97},{2,98},{3,99},{4,100},{5,101},{6,102},{7,103},{8,104... | collective-permute-start | bytes 24584 | tf_op jit(solution)/shard_map/ppermute | solution.py:37
  58.8 15.3 %collective-permute-start.21 = (bf16[528,512]{1,0:T(8,128)(2,1)S(1)}, bf16[528,512]{1,0:T(8,128)(2,1)S(1)}, u32[]{:S(2)}, u32[]{:S(2)}) collective-permute-start(bf16[528,512]{1,0:T(8,128)(2,1)S(1)} %shard_map.87.refs_2_), channel_id=1, source_target_pairs={{0,2},{1,3},{2,0},{3,1},{4,6},{5,7},{6,4},{7,5},{8,10},{9,11},{10,... | collective-permute-start | bytes 1622024 | tf_op jit(solution)/shard_map/ppermute | solution.py:37
  62.9 12.7 %collective-permute-start.20 = (bf16[528,512]{1,0:T(8,128)(2,1)S(1)}, bf16[528,512]{1,0:T(8,128)(2,1)S(1)}, u32[]{:S(2)}, u32[]{:S(2)}) collective-permute-start(bf16[528,512]{1,0:T(8,128)(2,1)S(1)} %shard_map.86.refs_1_), channel_id=1, source_target_pairs={{0,1},{1,2},{2,3},{3,0},{4,5},{5,6},{6,7},{7,4},{8,9},{9,10},{10,1... | collective-permute-start | bytes 1622024 | tf_op jit(solution)/shard_map/ppermute | solution.py:37
  65.2 10.4 %collective-permute-start.19 = (bf16[528,512]{1,0:T(8,128)(2,1)S(1)}, bf16[528,512]{1,0:T(8,128)(2,1)S(1)}, u32[]{:S(2)}, u32[]{:S(2)}) collective-permute-start(bf16[528,512]{1,0:T(8,128)(2,1)S(1)} %shard_map.85.refs_0_), channel_id=1, source_target_pairs={{0,3},{1,0},{2,1},{3,2},{4,7},{5,4},{6,5},{7,6},{8,11},{9,8},{10,9... | collective-permute-start | bytes 1622024 | tf_op jit(solution)/shard_map/ppermute | solution.py:37
  68.8 2.0 %collective-permute-start.18 = (bf16[528,512]{1,0:T(8,128)(2,1)S(1)}, bf16[528,512]{1,0:T(8,128)(2,1)S(1)}, u32[]{:S(2)}, u32[]{:S(2)}) collective-permute-start(bf16[528,512]{1,0:T(8,128)(2,1)S(1)} %shard_map.88.refs_0_), channel_id=1, source_target_pairs={{0,16},{1,17},{2,18},{3,19},{4,20},{5,21},{6,22},{7,23},{8,24},{9,... | collective-permute-start | bytes 1622024 | tf_op jit(solution)/shard_map/ppermute | solution.py:37
  71.0 7.1 %collective-permute-start.25 = (bf16[144,512]{1,0:T(8,128)(2,1)S(1)}, bf16[144,512]{1,0:T(8,128)(2,1)S(1)}, u32[]{:S(2)}, u32[]{:S(2)}) collective-permute-start(bf16[144,512]{1,0:T(8,128)(2,1)S(1)} %get-tuple-element.55), channel_id=1, source_target_pairs={{0,96},{1,97},{2,98},{3,99},{4,100},{5,101},{6,102},{7,103},{8,104... | collective-permute-start | bytes 442376 | tf_op jit(solution)/shard_map/ppermute | solution.py:37
  74.0 10.7 %copy-start.1 = (bf16[128,512]{1,0:T(8,128)(2,1)S(1)}, bf16[128,512]{1,0:T(8,128)(2,1)}, u32[]{:S(2)}) copy-start(bf16[128,512]{1,0:T(8,128)(2,1)} %txt_ref.1) | copy-start | bytes 393220
  74.0 10.7 %copy-start.3 = (bf16[128,512]{1,0:T(8,128)(2,1)S(1)}, bf16[128,512]{1,0:T(8,128)(2,1)}, u32[]{:S(2)}) copy-start(bf16[128,512]{1,0:T(8,128)(2,1)} %img_ref.1) | copy-start | bytes 393220
  74.1 10.0 %collective-permute-start.26 = (bf16[144,512]{1,0:T(8,128)(2,1)S(1)}, bf16[144,512]{1,0:T(8,128)(2,1)S(1)}, u32[]{:S(2)}, u32[]{:S(2)}) collective-permute-start(bf16[144,512]{1,0:T(8,128)(2,1)S(1)} %get-tuple-element.56), channel_id=1, source_target_pairs={{0,32},{1,33},{2,34},{3,35},{4,36},{5,37},{6,38},{7,39},{8,40},{9,... | collective-permute-start | bytes 442376 | tf_op jit(solution)/shard_map/ppermute | solution.py:37
  74.2 10.0 %collective-permute-start.27 = (bf16[144,512]{1,0:T(8,128)(2,1)S(1)}, bf16[144,512]{1,0:T(8,128)(2,1)S(1)}, u32[]{:S(2)}, u32[]{:S(2)}) collective-permute-start(bf16[144,512]{1,0:T(8,128)(2,1)S(1)} %get-tuple-element.57), channel_id=1, source_target_pairs={{0,64},{1,65},{2,66},{3,67},{4,68},{5,69},{6,70},{7,71},{8,72},{9,... | collective-permute-start | bytes 442376 | tf_op jit(solution)/shard_map/ppermute | solution.py:37
  76.0 8.1 %collective-permute-start.22 = (bf16[144,512]{1,0:T(8,128)(2,1)S(1)}, bf16[144,512]{1,0:T(8,128)(2,1)S(1)}, u32[]{:S(2)}, u32[]{:S(2)}) collective-permute-start(bf16[144,512]{1,0:T(8,128)(2,1)S(1)} %get-tuple-element.52), channel_id=1, source_target_pairs={{0,12},{1,13},{2,14},{3,15},{4,0},{5,1},{6,2},{7,3},{8,4},{9,5},{1... | collective-permute-start | bytes 442376 | tf_op jit(solution)/shard_map/ppermute | solution.py:37
  76.1 8.0 %collective-permute-start.23 = (bf16[144,512]{1,0:T(8,128)(2,1)S(1)}, bf16[144,512]{1,0:T(8,128)(2,1)S(1)}, u32[]{:S(2)}, u32[]{:S(2)}) collective-permute-start(bf16[144,512]{1,0:T(8,128)(2,1)S(1)} %get-tuple-element.53), channel_id=1, source_target_pairs={{0,4},{1,5},{2,6},{3,7},{4,8},{5,9},{6,10},{7,11},{8,12},{9,13},{1... | collective-permute-start | bytes 442376 | tf_op jit(solution)/shard_map/ppermute | solution.py:37
  78.1 6.6 %collective-permute-start.24 = (bf16[144,512]{1,0:T(8,128)(2,1)S(1)}, bf16[144,512]{1,0:T(8,128)(2,1)S(1)}, u32[]{:S(2)}, u32[]{:S(2)}) collective-permute-start(bf16[144,512]{1,0:T(8,128)(2,1)S(1)} %get-tuple-element.54), channel_id=1, source_target_pairs={{0,8},{1,9},{2,10},{3,11},{4,12},{5,13},{6,14},{7,15},{8,0},{9,1},... | collective-permute-start | bytes 442376 | tf_op jit(solution)/shard_map/ppermute | solution.py:37

commit v6 on v5

--- a/solution.py
+++ b/solution.py
@@ -188,6 +188,7 @@
             state_out[i : i + 1, :] = value
         return
     row_out[32:40, :] = jnp.broadcast_to(jnp.sum(picked, axis=1, keepdims=True), (8, ROWS))
+    col_out[16:, :] = jnp.zeros_like(col_out[16:, :])
     col_lse = col_high + jnp.log2(col_total)
     col_mean = col_weighted / col_total
     for j in range(2):
@@ -212,6 +213,7 @@
     row_out[0:16, :], row_out[16:32, :] = merged(refs, 16)
     row_out[32:40, :] = sum(r[32:40, :] for r in refs)
     col_out[0:8, :], col_out[8:16, :] = merged((c0, c1), 8)
+    col_out[16:, :] = jnp.zeros_like(col_out[16:, :])
 
 
 def in_parts(first, second):
@@ -373,11 +375,11 @@
     )
     row_stat, col_stat, *far_kept = call(
         functools.partial(forward_kernel, True, (2, 1)),
-        [row_shape, shape((16, ROWS), F32), kept, kept],
+        [row_shape, shape((48, ROWS), F32), kept, kept],
         *common, imgs[2], imgs[1], txt0, txt1, row_stat, state, specs=[SMEM, SMEM] + [VMEM] * 7,
     )
     kept = (near_kept[0], far_kept[1], far_kept[0], near_kept[1])
-    col_shape = shape((16, ROWS), F32)
+    col_shape = shape((48, ROWS), F32)
     row_stat, col_stat = call(
         merge_kernel, [row_shape, col_shape],
         *gathered(row_stat, ring_a), col_stat, shifted(col_stat, other_core),

time: 86.8 us -> 86.5 us (level)
  starting transfers between devices: 39 us -> 40.6 us
  waiting for transfers between devices: 21.4 us -> 19.9 us
    ppermute x28, starting transfers between devices: 39 us -> 40.6 us  [shifted(): return lax.ppermute(value, RC, pairs)]
    ppermute x28, waiting for transfers between devices: 21.4 us -> 19.9 us  [shifted(): return lax.ppermute(value, RC, pairs)]
  transfers between devices with their start and end apart: 28 -> 28, of which waited for: 13 -> 12; matrix products, arithmetic and copies ran while one was open for 1% -> 1% of each run, Pallas kernels for 15% -> 15%
where the time goes in v6:
time: 86.5 us; the launch traced here: 86.2 us
  starting transfers between devices  40.6 us (47%)
  Pallas kernels  21.7 us (25%)
  waiting for transfers between devices  19.9 us (23%)
  local copies, waits for them, and re-layouts  2.14 us (2%)
  between operations  1.69 us (2%)
    ppermute x28, starting transfers between devices, shifted(): return lax.ppermute(value, RC, pairs)  40.6 us
    pallas_call x18, Pallas kernels, call(): pl.pallas_call(kernel, out_shape=outs, in_specs=specs or [VMEM] * len(arg...  20.6 us
    ppermute x28, waiting for transfers between devices, shifted(): return lax.ppermute(value, RC, pairs)  19.9 us
    unnamed x10, local copies, waits for them, and re-layouts  1.82 us
  transfers between devices with their start and end apart: 28, of which 12 were waited for; matrix products, arithmetic and copies ran while one was open for 1% of the time, Pallas kernels for 15%

profile of v6, /device:TPU:0, one launch (start us, length us, event | category | flops | bytes accessed | tf_op | source)
XLA Modules:
  0.0 86.2 jit_solution(15919002776924954273)
XLA Ops:
  0.6 0.0 copy-start.2
  0.6 0.9 %copy-done.2 = bf16[128,512]{1,0:T(8,128)(2,1)S(1)} copy-done((bf16[128,512]{1,0:T(8,128)(2,1)S(1)}, bf16[128,512]{1,0:T(8,128)(2,1)}, u32[]{:S(2)}) %copy-start.2) | copy-done | bytes 131096
  1.5 0.1 shard_map.75.refs_0_
  1.7 3.2 %collective-permute-start.2 = (bf16[128,512]{1,0:T(8,128)(2,1)S(1)}, bf16[128,512]{1,0:T(8,128)(2,1)S(1)}, u32[]{:S(2)}, u32[]{:S(2)}) collective-permute-start(bf16[128,512]{1,0:T(8,128)(2,1)S(1)} %shard_map.75.refs_0_), channel_id=1, source_target_pairs={{0,8},{1,9},{2,10},{3,11},{4,12},{5,13},{6,14},{7,15},{8,0},{9,1},... | collective-permute-start | bytes 393224 | tf_op jit(solution)/shard_map/ppermute | solution.py:37
  4.8 1.1 %collective-permute-start.1 = (bf16[128,512]{1,0:T(8,128)(2,1)S(1)}, bf16[128,512]{1,0:T(8,128)(2,1)S(1)}, u32[]{:S(2)}, u32[]{:S(2)}) collective-permute-start(bf16[128,512]{1,0:T(8,128)(2,1)S(1)} %shard_map.75.refs_0_), channel_id=1, source_target_pairs={{0,12},{1,13},{2,14},{3,15},{4,0},{5,1},{6,2},{7,3},{8,4},{9,5},{1... | collective-permute-start | bytes 393224 | tf_op jit(solution)/shard_map/ppermute | solution.py:37
  6.0 0.9 %collective-permute-start = (bf16[128,512]{1,0:T(8,128)(2,1)S(1)}, bf16[128,512]{1,0:T(8,128)(2,1)S(1)}, u32[]{:S(2)}, u32[]{:S(2)}) collective-permute-start(bf16[128,512]{1,0:T(8,128)(2,1)S(1)} %shard_map.75.refs_0_), channel_id=1, source_target_pairs={{0,4},{1,5},{2,6},{3,7},{4,8},{5,9},{6,10},{7,11},{8,12},{9,13},{1... | collective-permute-start | bytes 393224 | tf_op jit(solution)/shard_map/ppermute | solution.py:37
  6.9 0.9 %copy-done = bf16[128,512]{1,0:T(8,128)(2,1)S(1)} copy-done((bf16[128,512]{1,0:T(8,128)(2,1)S(1)}, bf16[128,512]{1,0:T(8,128)(2,1)}, u32[]{:S(2)}) %copy-start) | copy-done | bytes 131096
  7.8 0.1 shard_map.76
  7.9 4.0 %collective-permute-start.7 = (bf16[128,512]{1,0:T(8,128)(2,1)S(1)}, bf16[128,512]{1,0:T(8,128)(2,1)S(1)}, u32[]{:S(2)}, u32[]{:S(2)}) collective-permute-start(bf16[128,512]{1,0:T(8,128)(2,1)S(1)} %shard_map.76), channel_id=1, source_target_pairs={{0,64},{1,65},{2,66},{3,67},{4,68},{5,69},{6,70},{7,71},{8,72},{9,... | collective-permute-start | bytes 393224 | tf_op jit(solution)/shard_map/ppermute | solution.py:37
  11.8 0.7 collective-permute-start.6
  12.6 1.3 %collective-permute-start.5 = (bf16[128,512]{1,0:T(8,128)(2,1)S(1)}, bf16[128,512]{1,0:T(8,128)(2,1)S(1)}, u32[]{:S(2)}, u32[]{:S(2)}) collective-permute-start(bf16[128,512]{1,0:T(8,128)(2,1)S(1)} %shard_map.76), channel_id=1, source_target_pairs={{0,32},{1,33},{2,34},{3,35},{4,36},{5,37},{6,38},{7,39},{8,40},{9,... | collective-permute-start | bytes 393224 | tf_op jit(solution)/shard_map/ppermute | solution.py:37
  13.9 3.3 %collective-permute-start.9 = (bf16[512,512]{1,0:T(8,128)(2,1)S(1)}, bf16[512,512]{1,0:T(8,128)(2,1)S(1)}, u32[]{:S(2)}, u32[]{:S(2)}) collective-permute-start(bf16[512,512]{1,0:T(8,128)(2,1)S(1)} %pad_maximum_fusion.refs_1_.i0), channel_id=1, source_target_pairs={{0,2},{1,3},{2,0},{3,1},{4,6},{5,7},{6,4},{7,5},{8,10},{9,11},{10,... | collective-permute-start | bytes 1572872 | tf_op jit(solution)/shard_map/ppermute | solution.py:37
  17.2 0.0 collective-permute-done.7
  17.2 1.1 %collective-permute-done.6 = bf16[128,512]{1,0:T(8,128)(2,1)S(1)} collective-permute-done((bf16[128,512]{1,0:T(8,128)(2,1)S(1)}, bf16[128,512]{1,0:T(8,128)(2,1)S(1)}, u32[]{:S(2)}, u32[]{:S(2)}) %collective-permute-start.6) | collective-permute-done | bytes 131104 | tf_op jit(solution)/shard_map/ppermute | solution.py:37
  18.3 0.5 collective-permute-done.5
  18.8 0.1 collective-permute-start.8
  18.9 1.6 %collective-permute-start.4 = (bf16[512,512]{1,0:T(8,128)(2,1)S(1)}, bf16[512,512]{1,0:T(8,128)(2,1)S(1)}, u32[]{:S(2)}, u32[]{:S(2)}) collective-permute-start(bf16[512,512]{1,0:T(8,128)(2,1)S(1)} %pad_maximum_fusion.refs_1_.i0), channel_id=1, source_target_pairs={{0,1},{1,2},{2,3},{3,0},{4,5},{5,6},{6,7},{7,4},{8,9},{9,10},{10,1... | collective-permute-start | bytes 1572872 | tf_op jit(solution)/shard_map/ppermute | solution.py:37
  20.5 1.7 %collective-permute-start.3 = (bf16[512,512]{1,0:T(8,128)(2,1)S(1)}, bf16[512,512]{1,0:T(8,128)(2,1)S(1)}, u32[]{:S(2)}, u32[]{:S(2)}) collective-permute-start(bf16[512,512]{1,0:T(8,128)(2,1)S(1)} %pad_maximum_fusion.refs_1_.i0), channel_id=1, source_target_pairs={{0,3},{1,0},{2,1},{3,2},{4,7},{5,4},{6,5},{7,6},{8,11},{9,8},{10,9... | collective-permute-start | bytes 1572872 | tf_op jit(solution)/shard_map/ppermute | solution.py:37
  22.9 0.1 pad_add_fusion.ids_ref
  23.0 1.8 %collective-permute-done.9.refs_0_.refs_2_.i3 = bf16[512,512]{1,0:T(8,128)(2,1)S(1)} collective-permute-done((bf16[512,512]{1,0:T(8,128)(2,1)S(1)}, bf16[512,512]{1,0:T(8,128)(2,1)S(1)}, u32[]{:S(2)}, u32[]{:S(2)}) %collective-permute-start.9) | collective-permute-done | bytes 524320 | tf_op jit(solution)/shard_map/ppermute | solution.py:37
  24.8 0.0 collective-permute-done.8.refs_4_.t1
  24.8 0.3 broadcast_in_dim.8.refs_0_
  25.1 4.4 %shard_map.78 = (f32[40,128]{1,0:T(8,128)S(1)}, f32[8,1024]{1,0:T(8,128)S(1)}, f32[512,1024]{1,0:T(8,128)S(1)}, f32[512,1024]{1,0:T(8,128)S(1)}) custom-call(s32[2]{0:T(128)S(1)} %pad_add_fusion.ids_ref, f32[1]{0:T(128)S(6)} %exp.3.scale_ref, s32[2048,128]{1,0:T(8,128)S(1)} %broadcast_in_dim.8.refs_0_, bf16[512,512]{1,0:T(8,128)(2,1)S(1)} %pad_maximum_fusion.refs_1_.i0, ...), custom_call_target="tpu_custom_call" | custom-call | tf_op jit(solution)/shard_map/pallas_call | solution.py:57
  29.5 0.8 collective-permute-done.4.refs_2_.i1
  30.3 0.3 collective-permute-done.3.refs_1_.i2
  30.6 5.0 %shard_map.79 = (f32[40,128]{1,0:T(8,128)S(1)}, f32[48,128]{1,0:T(8,128)S(1)}, f32[512,1024]{1,0:T(8,128)S(1)}, f32[512,1024]{1,0:T(8,128)S(1)}) custom-call(s32[2]{0:T(128)S(1)} %pad_add_fusion.ids_ref, f32[1]{0:T(128)S(6)} %exp.3.scale_ref, s32[2048,128]{1,0:T(8,128)S(1)} %broadcast_in_dim.8.refs_0_, ...), custom_call_target="tpu_custom_call" | custom-call | tf_op jit(solution)/shard_map/pallas_call | solution.py:57
  35.6 0.1 collective-permute-start.13
  35.7 0.8 collective-permute-start.12
  36.5 2.5 %collective-permute-start.11 = (f32[40,128]{1,0:T(8,128)S(1)}, f32[40,128]{1,0:T(8,128)S(1)}, u32[]{:S(2)}, u32[]{:S(2)}) collective-permute-start(f32[40,128]{1,0:T(8,128)S(1)} %get-tuple-element.33.refs_0_), channel_id=1, source_target_pairs={{0,12},{1,13},{2,14},{3,15},{4,0},{5,1},{6,2},{7,3},{8,4},{9,5},{1... | collective-permute-start | bytes 61448 | tf_op jit(solution)/shard_map/ppermute | solution.py:37
  39.1 2.0 %collective-permute-done.12.refs_3_ = f32[40,128]{1,0:T(8,128)S(1)} collective-permute-done((f32[40,128]{1,0:T(8,128)S(1)}, f32[40,128]{1,0:T(8,128)S(1)}, u32[]{:S(2)}, u32[]{:S(2)}) %collective-permute-start.12) | collective-permute-done | bytes 20512 | tf_op jit(solution)/shard_map/ppermute | solution.py:37
  41.1 3.0 %collective-permute-done.10.refs_1_ = f32[40,128]{1,0:T(8,128)S(1)} collective-permute-done((f32[40,128]{1,0:T(8,128)S(1)}, f32[40,128]{1,0:T(8,128)S(1)}, u32[]{:S(2)}, u32[]{:S(2)}) %collective-permute-start.10) | collective-permute-done | bytes 20512 | tf_op jit(solution)/shard_map/ppermute | solution.py:37
  44.1 1.1 %collective-permute-start.15 = (f32[48,128]{1,0:T(8,128)S(1)}, f32[48,128]{1,0:T(8,128)S(1)}, u32[]{:S(2)}, u32[]{:S(2)}) collective-permute-start(f32[48,128]{1,0:T(8,128)S(1)} %get-tuple-element.36.refs_2_), channel_id=1, source_target_pairs={{0,32},{1,33},{2,34},{3,35},{4,36},{5,37},{6,38},{7,39},{8,40},{9,... | collective-permute-start | bytes 73736 | tf_op jit(solution)/shard_map/ppermute | solution.py:37
  45.2 1.4 %collective-permute-start.14 = (f32[40,128]{1,0:T(8,128)S(1)}, f32[40,128]{1,0:T(8,128)S(1)}, u32[]{:S(2)}, u32[]{:S(2)}) collective-permute-start(f32[40,128]{1,0:T(8,128)S(1)} %get-tuple-element.35.refs_0_), channel_id=1, source_target_pairs={{0,1},{1,0},{2,3},{3,2},{4,5},{5,4},{6,7},{7,6},{8,9},{9,8},{10,11... | collective-permute-start | bytes 61448 | tf_op jit(solution)/shard_map/ppermute | solution.py:37
  46.6 2.4 %collective-permute-done.14.refs_1_ = f32[40,128]{1,0:T(8,128)S(1)} collective-permute-done((f32[40,128]{1,0:T(8,128)S(1)}, f32[40,128]{1,0:T(8,128)S(1)}, u32[]{:S(2)}, u32[]{:S(2)}) %collective-permute-start.14) | collective-permute-done | bytes 20512 | tf_op jit(solution)/shard_map/ppermute | solution.py:37
  49.0 1.2 %collective-permute-start.17 = (f32[48,128]{1,0:T(8,128)S(1)}, f32[48,128]{1,0:T(8,128)S(1)}, u32[]{:S(2)}, u32[]{:S(2)}) collective-permute-start(f32[48,128]{1,0:T(8,128)S(1)} %get-tuple-element.38.c0), channel_id=1, source_target_pairs={{0,96},{1,97},{2,98},{3,99},{4,100},{5,101},{6,102},{7,103},{8,104... | collective-permute-start | bytes 73736 | tf_op jit(solution)/shard_map/ppermute | solution.py:37
  50.2 3.2 %collective-permute-start.16 = (f32[40,128]{1,0:T(8,128)S(1)}, f32[40,128]{1,0:T(8,128)S(1)}, u32[]{:S(2)}, u32[]{:S(2)}) collective-permute-start(f32[40,128]{1,0:T(8,128)S(1)} %get-tuple-element.37.r0), channel_id=1, source_target_pairs={{0,3},{1,2},{2,1},{3,0},{4,7},{5,6},{6,5},{7,4},{8,11},{9,10},{10,... | collective-permute-start | bytes 61448 | tf_op jit(solution)/shard_map/ppermute | solution.py:37
  53.4 1.8 %collective-permute-done.16.r1 = f32[40,128]{1,0:T(8,128)S(1)} collective-permute-done((f32[40,128]{1,0:T(8,128)S(1)}, f32[40,128]{1,0:T(8,128)S(1)}, u32[]{:S(2)}, u32[]{:S(2)}) %collective-permute-start.16) | collective-permute-done | bytes 20512 | tf_op jit(solution)/shard_map/ppermute | solution.py:37
  55.2 0.7 shard_map.82
  55.9 1.3 %shard_map.84.d_ref.d3 = bf16[512,1024]{1,0:T(8,128)(2,1)S(1)} custom-call(s32[2]{0:T(128)S(1)} %pad_add_fusion.ids_ref, f32[1]{0:T(128)S(6)} %exp.3.scale_ref, s32[2048,128]{1,0:T(8,128)S(1)} %broadcast_in_dim.8.refs_0_, f32[16,128]{1,0:T(8,128)S(1)} %get-tuple-element.40.refs_1_, f32[1,1024]{1,0:T(1,128)S(1)} %get-tuple-element.41.refs_2_, ...), custom_call_target="tpu_custom_call" | custom-call | flops 10000000000 | bytes 1000000 | tf_op jit(solution)/shard_map/pallas_call | solution.py:57
  57.2 0.7 shard_map.87.refs_2_
  57.9 1.9 %collective-permute-start.21 = (bf16[528,512]{1,0:T(8,128)(2,1)S(1)}, bf16[528,512]{1,0:T(8,128)(2,1)S(1)}, u32[]{:S(2)}, u32[]{:S(2)}) collective-permute-start(bf16[528,512]{1,0:T(8,128)(2,1)S(1)} %shard_map.87.refs_2_), channel_id=1, source_target_pairs={{0,2},{1,3},{2,0},{3,1},{4,6},{5,7},{6,4},{7,5},{8,10},{9,11},{10,... | collective-permute-start | bytes 1622024 | tf_op jit(solution)/shard_map/ppermute | solution.py:37
  59.8 2.5 %shard_map.83 = (bf16[512,1024]{1,0:T(8,128)(2,1)S(1)}, bf16[512,1024]{1,0:T(8,128)(2,1)S(1)}, bf16[512,1024]{1,0:T(8,128)(2,1)S(1)}) custom-call(s32[2]{0:T(128)S(1)} %pad_add_fusion.ids_ref, f32[1]{0:T(128)S(6)} %exp.3.scale_ref, s32[2048,128]{1,0:T(8,128)S(1)} %broadcast_in_dim.8.refs_0_, f32[16,128]{1,0:T(8,128)S(1)} %get-tuple-element.40.refs_1_, ...), custom_call_target="tpu_custom_call" | custom-call | flops 10000000000 | bytes 1000000 | tf_op jit(solution)/shard_map/pallas_call | solution.py:57
  62.3 0.7 shard_map.86.refs_1_
  63.0 2.6 %collective-permute-start.20 = (bf16[528,512]{1,0:T(8,128)(2,1)S(1)}, bf16[528,512]{1,0:T(8,128)(2,1)S(1)}, u32[]{:S(2)}, u32[]{:S(2)}) collective-permute-start(bf16[528,512]{1,0:T(8,128)(2,1)S(1)} %shard_map.86.refs_1_), channel_id=1, source_target_pairs={{0,1},{1,2},{2,3},{3,0},{4,5},{5,6},{6,7},{7,4},{8,9},{9,10},{10,1... | collective-permute-start | bytes 1622024 | tf_op jit(solution)/shard_map/ppermute | solution.py:37
  65.6 0.7 shard_map.85.refs_0_
  66.3 1.0 %collective-permute-start.19 = (bf16[528,512]{1,0:T(8,128)(2,1)S(1)}, bf16[528,512]{1,0:T(8,128)(2,1)S(1)}, u32[]{:S(2)}, u32[]{:S(2)}) collective-permute-start(bf16[528,512]{1,0:T(8,128)(2,1)S(1)} %shard_map.85.refs_0_), channel_id=1, source_target_pairs={{0,3},{1,0},{2,1},{3,2},{4,7},{5,4},{6,5},{7,6},{8,11},{9,8},{10,9... | collective-permute-start | bytes 1622024 | tf_op jit(solution)/shard_map/ppermute | solution.py:37
  67.3 1.5 %shard_map.88.refs_0_ = bf16[528,512]{1,0:T(8,128)(2,1)S(1)} custom-call(f32[1]{0:T(128)S(6)} %exp.3.scale_ref, bf16[16,512]{1,0:T(8,128)(2,1)S(1)} %get-tuple-element.39.row_tail, bf16[512,512]{1,0:T(8,128)(2,1)S(1)} %pad_maximum_fusion.refs_1_.i0, bf16[512,512]{1,0:T(8,128)(2,1)S(1)} %collective-permute-done.4.refs_2_.i1, ...), custom_call_target="tpu_custom_call" | custom-call | flops 10000000000 | bytes 1000000 | tf_op jit(solution)/shard_map/pallas_call | solution.py:57
  68.9 0.1 collective-permute-start.18
  69.0 1.5 %shard_map.89.refs_0_ = bf16[528,512]{1,0:T(8,128)(2,1)S(1)} custom-call(f32[1]{0:T(128)S(6)} %exp.3.scale_ref, bf16[16,512]{1,0:T(8,128)(2,1)S(1)} %get-tuple-element.39.row_tail, bf16[512,512]{1,0:T(8,128)(2,1)S(1)} %pad_maximum_fusion.refs_1_.i0, bf16[512,512]{1,0:T(8,128)(2,1)S(1)} %collective-permute-done.4.refs_2_.i1, ...), custom_call_target="tpu_custom_call" | custom-call | flops 10000000000 | bytes 1000000 | tf_op jit(solution)/shard_map/pallas_call | solution.py:57
  70.5 0.4 collective-permute-done.18.refs_1_
  70.9 0.2 shard_map.90
  71.1 2.0 %collective-permute-start.25 = (bf16[144,512]{1,0:T(8,128)(2,1)S(1)}, bf16[144,512]{1,0:T(8,128)(2,1)S(1)}, u32[]{:S(2)}, u32[]{:S(2)}) collective-permute-start(bf16[144,512]{1,0:T(8,128)(2,1)S(1)} %get-tuple-element.55), channel_id=1, source_target_pairs={{0,96},{1,97},{2,98},{3,99},{4,100},{5,101},{6,102},{7,103},{8,104... | collective-permute-start | bytes 442376 | tf_op jit(solution)/shard_map/ppermute | solution.py:37
  73.1 0.7 shard_map.91.refs_0_
  73.8 0.0 copy-start.1
  73.8 0.0 copy-start.3
  73.8 0.1 collective-permute-start.26
  74.0 1.8 %collective-permute-start.27 = (bf16[144,512]{1,0:T(8,128)(2,1)S(1)}, bf16[144,512]{1,0:T(8,128)(2,1)S(1)}, u32[]{:S(2)}, u32[]{:S(2)}) collective-permute-start(bf16[144,512]{1,0:T(8,128)(2,1)S(1)} %get-tuple-element.57), channel_id=1, source_target_pairs={{0,64},{1,65},{2,66},{3,67},{4,68},{5,69},{6,70},{7,71},{8,72},{9,... | collective-permute-start | bytes 442376 | tf_op jit(solution)/shard_map/ppermute | solution.py:37
  75.8 0.4 shard_map.92
  76.1 0.1 collective-permute-start.22
  76.2 2.0 %collective-permute-start.23 = (bf16[144,512]{1,0:T(8,128)(2,1)S(1)}, bf16[144,512]{1,0:T(8,128)(2,1)S(1)}, u32[]{:S(2)}, u32[]{:S(2)}) collective-permute-start(bf16[144,512]{1,0:T(8,128)(2,1)S(1)} %get-tuple-element.53), channel_id=1, source_target_pairs={{0,4},{1,5},{2,6},{3,7},{4,8},{5,9},{6,10},{7,11},{8,12},{9,13},{1... | collective-permute-start | bytes 442376 | tf_op jit(solution)/shard_map/ppermute | solution.py:37
  78.2 0.8 collective-permute-start.24
  79.1 4.8 %collective-permute-done.26.b2 = bf16[144,512]{1,0:T(8,128)(2,1)S(1)} collective-permute-done((bf16[144,512]{1,0:T(8,128)(2,1)S(1)}, bf16[144,512]{1,0:T(8,128)(2,1)S(1)}, u32[]{:S(2)}, u32[]{:S(2)}) %collective-permute-start.26) | collective-permute-done | bytes 147488 | tf_op jit(solution)/shard_map/ppermute | solution.py:37
  83.9 1.0 %collective-permute-done.24.a3 = bf16[144,512]{1,0:T(8,128)(2,1)S(1)} collective-permute-done((bf16[144,512]{1,0:T(8,128)(2,1)S(1)}, bf16[144,512]{1,0:T(8,128)(2,1)S(1)}, u32[]{:S(2)}, u32[]{:S(2)}) %collective-permute-start.24) | collective-permute-done | bytes 147488 | tf_op jit(solution)/shard_map/ppermute | solution.py:37
  84.9 1.1 %shard_map.93 = (f32[128,512]{1,0:T(8,128)}, f32[128,512]{1,0:T(8,128)}, f32[1]{0:T(128)}, f32[1]{0:T(128)}) custom-call(bf16[128,512]{1,0:T(8,128)(2,1)S(1)} %copy-done.3, bf16[128,512]{1,0:T(8,128)(2,1)S(1)} %copy-done.1, bf16[144,512]{1,0:T(8,128)(2,1)S(1)} %get-tuple-element.51.a0, bf16[144,512]{1,0:T(8,128)(2,1)S(1)} %collective-permute-done.22.a1, ...), custom_call_target="tpu_custom_call" | custom-call | tf_op jit(solution)/shard_map/pallas_call | solution.py:433
  (26 shorter events, 0.2 us)
Async XLA Ops:
  0.6 0.9 %copy-start.2 = (bf16[128,512]{1,0:T(8,128)(2,1)S(1)}, bf16[128,512]{1,0:T(8,128)(2,1)}, u32[]{:S(2)}) copy-start(bf16[128,512]{1,0:T(8,128)(2,1)} %img_ref.1) | copy-start | bytes 393220
  1.5 21.4 %copy-start.4 = (s32[2048]{0:T(1024)S(1)}, s32[2048]{0:T(1024)}, u32[]{:S(2)}) copy-start(s32[2048]{0:T(1024)} %param.6) | copy-start | bytes 24580
  1.7 10.9 %collective-permute-start.2 = (bf16[128,512]{1,0:T(8,128)(2,1)S(1)}, bf16[128,512]{1,0:T(8,128)(2,1)S(1)}, u32[]{:S(2)}, u32[]{:S(2)}) collective-permute-start(bf16[128,512]{1,0:T(8,128)(2,1)S(1)} %shard_map.75.refs_0_), channel_id=1, source_target_pairs={{0,8},{1,9},{2,10},{3,11},{4,12},{5,13},{6,14},{7,15},{8,0},{9,1},... | collective-permute-start | bytes 393224 | tf_op jit(solution)/shard_map/ppermute | solution.py:37
  4.8 9.0 %collective-permute-start.1 = (bf16[128,512]{1,0:T(8,128)(2,1)S(1)}, bf16[128,512]{1,0:T(8,128)(2,1)S(1)}, u32[]{:S(2)}, u32[]{:S(2)}) collective-permute-start(bf16[128,512]{1,0:T(8,128)(2,1)S(1)} %shard_map.75.refs_0_), channel_id=1, source_target_pairs={{0,12},{1,13},{2,14},{3,15},{4,0},{5,1},{6,2},{7,3},{8,4},{9,5},{1... | collective-permute-start | bytes 393224 | tf_op jit(solution)/shard_map/ppermute | solution.py:37
  6.0 7.9 %collective-permute-start = (bf16[128,512]{1,0:T(8,128)(2,1)S(1)}, bf16[128,512]{1,0:T(8,128)(2,1)S(1)}, u32[]{:S(2)}, u32[]{:S(2)}) collective-permute-start(bf16[128,512]{1,0:T(8,128)(2,1)S(1)} %shard_map.75.refs_0_), channel_id=1, source_target_pairs={{0,4},{1,5},{2,6},{3,7},{4,8},{5,9},{6,10},{7,11},{8,12},{9,13},{1... | collective-permute-start | bytes 393224 | tf_op jit(solution)/shard_map/ppermute | solution.py:37
  6.9 0.9 %copy-start = (bf16[128,512]{1,0:T(8,128)(2,1)S(1)}, bf16[128,512]{1,0:T(8,128)(2,1)}, u32[]{:S(2)}) copy-start(bf16[128,512]{1,0:T(8,128)(2,1)} %txt_ref.1) | copy-start | bytes 393220
  7.9 9.3 %collective-permute-start.7 = (bf16[128,512]{1,0:T(8,128)(2,1)S(1)}, bf16[128,512]{1,0:T(8,128)(2,1)S(1)}, u32[]{:S(2)}, u32[]{:S(2)}) collective-permute-start(bf16[128,512]{1,0:T(8,128)(2,1)S(1)} %shard_map.76), channel_id=1, source_target_pairs={{0,64},{1,65},{2,66},{3,67},{4,68},{5,69},{6,70},{7,71},{8,72},{9,... | collective-permute-start | bytes 393224 | tf_op jit(solution)/shard_map/ppermute | solution.py:37
  11.8 6.4 %collective-permute-start.6 = (bf16[128,512]{1,0:T(8,128)(2,1)S(1)}, bf16[128,512]{1,0:T(8,128)(2,1)S(1)}, u32[]{:S(2)}, u32[]{:S(2)}) collective-permute-start(bf16[128,512]{1,0:T(8,128)(2,1)S(1)} %shard_map.76), channel_id=1, source_target_pairs={{0,96},{1,97},{2,98},{3,99},{4,100},{5,101},{6,102},{7,103},{8,104... | collective-permute-start | bytes 393224 | tf_op jit(solution)/shard_map/ppermute | solution.py:37
  12.6 6.2 %collective-permute-start.5 = (bf16[128,512]{1,0:T(8,128)(2,1)S(1)}, bf16[128,512]{1,0:T(8,128)(2,1)S(1)}, u32[]{:S(2)}, u32[]{:S(2)}) collective-permute-start(bf16[128,512]{1,0:T(8,128)(2,1)S(1)} %shard_map.76), channel_id=1, source_target_pairs={{0,32},{1,33},{2,34},{3,35},{4,36},{5,37},{6,38},{7,39},{8,40},{9,... | collective-permute-start | bytes 393224 | tf_op jit(solution)/shard_map/ppermute | solution.py:37
  13.9 10.9 %collective-permute-start.9 = (bf16[512,512]{1,0:T(8,128)(2,1)S(1)}, bf16[512,512]{1,0:T(8,128)(2,1)S(1)}, u32[]{:S(2)}, u32[]{:S(2)}) collective-permute-start(bf16[512,512]{1,0:T(8,128)(2,1)S(1)} %pad_maximum_fusion.refs_1_.i0), channel_id=1, source_target_pairs={{0,2},{1,3},{2,0},{3,1},{4,6},{5,7},{6,4},{7,5},{8,10},{9,11},{10,... | collective-permute-start | bytes 1572872 | tf_op jit(solution)/shard_map/ppermute | solution.py:37
  18.8 6.0 %collective-permute-start.8 = (bf16[512,512]{1,0:T(8,128)(2,1)S(1)}, bf16[512,512]{1,0:T(8,128)(2,1)S(1)}, u32[]{:S(2)}, u32[]{:S(2)}) collective-permute-start(bf16[512,512]{1,0:T(8,128)(2,1)S(1)} %pad_maximum_fusion.1.refs_3_.t0), channel_id=1, source_target_pairs={{0,16},{1,17},{2,18},{3,19},{4,20},{5,21},{6,22},{7,23},{8,24},{9,... | collective-permute-start | bytes 1572872 | tf_op jit(solution)/shard_map/ppermute | solution.py:37
  18.9 11.4 %collective-permute-start.4 = (bf16[512,512]{1,0:T(8,128)(2,1)S(1)}, bf16[512,512]{1,0:T(8,128)(2,1)S(1)}, u32[]{:S(2)}, u32[]{:S(2)}) collective-permute-start(bf16[512,512]{1,0:T(8,128)(2,1)S(1)} %pad_maximum_fusion.refs_1_.i0), channel_id=1, source_target_pairs={{0,1},{1,2},{2,3},{3,0},{4,5},{5,6},{6,7},{7,4},{8,9},{9,10},{10,1... | collective-permute-start | bytes 1572872 | tf_op jit(solution)/shard_map/ppermute | solution.py:37
  20.5 10.1 %collective-permute-start.3 = (bf16[512,512]{1,0:T(8,128)(2,1)S(1)}, bf16[512,512]{1,0:T(8,128)(2,1)S(1)}, u32[]{:S(2)}, u32[]{:S(2)}) collective-permute-start(bf16[512,512]{1,0:T(8,128)(2,1)S(1)} %pad_maximum_fusion.refs_1_.i0), channel_id=1, source_target_pairs={{0,3},{1,0},{2,1},{3,2},{4,7},{5,4},{6,5},{7,6},{8,11},{9,8},{10,9... | collective-permute-start | bytes 1572872 | tf_op jit(solution)/shard_map/ppermute | solution.py:37
  35.6 8.4 %collective-permute-start.13 = (f32[48,128]{1,0:T(8,128)S(1)}, f32[48,128]{1,0:T(8,128)S(1)}, u32[]{:S(2)}, u32[]{:S(2)}) collective-permute-start(f32[48,128]{1,0:T(8,128)S(1)} %get-tuple-element.34.refs_4_), channel_id=1, source_target_pairs={{0,16},{1,17},{2,18},{3,19},{4,20},{5,21},{6,22},{7,23},{8,24},{9,... | collective-permute-start | bytes 73736 | tf_op jit(solution)/shard_map/ppermute | solution.py:37
  35.7 5.4 %collective-permute-start.12 = (f32[40,128]{1,0:T(8,128)S(1)}, f32[40,128]{1,0:T(8,128)S(1)}, u32[]{:S(2)}, u32[]{:S(2)}) collective-permute-start(f32[40,128]{1,0:T(8,128)S(1)} %get-tuple-element.33.refs_0_), channel_id=1, source_target_pairs={{0,8},{1,9},{2,10},{3,11},{4,12},{5,13},{6,14},{7,15},{8,0},{9,1},... | collective-permute-start | bytes 61448 | tf_op jit(solution)/shard_map/ppermute | solution.py:37
  36.5 4.5 %collective-permute-start.11 = (f32[40,128]{1,0:T(8,128)S(1)}, f32[40,128]{1,0:T(8,128)S(1)}, u32[]{:S(2)}, u32[]{:S(2)}) collective-permute-start(f32[40,128]{1,0:T(8,128)S(1)} %get-tuple-element.33.refs_0_), channel_id=1, source_target_pairs={{0,12},{1,13},{2,14},{3,15},{4,0},{5,1},{6,2},{7,3},{8,4},{9,5},{1... | collective-permute-start | bytes 61448 | tf_op jit(solution)/shard_map/ppermute | solution.py:37
  39.0 5.0 %collective-permute-start.10 = (f32[40,128]{1,0:T(8,128)S(1)}, f32[40,128]{1,0:T(8,128)S(1)}, u32[]{:S(2)}, u32[]{:S(2)}) collective-permute-start(f32[40,128]{1,0:T(8,128)S(1)} %get-tuple-element.33.refs_0_), channel_id=1, source_target_pairs={{0,4},{1,5},{2,6},{3,7},{4,8},{5,9},{6,10},{7,11},{8,12},{9,13},{1... | collective-permute-start | bytes 61448 | tf_op jit(solution)/shard_map/ppermute | solution.py:37
  44.1 4.9 %collective-permute-start.15 = (f32[48,128]{1,0:T(8,128)S(1)}, f32[48,128]{1,0:T(8,128)S(1)}, u32[]{:S(2)}, u32[]{:S(2)}) collective-permute-start(f32[48,128]{1,0:T(8,128)S(1)} %get-tuple-element.36.refs_2_), channel_id=1, source_target_pairs={{0,32},{1,33},{2,34},{3,35},{4,36},{5,37},{6,38},{7,39},{8,40},{9,... | collective-permute-start | bytes 73736 | tf_op jit(solution)/shard_map/ppermute | solution.py:37
  45.2 3.8 %collective-permute-start.14 = (f32[40,128]{1,0:T(8,128)S(1)}, f32[40,128]{1,0:T(8,128)S(1)}, u32[]{:S(2)}, u32[]{:S(2)}) collective-permute-start(f32[40,128]{1,0:T(8,128)S(1)} %get-tuple-element.35.refs_0_), channel_id=1, source_target_pairs={{0,1},{1,0},{2,3},{3,2},{4,5},{5,4},{6,7},{7,6},{8,9},{9,8},{10,11... | collective-permute-start | bytes 61448 | tf_op jit(solution)/shard_map/ppermute | solution.py:37
  49.0 6.2 %collective-permute-start.17 = (f32[48,128]{1,0:T(8,128)S(1)}, f32[48,128]{1,0:T(8,128)S(1)}, u32[]{:S(2)}, u32[]{:S(2)}) collective-permute-start(f32[48,128]{1,0:T(8,128)S(1)} %get-tuple-element.38.c0), channel_id=1, source_target_pairs={{0,96},{1,97},{2,98},{3,99},{4,100},{5,101},{6,102},{7,103},{8,104... | collective-permute-start | bytes 73736 | tf_op jit(solution)/shard_map/ppermute | solution.py:37
  50.2 5.0 %collective-permute-start.16 = (f32[40,128]{1,0:T(8,128)S(1)}, f32[40,128]{1,0:T(8,128)S(1)}, u32[]{:S(2)}, u32[]{:S(2)}) collective-permute-start(f32[40,128]{1,0:T(8,128)S(1)} %get-tuple-element.37.r0), channel_id=1, source_target_pairs={{0,3},{1,2},{2,1},{3,0},{4,7},{5,6},{6,5},{7,4},{8,11},{9,10},{10,... | collective-permute-start | bytes 61448 | tf_op jit(solution)/shard_map/ppermute | solution.py:37
  57.9 16.1 %collective-permute-start.21 = (bf16[528,512]{1,0:T(8,128)(2,1)S(1)}, bf16[528,512]{1,0:T(8,128)(2,1)S(1)}, u32[]{:S(2)}, u32[]{:S(2)}) collective-permute-start(bf16[528,512]{1,0:T(8,128)(2,1)S(1)} %shard_map.87.refs_2_), channel_id=1, source_target_pairs={{0,2},{1,3},{2,0},{3,1},{4,6},{5,7},{6,4},{7,5},{8,10},{9,11},{10,... | collective-permute-start | bytes 1622024 | tf_op jit(solution)/shard_map/ppermute | solution.py:37
  63.0 12.8 %collective-permute-start.20 = (bf16[528,512]{1,0:T(8,128)(2,1)S(1)}, bf16[528,512]{1,0:T(8,128)(2,1)S(1)}, u32[]{:S(2)}, u32[]{:S(2)}) collective-permute-start(bf16[528,512]{1,0:T(8,128)(2,1)S(1)} %shard_map.86.refs_1_), channel_id=1, source_target_pairs={{0,1},{1,2},{2,3},{3,0},{4,5},{5,6},{6,7},{7,4},{8,9},{9,10},{10,1... | collective-permute-start | bytes 1622024 | tf_op jit(solution)/shard_map/ppermute | solution.py:37
  66.3 9.4 %collective-permute-start.19 = (bf16[528,512]{1,0:T(8,128)(2,1)S(1)}, bf16[528,512]{1,0:T(8,128)(2,1)S(1)}, u32[]{:S(2)}, u32[]{:S(2)}) collective-permute-start(bf16[528,512]{1,0:T(8,128)(2,1)S(1)} %shard_map.85.refs_0_), channel_id=1, source_target_pairs={{0,3},{1,0},{2,1},{3,2},{4,7},{5,4},{6,5},{7,6},{8,11},{9,8},{10,9... | collective-permute-start | bytes 1622024 | tf_op jit(solution)/shard_map/ppermute | solution.py:37
  68.9 2.0 %collective-permute-start.18 = (bf16[528,512]{1,0:T(8,128)(2,1)S(1)}, bf16[528,512]{1,0:T(8,128)(2,1)S(1)}, u32[]{:S(2)}, u32[]{:S(2)}) collective-permute-start(bf16[528,512]{1,0:T(8,128)(2,1)S(1)} %shard_map.88.refs_0_), channel_id=1, source_target_pairs={{0,16},{1,17},{2,18},{3,19},{4,20},{5,21},{6,22},{7,23},{8,24},{9,... | collective-permute-start | bytes 1622024 | tf_op jit(solution)/shard_map/ppermute | solution.py:37
  71.1 7.2 %collective-permute-start.25 = (bf16[144,512]{1,0:T(8,128)(2,1)S(1)}, bf16[144,512]{1,0:T(8,128)(2,1)S(1)}, u32[]{:S(2)}, u32[]{:S(2)}) collective-permute-start(bf16[144,512]{1,0:T(8,128)(2,1)S(1)} %get-tuple-element.55), channel_id=1, source_target_pairs={{0,96},{1,97},{2,98},{3,99},{4,100},{5,101},{6,102},{7,103},{8,104... | collective-permute-start | bytes 442376 | tf_op jit(solution)/shard_map/ppermute | solution.py:37
  73.8 11.1 %copy-start.1 = (bf16[128,512]{1,0:T(8,128)(2,1)S(1)}, bf16[128,512]{1,0:T(8,128)(2,1)}, u32[]{:S(2)}) copy-start(bf16[128,512]{1,0:T(8,128)(2,1)} %txt_ref.1) | copy-start | bytes 393220
  73.8 11.1 %copy-start.3 = (bf16[128,512]{1,0:T(8,128)(2,1)S(1)}, bf16[128,512]{1,0:T(8,128)(2,1)}, u32[]{:S(2)}) copy-start(bf16[128,512]{1,0:T(8,128)(2,1)} %img_ref.1) | copy-start | bytes 393220
  73.8 10.0 %collective-permute-start.26 = (bf16[144,512]{1,0:T(8,128)(2,1)S(1)}, bf16[144,512]{1,0:T(8,128)(2,1)S(1)}, u32[]{:S(2)}, u32[]{:S(2)}) collective-permute-start(bf16[144,512]{1,0:T(8,128)(2,1)S(1)} %get-tuple-element.56), channel_id=1, source_target_pairs={{0,32},{1,33},{2,34},{3,35},{4,36},{5,37},{6,38},{7,39},{8,40},{9,... | collective-permute-start | bytes 442376 | tf_op jit(solution)/shard_map/ppermute | solution.py:37
  74.0 9.9 %collective-permute-start.27 = (bf16[144,512]{1,0:T(8,128)(2,1)S(1)}, bf16[144,512]{1,0:T(8,128)(2,1)S(1)}, u32[]{:S(2)}, u32[]{:S(2)}) collective-permute-start(bf16[144,512]{1,0:T(8,128)(2,1)S(1)} %get-tuple-element.57), channel_id=1, source_target_pairs={{0,64},{1,65},{2,66},{3,67},{4,68},{5,69},{6,70},{7,71},{8,72},{9,... | collective-permute-start | bytes 442376 | tf_op jit(solution)/shard_map/ppermute | solution.py:37
  76.1 7.7 %collective-permute-start.22 = (bf16[144,512]{1,0:T(8,128)(2,1)S(1)}, bf16[144,512]{1,0:T(8,128)(2,1)S(1)}, u32[]{:S(2)}, u32[]{:S(2)}) collective-permute-start(bf16[144,512]{1,0:T(8,128)(2,1)S(1)} %get-tuple-element.52), channel_id=1, source_target_pairs={{0,12},{1,13},{2,14},{3,15},{4,0},{5,1},{6,2},{7,3},{8,4},{9,5},{1... | collective-permute-start | bytes 442376 | tf_op jit(solution)/shard_map/ppermute | solution.py:37
  76.2 7.7 %collective-permute-start.23 = (bf16[144,512]{1,0:T(8,128)(2,1)S(1)}, bf16[144,512]{1,0:T(8,128)(2,1)S(1)}, u32[]{:S(2)}, u32[]{:S(2)}) collective-permute-start(bf16[144,512]{1,0:T(8,128)(2,1)S(1)} %get-tuple-element.53), channel_id=1, source_target_pairs={{0,4},{1,5},{2,6},{3,7},{4,8},{5,9},{6,10},{7,11},{8,12},{9,13},{1... | collective-permute-start | bytes 442376 | tf_op jit(solution)/shard_map/ppermute | solution.py:37
  78.2 6.6 %collective-permute-start.24 = (bf16[144,512]{1,0:T(8,128)(2,1)S(1)}, bf16[144,512]{1,0:T(8,128)(2,1)S(1)}, u32[]{:S(2)}, u32[]{:S(2)}) collective-permute-start(bf16[144,512]{1,0:T(8,128)(2,1)S(1)} %get-tuple-element.54), channel_id=1, source_target_pairs={{0,8},{1,9},{2,10},{3,11},{4,12},{5,13},{6,14},{7,15},{8,0},{9,1},... | collective-permute-start | bytes 442376 | tf_op jit(solution)/shard_map/ppermute | solution.py:37

commit v7 on v6

--- a/solution.py
+++ b/solution.py
@@ -350,7 +350,7 @@
     anywhere = pl.BlockSpec(memory_space=pl.ANY)
     token = shape((8, ROWS), F32)
     unit_img = call(unit_kernel, unit, images)
-    unit_txt = call(unit_kernel, unit, texts, unit_img, specs=[VMEM, anywhere])
+    unit_txt = call(unit_kernel, unit, texts)
     img_own = jnp.concatenate(gathered(unit_img, ring_a), axis=0)
     txt0 = jnp.concatenate(gathered(unit_txt, ring_z), axis=0)
     imgs = gathered(img_own, ring_b)

time: 86.5 us -> 86.5 us (level)
  no operation moved by 1% of the time
where the time goes in v7:
time: 86.5 us; the launch traced here: 86.2 us
  starting transfers between devices  40.6 us (47%)
  Pallas kernels  21.7 us (25%)
  waiting for transfers between devices  19.9 us (23%)
  local copies, waits for them, and re-layouts  2.14 us (2%)
  between operations  1.69 us (2%)
    ppermute x28, starting transfers between devices, shifted(): return lax.ppermute(value, RC, pairs)  40.6 us
    pallas_call x18, Pallas kernels, call(): pl.pallas_call(kernel, out_shape=outs, in_specs=specs or [VMEM] * len(arg...  20.6 us
    ppermute x28, waiting for transfers between devices, shifted(): return lax.ppermute(value, RC, pairs)  19.9 us
    unnamed x10, local copies, waits for them, and re-layouts  1.82 us
  transfers between devices with their start and end apart: 28, of which 12 were waited for; matrix products, arithmetic and copies ran while one was open for 1% of the time, Pallas kernels for 15%

profile of v7, /device:TPU:0, one launch (start us, length us, event | category | flops | bytes accessed | tf_op | source)
XLA Modules:
  0.0 86.2 jit_solution(6292548638588738029)
XLA Ops:
  0.6 0.0 copy-start
  0.6 0.9 %copy-done = bf16[128,512]{1,0:T(8,128)(2,1)S(1)} copy-done((bf16[128,512]{1,0:T(8,128)(2,1)S(1)}, bf16[128,512]{1,0:T(8,128)(2,1)}, u32[]{:S(2)}) %copy-start) | copy-done | bytes 131096
  1.5 0.1 shard_map.75
  1.7 3.2 %collective-permute-start.2 = (bf16[128,512]{1,0:T(8,128)(2,1)S(1)}, bf16[128,512]{1,0:T(8,128)(2,1)S(1)}, u32[]{:S(2)}, u32[]{:S(2)}) collective-permute-start(bf16[128,512]{1,0:T(8,128)(2,1)S(1)} %shard_map.75), channel_id=1, source_target_pairs={{0,8},{1,9},{2,10},{3,11},{4,12},{5,13},{6,14},{7,15},{8,0},{9,1},... | collective-permute-start | bytes 393224 | tf_op jit(solution)/shard_map/ppermute | solution.py:37
  4.8 1.1 %collective-permute-start.1 = (bf16[128,512]{1,0:T(8,128)(2,1)S(1)}, bf16[128,512]{1,0:T(8,128)(2,1)S(1)}, u32[]{:S(2)}, u32[]{:S(2)}) collective-permute-start(bf16[128,512]{1,0:T(8,128)(2,1)S(1)} %shard_map.75), channel_id=1, source_target_pairs={{0,12},{1,13},{2,14},{3,15},{4,0},{5,1},{6,2},{7,3},{8,4},{9,5},{1... | collective-permute-start | bytes 393224 | tf_op jit(solution)/shard_map/ppermute | solution.py:37
  6.0 0.9 %collective-permute-start = (bf16[128,512]{1,0:T(8,128)(2,1)S(1)}, bf16[128,512]{1,0:T(8,128)(2,1)S(1)}, u32[]{:S(2)}, u32[]{:S(2)}) collective-permute-start(bf16[128,512]{1,0:T(8,128)(2,1)S(1)} %shard_map.75), channel_id=1, source_target_pairs={{0,4},{1,5},{2,6},{3,7},{4,8},{5,9},{6,10},{7,11},{8,12},{9,13},{1... | collective-permute-start | bytes 393224 | tf_op jit(solution)/shard_map/ppermute | solution.py:37
  6.9 0.9 %copy-done.2 = bf16[128,512]{1,0:T(8,128)(2,1)S(1)} copy-done((bf16[128,512]{1,0:T(8,128)(2,1)S(1)}, bf16[128,512]{1,0:T(8,128)(2,1)}, u32[]{:S(2)}) %copy-start.2) | copy-done | bytes 131096
  7.8 0.1 shard_map.76
  7.9 4.0 %collective-permute-start.7 = (bf16[128,512]{1,0:T(8,128)(2,1)S(1)}, bf16[128,512]{1,0:T(8,128)(2,1)S(1)}, u32[]{:S(2)}, u32[]{:S(2)}) collective-permute-start(bf16[128,512]{1,0:T(8,128)(2,1)S(1)} %shard_map.76), channel_id=1, source_target_pairs={{0,64},{1,65},{2,66},{3,67},{4,68},{5,69},{6,70},{7,71},{8,72},{9,... | collective-permute-start | bytes 393224 | tf_op jit(solution)/shard_map/ppermute | solution.py:37
  11.8 0.7 collective-permute-start.6
  12.6 1.3 %collective-permute-start.5 = (bf16[128,512]{1,0:T(8,128)(2,1)S(1)}, bf16[128,512]{1,0:T(8,128)(2,1)S(1)}, u32[]{:S(2)}, u32[]{:S(2)}) collective-permute-start(bf16[128,512]{1,0:T(8,128)(2,1)S(1)} %shard_map.76), channel_id=1, source_target_pairs={{0,32},{1,33},{2,34},{3,35},{4,36},{5,37},{6,38},{7,39},{8,40},{9,... | collective-permute-start | bytes 393224 | tf_op jit(solution)/shard_map/ppermute | solution.py:37
  13.9 3.3 %collective-permute-start.9 = (bf16[512,512]{1,0:T(8,128)(2,1)S(1)}, bf16[512,512]{1,0:T(8,128)(2,1)S(1)}, u32[]{:S(2)}, u32[]{:S(2)}) collective-permute-start(bf16[512,512]{1,0:T(8,128)(2,1)S(1)} %pad_maximum_fusion.refs_1_.i0), channel_id=1, source_target_pairs={{0,2},{1,3},{2,0},{3,1},{4,6},{5,7},{6,4},{7,5},{8,10},{9,11},{10,... | collective-permute-start | bytes 1572872 | tf_op jit(solution)/shard_map/ppermute | solution.py:37
  17.2 0.0 collective-permute-done.7
  17.2 1.1 %collective-permute-done.6 = bf16[128,512]{1,0:T(8,128)(2,1)S(1)} collective-permute-done((bf16[128,512]{1,0:T(8,128)(2,1)S(1)}, bf16[128,512]{1,0:T(8,128)(2,1)S(1)}, u32[]{:S(2)}, u32[]{:S(2)}) %collective-permute-start.6) | collective-permute-done | bytes 131104 | tf_op jit(solution)/shard_map/ppermute | solution.py:37
  18.3 0.5 collective-permute-done.5
  18.8 0.1 collective-permute-start.8
  18.9 1.6 %collective-permute-start.4 = (bf16[512,512]{1,0:T(8,128)(2,1)S(1)}, bf16[512,512]{1,0:T(8,128)(2,1)S(1)}, u32[]{:S(2)}, u32[]{:S(2)}) collective-permute-start(bf16[512,512]{1,0:T(8,128)(2,1)S(1)} %pad_maximum_fusion.refs_1_.i0), channel_id=1, source_target_pairs={{0,1},{1,2},{2,3},{3,0},{4,5},{5,6},{6,7},{7,4},{8,9},{9,10},{10,1... | collective-permute-start | bytes 1572872 | tf_op jit(solution)/shard_map/ppermute | solution.py:37
  20.5 1.7 %collective-permute-start.3 = (bf16[512,512]{1,0:T(8,128)(2,1)S(1)}, bf16[512,512]{1,0:T(8,128)(2,1)S(1)}, u32[]{:S(2)}, u32[]{:S(2)}) collective-permute-start(bf16[512,512]{1,0:T(8,128)(2,1)S(1)} %pad_maximum_fusion.refs_1_.i0), channel_id=1, source_target_pairs={{0,3},{1,0},{2,1},{3,2},{4,7},{5,4},{6,5},{7,6},{8,11},{9,8},{10,9... | collective-permute-start | bytes 1572872 | tf_op jit(solution)/shard_map/ppermute | solution.py:37
  22.9 0.1 pad_add_fusion.ids_ref
  23.0 1.8 %collective-permute-done.9.refs_0_.refs_2_.i3 = bf16[512,512]{1,0:T(8,128)(2,1)S(1)} collective-permute-done((bf16[512,512]{1,0:T(8,128)(2,1)S(1)}, bf16[512,512]{1,0:T(8,128)(2,1)S(1)}, u32[]{:S(2)}, u32[]{:S(2)}) %collective-permute-start.9) | collective-permute-done | bytes 524320 | tf_op jit(solution)/shard_map/ppermute | solution.py:37
  24.8 0.0 collective-permute-done.8.refs_4_.t1
  24.8 0.3 broadcast_in_dim.8.refs_0_
  25.1 4.4 %shard_map.78 = (f32[40,128]{1,0:T(8,128)S(1)}, f32[8,1024]{1,0:T(8,128)S(1)}, f32[512,1024]{1,0:T(8,128)S(1)}, f32[512,1024]{1,0:T(8,128)S(1)}) custom-call(s32[2]{0:T(128)S(1)} %pad_add_fusion.ids_ref, f32[1]{0:T(128)S(6)} %exp.3.scale_ref, s32[2048,128]{1,0:T(8,128)S(1)} %broadcast_in_dim.8.refs_0_, bf16[512,512]{1,0:T(8,128)(2,1)S(1)} %pad_maximum_fusion.refs_1_.i0, ...), custom_call_target="tpu_custom_call" | custom-call | tf_op jit(solution)/shard_map/pallas_call | solution.py:57
  29.5 0.8 collective-permute-done.4.refs_2_.i1
  30.3 0.3 collective-permute-done.3.refs_1_.i2
  30.6 5.0 %shard_map.79 = (f32[40,128]{1,0:T(8,128)S(1)}, f32[48,128]{1,0:T(8,128)S(1)}, f32[512,1024]{1,0:T(8,128)S(1)}, f32[512,1024]{1,0:T(8,128)S(1)}) custom-call(s32[2]{0:T(128)S(1)} %pad_add_fusion.ids_ref, f32[1]{0:T(128)S(6)} %exp.3.scale_ref, s32[2048,128]{1,0:T(8,128)S(1)} %broadcast_in_dim.8.refs_0_, ...), custom_call_target="tpu_custom_call" | custom-call | tf_op jit(solution)/shard_map/pallas_call | solution.py:57
  35.6 0.1 collective-permute-start.13
  35.7 0.8 collective-permute-start.12
  36.5 2.5 %collective-permute-start.11 = (f32[40,128]{1,0:T(8,128)S(1)}, f32[40,128]{1,0:T(8,128)S(1)}, u32[]{:S(2)}, u32[]{:S(2)}) collective-permute-start(f32[40,128]{1,0:T(8,128)S(1)} %get-tuple-element.33.refs_0_), channel_id=1, source_target_pairs={{0,12},{1,13},{2,14},{3,15},{4,0},{5,1},{6,2},{7,3},{8,4},{9,5},{1... | collective-permute-start | bytes 61448 | tf_op jit(solution)/shard_map/ppermute | solution.py:37
  39.1 2.0 %collective-permute-done.12.refs_3_ = f32[40,128]{1,0:T(8,128)S(1)} collective-permute-done((f32[40,128]{1,0:T(8,128)S(1)}, f32[40,128]{1,0:T(8,128)S(1)}, u32[]{:S(2)}, u32[]{:S(2)}) %collective-permute-start.12) | collective-permute-done | bytes 20512 | tf_op jit(solution)/shard_map/ppermute | solution.py:37
  41.1 3.0 %collective-permute-done.10.refs_1_ = f32[40,128]{1,0:T(8,128)S(1)} collective-permute-done((f32[40,128]{1,0:T(8,128)S(1)}, f32[40,128]{1,0:T(8,128)S(1)}, u32[]{:S(2)}, u32[]{:S(2)}) %collective-permute-start.10) | collective-permute-done | bytes 20512 | tf_op jit(solution)/shard_map/ppermute | solution.py:37
  44.1 1.1 %collective-permute-start.15 = (f32[48,128]{1,0:T(8,128)S(1)}, f32[48,128]{1,0:T(8,128)S(1)}, u32[]{:S(2)}, u32[]{:S(2)}) collective-permute-start(f32[48,128]{1,0:T(8,128)S(1)} %get-tuple-element.36.refs_2_), channel_id=1, source_target_pairs={{0,32},{1,33},{2,34},{3,35},{4,36},{5,37},{6,38},{7,39},{8,40},{9,... | collective-permute-start | bytes 73736 | tf_op jit(solution)/shard_map/ppermute | solution.py:37
  45.2 1.4 %collective-permute-start.14 = (f32[40,128]{1,0:T(8,128)S(1)}, f32[40,128]{1,0:T(8,128)S(1)}, u32[]{:S(2)}, u32[]{:S(2)}) collective-permute-start(f32[40,128]{1,0:T(8,128)S(1)} %get-tuple-element.35.refs_0_), channel_id=1, source_target_pairs={{0,1},{1,0},{2,3},{3,2},{4,5},{5,4},{6,7},{7,6},{8,9},{9,8},{10,11... | collective-permute-start | bytes 61448 | tf_op jit(solution)/shard_map/ppermute | solution.py:37
  46.6 2.4 %collective-permute-done.14.refs_1_ = f32[40,128]{1,0:T(8,128)S(1)} collective-permute-done((f32[40,128]{1,0:T(8,128)S(1)}, f32[40,128]{1,0:T(8,128)S(1)}, u32[]{:S(2)}, u32[]{:S(2)}) %collective-permute-start.14) | collective-permute-done | bytes 20512 | tf_op jit(solution)/shard_map/ppermute | solution.py:37
  49.0 1.2 %collective-permute-start.17 = (f32[48,128]{1,0:T(8,128)S(1)}, f32[48,128]{1,0:T(8,128)S(1)}, u32[]{:S(2)}, u32[]{:S(2)}) collective-permute-start(f32[48,128]{1,0:T(8,128)S(1)} %get-tuple-element.38.c0), channel_id=1, source_target_pairs={{0,96},{1,97},{2,98},{3,99},{4,100},{5,101},{6,102},{7,103},{8,104... | collective-permute-start | bytes 73736 | tf_op jit(solution)/shard_map/ppermute | solution.py:37
  50.2 3.2 %collective-permute-start.16 = (f32[40,128]{1,0:T(8,128)S(1)}, f32[40,128]{1,0:T(8,128)S(1)}, u32[]{:S(2)}, u32[]{:S(2)}) collective-permute-start(f32[40,128]{1,0:T(8,128)S(1)} %get-tuple-element.37.r0), channel_id=1, source_target_pairs={{0,3},{1,2},{2,1},{3,0},{4,7},{5,6},{6,5},{7,4},{8,11},{9,10},{10,... | collective-permute-start | bytes 61448 | tf_op jit(solution)/shard_map/ppermute | solution.py:37
  53.4 1.8 %collective-permute-done.16.r1 = f32[40,128]{1,0:T(8,128)S(1)} collective-permute-done((f32[40,128]{1,0:T(8,128)S(1)}, f32[40,128]{1,0:T(8,128)S(1)}, u32[]{:S(2)}, u32[]{:S(2)}) %collective-permute-start.16) | collective-permute-done | bytes 20512 | tf_op jit(solution)/shard_map/ppermute | solution.py:37
  55.2 0.7 shard_map.82
  55.9 1.3 %shard_map.84.d_ref.d3 = bf16[512,1024]{1,0:T(8,128)(2,1)S(1)} custom-call(s32[2]{0:T(128)S(1)} %pad_add_fusion.ids_ref, f32[1]{0:T(128)S(6)} %exp.3.scale_ref, s32[2048,128]{1,0:T(8,128)S(1)} %broadcast_in_dim.8.refs_0_, f32[16,128]{1,0:T(8,128)S(1)} %get-tuple-element.40.refs_1_, f32[1,1024]{1,0:T(1,128)S(1)} %get-tuple-element.41.refs_2_, ...), custom_call_target="tpu_custom_call" | custom-call | flops 10000000000 | bytes 1000000 | tf_op jit(solution)/shard_map/pallas_call | solution.py:57
  57.2 0.7 shard_map.87.refs_2_
  57.9 1.9 %collective-permute-start.21 = (bf16[528,512]{1,0:T(8,128)(2,1)S(1)}, bf16[528,512]{1,0:T(8,128)(2,1)S(1)}, u32[]{:S(2)}, u32[]{:S(2)}) collective-permute-start(bf16[528,512]{1,0:T(8,128)(2,1)S(1)} %shard_map.87.refs_2_), channel_id=1, source_target_pairs={{0,2},{1,3},{2,0},{3,1},{4,6},{5,7},{6,4},{7,5},{8,10},{9,11},{10,... | collective-permute-start | bytes 1622024 | tf_op jit(solution)/shard_map/ppermute | solution.py:37
  59.8 2.5 %shard_map.83 = (bf16[512,1024]{1,0:T(8,128)(2,1)S(1)}, bf16[512,1024]{1,0:T(8,128)(2,1)S(1)}, bf16[512,1024]{1,0:T(8,128)(2,1)S(1)}) custom-call(s32[2]{0:T(128)S(1)} %pad_add_fusion.ids_ref, f32[1]{0:T(128)S(6)} %exp.3.scale_ref, s32[2048,128]{1,0:T(8,128)S(1)} %broadcast_in_dim.8.refs_0_, f32[16,128]{1,0:T(8,128)S(1)} %get-tuple-element.40.refs_1_, ...), custom_call_target="tpu_custom_call" | custom-call | flops 10000000000 | bytes 1000000 | tf_op jit(solution)/shard_map/pallas_call | solution.py:57
  62.3 0.7 shard_map.86.refs_1_
  63.0 2.6 %collective-permute-start.20 = (bf16[528,512]{1,0:T(8,128)(2,1)S(1)}, bf16[528,512]{1,0:T(8,128)(2,1)S(1)}, u32[]{:S(2)}, u32[]{:S(2)}) collective-permute-start(bf16[528,512]{1,0:T(8,128)(2,1)S(1)} %shard_map.86.refs_1_), channel_id=1, source_target_pairs={{0,1},{1,2},{2,3},{3,0},{4,5},{5,6},{6,7},{7,4},{8,9},{9,10},{10,1... | collective-permute-start | bytes 1622024 | tf_op jit(solution)/shard_map/ppermute | solution.py:37
  65.6 0.7 shard_map.85.refs_0_
  66.3 1.0 %collective-permute-start.19 = (bf16[528,512]{1,0:T(8,128)(2,1)S(1)}, bf16[528,512]{1,0:T(8,128)(2,1)S(1)}, u32[]{:S(2)}, u32[]{:S(2)}) collective-permute-start(bf16[528,512]{1,0:T(8,128)(2,1)S(1)} %shard_map.85.refs_0_), channel_id=1, source_target_pairs={{0,3},{1,0},{2,1},{3,2},{4,7},{5,4},{6,5},{7,6},{8,11},{9,8},{10,9... | collective-permute-start | bytes 1622024 | tf_op jit(solution)/shard_map/ppermute | solution.py:37
  67.3 1.5 %shard_map.88.refs_0_ = bf16[528,512]{1,0:T(8,128)(2,1)S(1)} custom-call(f32[1]{0:T(128)S(6)} %exp.3.scale_ref, bf16[16,512]{1,0:T(8,128)(2,1)S(1)} %get-tuple-element.39.row_tail, bf16[512,512]{1,0:T(8,128)(2,1)S(1)} %pad_maximum_fusion.refs_1_.i0, bf16[512,512]{1,0:T(8,128)(2,1)S(1)} %collective-permute-done.4.refs_2_.i1, ...), custom_call_target="tpu_custom_call" | custom-call | flops 10000000000 | bytes 1000000 | tf_op jit(solution)/shard_map/pallas_call | solution.py:57
  68.9 0.1 collective-permute-start.18
  69.0 1.5 %shard_map.89.refs_0_ = bf16[528,512]{1,0:T(8,128)(2,1)S(1)} custom-call(f32[1]{0:T(128)S(6)} %exp.3.scale_ref, bf16[16,512]{1,0:T(8,128)(2,1)S(1)} %get-tuple-element.39.row_tail, bf16[512,512]{1,0:T(8,128)(2,1)S(1)} %pad_maximum_fusion.refs_1_.i0, bf16[512,512]{1,0:T(8,128)(2,1)S(1)} %collective-permute-done.4.refs_2_.i1, ...), custom_call_target="tpu_custom_call" | custom-call | flops 10000000000 | bytes 1000000 | tf_op jit(solution)/shard_map/pallas_call | solution.py:57
  70.5 0.4 collective-permute-done.18.refs_1_
  70.9 0.2 shard_map.90
  71.1 2.0 %collective-permute-start.25 = (bf16[144,512]{1,0:T(8,128)(2,1)S(1)}, bf16[144,512]{1,0:T(8,128)(2,1)S(1)}, u32[]{:S(2)}, u32[]{:S(2)}) collective-permute-start(bf16[144,512]{1,0:T(8,128)(2,1)S(1)} %get-tuple-element.55), channel_id=1, source_target_pairs={{0,96},{1,97},{2,98},{3,99},{4,100},{5,101},{6,102},{7,103},{8,104... | collective-permute-start | bytes 442376 | tf_op jit(solution)/shard_map/ppermute | solution.py:37
  73.1 0.7 shard_map.91.refs_0_
  73.8 0.0 copy-start.1
  73.8 0.0 copy-start.3
  73.8 0.1 collective-permute-start.26
  74.0 1.8 %collective-permute-start.27 = (bf16[144,512]{1,0:T(8,128)(2,1)S(1)}, bf16[144,512]{1,0:T(8,128)(2,1)S(1)}, u32[]{:S(2)}, u32[]{:S(2)}) collective-permute-start(bf16[144,512]{1,0:T(8,128)(2,1)S(1)} %get-tuple-element.57), channel_id=1, source_target_pairs={{0,64},{1,65},{2,66},{3,67},{4,68},{5,69},{6,70},{7,71},{8,72},{9,... | collective-permute-start | bytes 442376 | tf_op jit(solution)/shard_map/ppermute | solution.py:37
  75.8 0.4 shard_map.92
  76.1 0.1 collective-permute-start.22
  76.2 2.0 %collective-permute-start.23 = (bf16[144,512]{1,0:T(8,128)(2,1)S(1)}, bf16[144,512]{1,0:T(8,128)(2,1)S(1)}, u32[]{:S(2)}, u32[]{:S(2)}) collective-permute-start(bf16[144,512]{1,0:T(8,128)(2,1)S(1)} %get-tuple-element.53), channel_id=1, source_target_pairs={{0,4},{1,5},{2,6},{3,7},{4,8},{5,9},{6,10},{7,11},{8,12},{9,13},{1... | collective-permute-start | bytes 442376 | tf_op jit(solution)/shard_map/ppermute | solution.py:37
  78.2 0.8 collective-permute-start.24
  79.1 4.8 %collective-permute-done.26.b2 = bf16[144,512]{1,0:T(8,128)(2,1)S(1)} collective-permute-done((bf16[144,512]{1,0:T(8,128)(2,1)S(1)}, bf16[144,512]{1,0:T(8,128)(2,1)S(1)}, u32[]{:S(2)}, u32[]{:S(2)}) %collective-permute-start.26) | collective-permute-done | bytes 147488 | tf_op jit(solution)/shard_map/ppermute | solution.py:37
  83.9 1.0 %collective-permute-done.24.a3 = bf16[144,512]{1,0:T(8,128)(2,1)S(1)} collective-permute-done((bf16[144,512]{1,0:T(8,128)(2,1)S(1)}, bf16[144,512]{1,0:T(8,128)(2,1)S(1)}, u32[]{:S(2)}, u32[]{:S(2)}) %collective-permute-start.24) | collective-permute-done | bytes 147488 | tf_op jit(solution)/shard_map/ppermute | solution.py:37
  84.9 1.1 %shard_map.93 = (f32[128,512]{1,0:T(8,128)}, f32[128,512]{1,0:T(8,128)}, f32[1]{0:T(128)}, f32[1]{0:T(128)}) custom-call(bf16[128,512]{1,0:T(8,128)(2,1)S(1)} %copy-done.1, bf16[128,512]{1,0:T(8,128)(2,1)S(1)} %copy-done.3, bf16[144,512]{1,0:T(8,128)(2,1)S(1)} %get-tuple-element.51.a0, bf16[144,512]{1,0:T(8,128)(2,1)S(1)} %collective-permute-done.22.a1, ...), custom_call_target="tpu_custom_call" | custom-call | tf_op jit(solution)/shard_map/pallas_call | solution.py:433
  (26 shorter events, 0.2 us)
Async XLA Ops:
  0.6 0.9 %copy-start = (bf16[128,512]{1,0:T(8,128)(2,1)S(1)}, bf16[128,512]{1,0:T(8,128)(2,1)}, u32[]{:S(2)}) copy-start(bf16[128,512]{1,0:T(8,128)(2,1)} %img_ref.1) | copy-start | bytes 393220
  1.5 21.4 %copy-start.4 = (s32[2048]{0:T(1024)S(1)}, s32[2048]{0:T(1024)}, u32[]{:S(2)}) copy-start(s32[2048]{0:T(1024)} %param.6) | copy-start | bytes 24580
  1.7 10.9 %collective-permute-start.2 = (bf16[128,512]{1,0:T(8,128)(2,1)S(1)}, bf16[128,512]{1,0:T(8,128)(2,1)S(1)}, u32[]{:S(2)}, u32[]{:S(2)}) collective-permute-start(bf16[128,512]{1,0:T(8,128)(2,1)S(1)} %shard_map.75), channel_id=1, source_target_pairs={{0,8},{1,9},{2,10},{3,11},{4,12},{5,13},{6,14},{7,15},{8,0},{9,1},... | collective-permute-start | bytes 393224 | tf_op jit(solution)/shard_map/ppermute | solution.py:37
  4.8 9.0 %collective-permute-start.1 = (bf16[128,512]{1,0:T(8,128)(2,1)S(1)}, bf16[128,512]{1,0:T(8,128)(2,1)S(1)}, u32[]{:S(2)}, u32[]{:S(2)}) collective-permute-start(bf16[128,512]{1,0:T(8,128)(2,1)S(1)} %shard_map.75), channel_id=1, source_target_pairs={{0,12},{1,13},{2,14},{3,15},{4,0},{5,1},{6,2},{7,3},{8,4},{9,5},{1... | collective-permute-start | bytes 393224 | tf_op jit(solution)/shard_map/ppermute | solution.py:37
  6.0 7.9 %collective-permute-start = (bf16[128,512]{1,0:T(8,128)(2,1)S(1)}, bf16[128,512]{1,0:T(8,128)(2,1)S(1)}, u32[]{:S(2)}, u32[]{:S(2)}) collective-permute-start(bf16[128,512]{1,0:T(8,128)(2,1)S(1)} %shard_map.75), channel_id=1, source_target_pairs={{0,4},{1,5},{2,6},{3,7},{4,8},{5,9},{6,10},{7,11},{8,12},{9,13},{1... | collective-permute-start | bytes 393224 | tf_op jit(solution)/shard_map/ppermute | solution.py:37
  6.9 0.9 %copy-start.2 = (bf16[128,512]{1,0:T(8,128)(2,1)S(1)}, bf16[128,512]{1,0:T(8,128)(2,1)}, u32[]{:S(2)}) copy-start(bf16[128,512]{1,0:T(8,128)(2,1)} %txt_ref.1) | copy-start | bytes 393220
  7.9 9.3 %collective-permute-start.7 = (bf16[128,512]{1,0:T(8,128)(2,1)S(1)}, bf16[128,512]{1,0:T(8,128)(2,1)S(1)}, u32[]{:S(2)}, u32[]{:S(2)}) collective-permute-start(bf16[128,512]{1,0:T(8,128)(2,1)S(1)} %shard_map.76), channel_id=1, source_target_pairs={{0,64},{1,65},{2,66},{3,67},{4,68},{5,69},{6,70},{7,71},{8,72},{9,... | collective-permute-start | bytes 393224 | tf_op jit(solution)/shard_map/ppermute | solution.py:37
  11.8 6.4 %collective-permute-start.6 = (bf16[128,512]{1,0:T(8,128)(2,1)S(1)}, bf16[128,512]{1,0:T(8,128)(2,1)S(1)}, u32[]{:S(2)}, u32[]{:S(2)}) collective-permute-start(bf16[128,512]{1,0:T(8,128)(2,1)S(1)} %shard_map.76), channel_id=1, source_target_pairs={{0,96},{1,97},{2,98},{3,99},{4,100},{5,101},{6,102},{7,103},{8,104... | collective-permute-start | bytes 393224 | tf_op jit(solution)/shard_map/ppermute | solution.py:37
  12.6 6.2 %collective-permute-start.5 = (bf16[128,512]{1,0:T(8,128)(2,1)S(1)}, bf16[128,512]{1,0:T(8,128)(2,1)S(1)}, u32[]{:S(2)}, u32[]{:S(2)}) collective-permute-start(bf16[128,512]{1,0:T(8,128)(2,1)S(1)} %shard_map.76), channel_id=1, source_target_pairs={{0,32},{1,33},{2,34},{3,35},{4,36},{5,37},{6,38},{7,39},{8,40},{9,... | collective-permute-start | bytes 393224 | tf_op jit(solution)/shard_map/ppermute | solution.py:37
  13.9 10.9 %collective-permute-start.9 = (bf16[512,512]{1,0:T(8,128)(2,1)S(1)}, bf16[512,512]{1,0:T(8,128)(2,1)S(1)}, u32[]{:S(2)}, u32[]{:S(2)}) collective-permute-start(bf16[512,512]{1,0:T(8,128)(2,1)S(1)} %pad_maximum_fusion.refs_1_.i0), channel_id=1, source_target_pairs={{0,2},{1,3},{2,0},{3,1},{4,6},{5,7},{6,4},{7,5},{8,10},{9,11},{10,... | collective-permute-start | bytes 1572872 | tf_op jit(solution)/shard_map/ppermute | solution.py:37
  18.8 6.0 %collective-permute-start.8 = (bf16[512,512]{1,0:T(8,128)(2,1)S(1)}, bf16[512,512]{1,0:T(8,128)(2,1)S(1)}, u32[]{:S(2)}, u32[]{:S(2)}) collective-permute-start(bf16[512,512]{1,0:T(8,128)(2,1)S(1)} %pad_maximum_fusion.1.refs_3_.t0), channel_id=1, source_target_pairs={{0,16},{1,17},{2,18},{3,19},{4,20},{5,21},{6,22},{7,23},{8,24},{9,... | collective-permute-start | bytes 1572872 | tf_op jit(solution)/shard_map/ppermute | solution.py:37
  18.9 11.4 %collective-permute-start.4 = (bf16[512,512]{1,0:T(8,128)(2,1)S(1)}, bf16[512,512]{1,0:T(8,128)(2,1)S(1)}, u32[]{:S(2)}, u32[]{:S(2)}) collective-permute-start(bf16[512,512]{1,0:T(8,128)(2,1)S(1)} %pad_maximum_fusion.refs_1_.i0), channel_id=1, source_target_pairs={{0,1},{1,2},{2,3},{3,0},{4,5},{5,6},{6,7},{7,4},{8,9},{9,10},{10,1... | collective-permute-start | bytes 1572872 | tf_op jit(solution)/shard_map/ppermute | solution.py:37
  20.5 10.1 %collective-permute-start.3 = (bf16[512,512]{1,0:T(8,128)(2,1)S(1)}, bf16[512,512]{1,0:T(8,128)(2,1)S(1)}, u32[]{:S(2)}, u32[]{:S(2)}) collective-permute-start(bf16[512,512]{1,0:T(8,128)(2,1)S(1)} %pad_maximum_fusion.refs_1_.i0), channel_id=1, source_target_pairs={{0,3},{1,0},{2,1},{3,2},{4,7},{5,4},{6,5},{7,6},{8,11},{9,8},{10,9... | collective-permute-start | bytes 1572872 | tf_op jit(solution)/shard_map/ppermute | solution.py:37
  35.6 8.4 %collective-permute-start.13 = (f32[48,128]{1,0:T(8,128)S(1)}, f32[48,128]{1,0:T(8,128)S(1)}, u32[]{:S(2)}, u32[]{:S(2)}) collective-permute-start(f32[48,128]{1,0:T(8,128)S(1)} %get-tuple-element.34.refs_4_), channel_id=1, source_target_pairs={{0,16},{1,17},{2,18},{3,19},{4,20},{5,21},{6,22},{7,23},{8,24},{9,... | collective-permute-start | bytes 73736 | tf_op jit(solution)/shard_map/ppermute | solution.py:37
  35.7 5.4 %collective-permute-start.12 = (f32[40,128]{1,0:T(8,128)S(1)}, f32[40,128]{1,0:T(8,128)S(1)}, u32[]{:S(2)}, u32[]{:S(2)}) collective-permute-start(f32[40,128]{1,0:T(8,128)S(1)} %get-tuple-element.33.refs_0_), channel_id=1, source_target_pairs={{0,8},{1,9},{2,10},{3,11},{4,12},{5,13},{6,14},{7,15},{8,0},{9,1},... | collective-permute-start | bytes 61448 | tf_op jit(solution)/shard_map/ppermute | solution.py:37
  36.5 4.5 %collective-permute-start.11 = (f32[40,128]{1,0:T(8,128)S(1)}, f32[40,128]{1,0:T(8,128)S(1)}, u32[]{:S(2)}, u32[]{:S(2)}) collective-permute-start(f32[40,128]{1,0:T(8,128)S(1)} %get-tuple-element.33.refs_0_), channel_id=1, source_target_pairs={{0,12},{1,13},{2,14},{3,15},{4,0},{5,1},{6,2},{7,3},{8,4},{9,5},{1... | collective-permute-start | bytes 61448 | tf_op jit(solution)/shard_map/ppermute | solution.py:37
  39.0 5.0 %collective-permute-start.10 = (f32[40,128]{1,0:T(8,128)S(1)}, f32[40,128]{1,0:T(8,128)S(1)}, u32[]{:S(2)}, u32[]{:S(2)}) collective-permute-start(f32[40,128]{1,0:T(8,128)S(1)} %get-tuple-element.33.refs_0_), channel_id=1, source_target_pairs={{0,4},{1,5},{2,6},{3,7},{4,8},{5,9},{6,10},{7,11},{8,12},{9,13},{1... | collective-permute-start | bytes 61448 | tf_op jit(solution)/shard_map/ppermute | solution.py:37
  44.1 4.9 %collective-permute-start.15 = (f32[48,128]{1,0:T(8,128)S(1)}, f32[48,128]{1,0:T(8,128)S(1)}, u32[]{:S(2)}, u32[]{:S(2)}) collective-permute-start(f32[48,128]{1,0:T(8,128)S(1)} %get-tuple-element.36.refs_2_), channel_id=1, source_target_pairs={{0,32},{1,33},{2,34},{3,35},{4,36},{5,37},{6,38},{7,39},{8,40},{9,... | collective-permute-start | bytes 73736 | tf_op jit(solution)/shard_map/ppermute | solution.py:37
  45.2 3.8 %collective-permute-start.14 = (f32[40,128]{1,0:T(8,128)S(1)}, f32[40,128]{1,0:T(8,128)S(1)}, u32[]{:S(2)}, u32[]{:S(2)}) collective-permute-start(f32[40,128]{1,0:T(8,128)S(1)} %get-tuple-element.35.refs_0_), channel_id=1, source_target_pairs={{0,1},{1,0},{2,3},{3,2},{4,5},{5,4},{6,7},{7,6},{8,9},{9,8},{10,11... | collective-permute-start | bytes 61448 | tf_op jit(solution)/shard_map/ppermute | solution.py:37
  49.0 6.2 %collective-permute-start.17 = (f32[48,128]{1,0:T(8,128)S(1)}, f32[48,128]{1,0:T(8,128)S(1)}, u32[]{:S(2)}, u32[]{:S(2)}) collective-permute-start(f32[48,128]{1,0:T(8,128)S(1)} %get-tuple-element.38.c0), channel_id=1, source_target_pairs={{0,96},{1,97},{2,98},{3,99},{4,100},{5,101},{6,102},{7,103},{8,104... | collective-permute-start | bytes 73736 | tf_op jit(solution)/shard_map/ppermute | solution.py:37
  50.2 5.0 %collective-permute-start.16 = (f32[40,128]{1,0:T(8,128)S(1)}, f32[40,128]{1,0:T(8,128)S(1)}, u32[]{:S(2)}, u32[]{:S(2)}) collective-permute-start(f32[40,128]{1,0:T(8,128)S(1)} %get-tuple-element.37.r0), channel_id=1, source_target_pairs={{0,3},{1,2},{2,1},{3,0},{4,7},{5,6},{6,5},{7,4},{8,11},{9,10},{10,... | collective-permute-start | bytes 61448 | tf_op jit(solution)/shard_map/ppermute | solution.py:37
  57.9 16.1 %collective-permute-start.21 = (bf16[528,512]{1,0:T(8,128)(2,1)S(1)}, bf16[528,512]{1,0:T(8,128)(2,1)S(1)}, u32[]{:S(2)}, u32[]{:S(2)}) collective-permute-start(bf16[528,512]{1,0:T(8,128)(2,1)S(1)} %shard_map.87.refs_2_), channel_id=1, source_target_pairs={{0,2},{1,3},{2,0},{3,1},{4,6},{5,7},{6,4},{7,5},{8,10},{9,11},{10,... | collective-permute-start | bytes 1622024 | tf_op jit(solution)/shard_map/ppermute | solution.py:37
  63.0 12.8 %collective-permute-start.20 = (bf16[528,512]{1,0:T(8,128)(2,1)S(1)}, bf16[528,512]{1,0:T(8,128)(2,1)S(1)}, u32[]{:S(2)}, u32[]{:S(2)}) collective-permute-start(bf16[528,512]{1,0:T(8,128)(2,1)S(1)} %shard_map.86.refs_1_), channel_id=1, source_target_pairs={{0,1},{1,2},{2,3},{3,0},{4,5},{5,6},{6,7},{7,4},{8,9},{9,10},{10,1... | collective-permute-start | bytes 1622024 | tf_op jit(solution)/shard_map/ppermute | solution.py:37
  66.3 9.4 %collective-permute-start.19 = (bf16[528,512]{1,0:T(8,128)(2,1)S(1)}, bf16[528,512]{1,0:T(8,128)(2,1)S(1)}, u32[]{:S(2)}, u32[]{:S(2)}) collective-permute-start(bf16[528,512]{1,0:T(8,128)(2,1)S(1)} %shard_map.85.refs_0_), channel_id=1, source_target_pairs={{0,3},{1,0},{2,1},{3,2},{4,7},{5,4},{6,5},{7,6},{8,11},{9,8},{10,9... | collective-permute-start | bytes 1622024 | tf_op jit(solution)/shard_map/ppermute | solution.py:37
  68.9 2.0 %collective-permute-start.18 = (bf16[528,512]{1,0:T(8,128)(2,1)S(1)}, bf16[528,512]{1,0:T(8,128)(2,1)S(1)}, u32[]{:S(2)}, u32[]{:S(2)}) collective-permute-start(bf16[528,512]{1,0:T(8,128)(2,1)S(1)} %shard_map.88.refs_0_), channel_id=1, source_target_pairs={{0,16},{1,17},{2,18},{3,19},{4,20},{5,21},{6,22},{7,23},{8,24},{9,... | collective-permute-start | bytes 1622024 | tf_op jit(solution)/shard_map/ppermute | solution.py:37
  71.1 7.2 %collective-permute-start.25 = (bf16[144,512]{1,0:T(8,128)(2,1)S(1)}, bf16[144,512]{1,0:T(8,128)(2,1)S(1)}, u32[]{:S(2)}, u32[]{:S(2)}) collective-permute-start(bf16[144,512]{1,0:T(8,128)(2,1)S(1)} %get-tuple-element.55), channel_id=1, source_target_pairs={{0,96},{1,97},{2,98},{3,99},{4,100},{5,101},{6,102},{7,103},{8,104... | collective-permute-start | bytes 442376 | tf_op jit(solution)/shard_map/ppermute | solution.py:37
  73.8 11.1 %copy-start.1 = (bf16[128,512]{1,0:T(8,128)(2,1)S(1)}, bf16[128,512]{1,0:T(8,128)(2,1)}, u32[]{:S(2)}) copy-start(bf16[128,512]{1,0:T(8,128)(2,1)} %img_ref.1) | copy-start | bytes 393220
  73.8 11.1 %copy-start.3 = (bf16[128,512]{1,0:T(8,128)(2,1)S(1)}, bf16[128,512]{1,0:T(8,128)(2,1)}, u32[]{:S(2)}) copy-start(bf16[128,512]{1,0:T(8,128)(2,1)} %txt_ref.1) | copy-start | bytes 393220
  73.8 10.0 %collective-permute-start.26 = (bf16[144,512]{1,0:T(8,128)(2,1)S(1)}, bf16[144,512]{1,0:T(8,128)(2,1)S(1)}, u32[]{:S(2)}, u32[]{:S(2)}) collective-permute-start(bf16[144,512]{1,0:T(8,128)(2,1)S(1)} %get-tuple-element.56), channel_id=1, source_target_pairs={{0,32},{1,33},{2,34},{3,35},{4,36},{5,37},{6,38},{7,39},{8,40},{9,... | collective-permute-start | bytes 442376 | tf_op jit(solution)/shard_map/ppermute | solution.py:37
  74.0 9.9 %collective-permute-start.27 = (bf16[144,512]{1,0:T(8,128)(2,1)S(1)}, bf16[144,512]{1,0:T(8,128)(2,1)S(1)}, u32[]{:S(2)}, u32[]{:S(2)}) collective-permute-start(bf16[144,512]{1,0:T(8,128)(2,1)S(1)} %get-tuple-element.57), channel_id=1, source_target_pairs={{0,64},{1,65},{2,66},{3,67},{4,68},{5,69},{6,70},{7,71},{8,72},{9,... | collective-permute-start | bytes 442376 | tf_op jit(solution)/shard_map/ppermute | solution.py:37
  76.1 7.7 %collective-permute-start.22 = (bf16[144,512]{1,0:T(8,128)(2,1)S(1)}, bf16[144,512]{1,0:T(8,128)(2,1)S(1)}, u32[]{:S(2)}, u32[]{:S(2)}) collective-permute-start(bf16[144,512]{1,0:T(8,128)(2,1)S(1)} %get-tuple-element.52), channel_id=1, source_target_pairs={{0,12},{1,13},{2,14},{3,15},{4,0},{5,1},{6,2},{7,3},{8,4},{9,5},{1... | collective-permute-start | bytes 442376 | tf_op jit(solution)/shard_map/ppermute | solution.py:37
  76.2 7.7 %collective-permute-start.23 = (bf16[144,512]{1,0:T(8,128)(2,1)S(1)}, bf16[144,512]{1,0:T(8,128)(2,1)S(1)}, u32[]{:S(2)}, u32[]{:S(2)}) collective-permute-start(bf16[144,512]{1,0:T(8,128)(2,1)S(1)} %get-tuple-element.53), channel_id=1, source_target_pairs={{0,4},{1,5},{2,6},{3,7},{4,8},{5,9},{6,10},{7,11},{8,12},{9,13},{1... | collective-permute-start | bytes 442376 | tf_op jit(solution)/shard_map/ppermute | solution.py:37
  78.2 6.6 %collective-permute-start.24 = (bf16[144,512]{1,0:T(8,128)(2,1)S(1)}, bf16[144,512]{1,0:T(8,128)(2,1)S(1)}, u32[]{:S(2)}, u32[]{:S(2)}) collective-permute-start(bf16[144,512]{1,0:T(8,128)(2,1)S(1)} %get-tuple-element.54), channel_id=1, source_target_pairs={{0,8},{1,9},{2,10},{3,11},{4,12},{5,13},{6,14},{7,15},{8,0},{9,1},... | collective-permute-start | bytes 442376 | tf_op jit(solution)/shard_map/ppermute | solution.py:37
